TPU v7x, 32 devices: a whole 2x2x4 slice. The times are simulated.
32 devices in a mesh: dp: 4 (over x, core), seq: 8 (over z, y).
Axes of the slice: x: 2, y: 2, z: 4, core: 2. Of those that a mesh axis runs over, the one named last changes fastest.
Arguments:
- tokens: bfloat16 [6144, 2048], P(('dp', 'seq')), may hold values from -6 to 6
- lengths: int32 [4], P('dp'), may hold values from 768 to 1536, as said below
- cotangent: bfloat16 [6144, 2048], P(('dp', 'seq')), may hold values from -6 to 6
- w_query: bfloat16 [2048, 2048], P('dp', 'seq'), may hold values from -0.125 to 0.125
- w_key: bfloat16 [2048, 2048], P('dp', 'seq'), may hold values from -0.125 to 0.125
- w_value: bfloat16 [2048, 2048], P('dp', 'seq'), may hold values from -0.125 to 0.125
- w_out: bfloat16 [2048, 2048], P('dp', 'seq'), may hold values from -2.5 to 2.5
- w_gate: bfloat16 [2048, 8192], P('dp', 'seq'), may hold values from -0.125 to 0.125
- w_up: bfloat16 [2048, 8192], P('dp', 'seq'), may hold values from -0.125 to 0.125
- w_down: bfloat16 [2048, 8192], P('dp', 'seq'), may hold values from -0.0625 to 0.0625
- gain_attn: bfloat16 [2048], P('dp'), may hold values from 0.099609375 to 1.8984375
- gain_ffn: bfloat16 [2048], P('dp'), may hold values from 0.099609375 to 1.8984375
Outputs:
- output: bfloat16 [6144, 2048], P(('dp', 'seq'))
- grad_tokens: float32 [6144, 2048], P(('dp', 'seq'))
- grad_w_query: float32 [2048, 2048], P('dp', 'seq')
- grad_w_key: float32 [2048, 2048], P('dp', 'seq')
- grad_w_value: float32 [2048, 2048], P('dp', 'seq')
- grad_w_out: float32 [2048, 2048], P('dp', 'seq')
- grad_w_gate: float32 [2048, 8192], P('dp', 'seq')
- grad_w_up: float32 [2048, 8192], P('dp', 'seq')
- grad_w_down: float32 [2048, 8192], P('dp', 'seq')
- grad_gain_attn: float32 [2048], P(('dp', 'seq'))
- grad_gain_ffn: float32 [2048], P(('dp', 'seq'))
Inputs may be any that keep to these rules, and one draw needn't show every extreme that they name: `lengths`: each sequence's count of real tokens; at least one sequence is full, 1536.
All inputs are finite; a program needn't handle non-finite values.
Results may differ from a plain program's by a relative error of at most 0.017.
Values may be sent and summed in bfloat16 or wider, within the bound.
A program may use at most 320 MiB of HBM per device.

v0:
```python
import math

import jax
import jax.numpy as jnp
from jax import lax
from jax.sharding import PartitionSpec as P

HD = 128
WINDOW = 2048


EPSILON = 1e-05
NEGATIVE = -1e30


def rope_tables(seq_len, head_dim):
    half_dim = head_dim // 2
    frequency = jnp.exp(
        -math.log(10000.0) * jnp.arange(half_dim, dtype=jnp.float32) * (2.0 / head_dim)
    )
    angles = jnp.arange(seq_len, dtype=jnp.float32)[:, None] * frequency[None, :]
    return (jnp.cos(angles), jnp.sin(angles))


def rotate(values, cos_table, sine_table):
    half_dim = values.shape[-1] // 2
    first_half = values[..., :half_dim]
    second_half = values[..., half_dim:]
    cos_part = cos_table[:, None, :]
    sine_part = sine_table[:, None, :]
    return jnp.concatenate(
        [
            first_half * cos_part - second_half * sine_part,
            second_half * cos_part + first_half * sine_part,
        ],
        axis=-1,
    )


def norm_factor(values):
    return lax.rsqrt(jnp.mean(values * values, axis=-1, keepdims=True) + EPSILON)


def norm_back(values, factor, gain, grad_normed):
    weighted = grad_normed * gain
    grad_values = factor * (
        weighted - values * factor * factor * jnp.mean(weighted * values, axis=-1, keepdims=True)
    )
    grad_gain = jnp.sum(grad_normed * values * factor, axis=0)
    return (grad_values, grad_gain)


def window_mask(row_start, block_rows, key_pos, length):
    query_pos = row_start + jnp.arange(block_rows, dtype=jnp.int32)
    distance = query_pos[:, None] - key_pos[None, :]
    return (distance >= 0) & (distance < WINDOW) & (key_pos < length)[None, :]


def attention_forward(queries, key_rot, values, length, block_rows):
    seq_len, heads_here, head_dim = queries.shape
    score_scale = 1.0 / math.sqrt(head_dim)
    key_pos = jnp.arange(seq_len, dtype=jnp.int32)

    def one_block(block_index):
        row_start = block_index * block_rows
        query_part = lax.dynamic_slice_in_dim(queries, row_start, block_rows, 0)
        scores = (
            jnp.einsum("qhd,khd->hqk", query_part, key_rot, preferred_element_type=jnp.float32)
            * score_scale
        )
        allowed = window_mask(row_start, block_rows, key_pos, length)
        scores = jnp.where(allowed[None], scores, NEGATIVE)
        row_max = jnp.max(scores, axis=-1, keepdims=True)
        exponent = jnp.exp(scores - row_max)
        row_total = jnp.sum(exponent, axis=-1, keepdims=True)
        weights = (exponent / row_total).astype(jnp.bfloat16)
        attended = jnp.einsum("hqk,khd->qhd", weights, values, preferred_element_type=jnp.float32)
        return (attended.astype(jnp.bfloat16), (row_max + jnp.log(row_total))[..., 0])

    block_ids = jnp.arange(seq_len // block_rows, dtype=jnp.int32)
    attended, log_total = lax.map(one_block, block_ids)
    return (attended.reshape(seq_len, heads_here * head_dim), log_total)


def attention_backward(queries, key_rot, values, grad_out, log_total, length, block_rows):
    seq_len, heads_here, head_dim = queries.shape
    score_scale = 1.0 / math.sqrt(head_dim)
    key_pos = jnp.arange(seq_len, dtype=jnp.int32)

    def one_block(grad_carry, block_index):
        grad_keys, grad_values = grad_carry
        row_start = block_index * block_rows
        query_part = lax.dynamic_slice_in_dim(queries, row_start, block_rows, 0)
        grad_part = lax.dynamic_slice_in_dim(grad_out, row_start, block_rows, 0)
        scores = (
            jnp.einsum("qhd,khd->hqk", query_part, key_rot, preferred_element_type=jnp.float32)
            * score_scale
        )
        allowed = window_mask(row_start, block_rows, key_pos, length)
        scores = jnp.where(allowed[None], scores, NEGATIVE)
        probabilities = jnp.exp(scores - log_total[block_index][..., None])
        grad_probs = jnp.einsum(
            "qhd,khd->hqk", grad_part, values, preferred_element_type=jnp.float32
        )
        grad_scores = (
            probabilities
            * (grad_probs - jnp.sum(probabilities * grad_probs, axis=-1, keepdims=True))
        ).astype(jnp.bfloat16)
        grad_query = (
            jnp.einsum("hqk,khd->qhd", grad_scores, key_rot, preferred_element_type=jnp.float32)
            * score_scale
        )
        grad_keys = (
            grad_keys
            + jnp.einsum(
                "hqk,qhd->khd", grad_scores, query_part, preferred_element_type=jnp.float32
            )
            * score_scale
        )
        grad_values = grad_values + jnp.einsum(
            "hqk,qhd->khd",
            probabilities.astype(jnp.bfloat16),
            grad_part,
            preferred_element_type=jnp.float32,
        )
        return ((grad_keys, grad_values), grad_query)

    block_ids = jnp.arange(seq_len // block_rows, dtype=jnp.int32)
    zero_keys = jnp.zeros(queries.shape, jnp.float32)
    (grad_keys, grad_values), grad_queries = lax.scan(one_block, (zero_keys, zero_keys), block_ids)
    return (grad_queries.reshape(seq_len, heads_here, head_dim), grad_keys, grad_values)


def contract_rows(left, right):
    return lax.dot_general(
        left, right, (((0,), (0,)), ((), ())), preferred_element_type=jnp.float32
    )


def contract_cols(left, right):
    return lax.dot_general(
        left, right, (((1,), (1,)), ((), ())), preferred_element_type=jnp.float32
    )


def sequence_rows(rows):
    return lax.all_gather(rows, "seq", axis=0, tiled=True)


def body(
    tokens,
    lengths,
    cotangent,
    w_query,
    w_key,
    w_value,
    w_out,
    w_gate,
    w_up,
    w_down,
    gain_attn,
    gain_ffn,
):
    tok_rows = tokens.shape[0]
    seq_len = tok_rows * lax.axis_size("seq")
    head_width = w_query.shape[1]
    heads_here = head_width // HD
    block_rows = min(512, seq_len)
    length = lengths[0]
    local_pos = lax.axis_index("seq") * tok_rows + jnp.arange(tok_rows, dtype=jnp.int32)
    valid_mask = (local_pos < length).astype(jnp.float32)[:, None]
    cos_table, sine_table = rope_tables(seq_len, HD)
    query_w, key_w, value_w, out_cols, gate_w, up_w, down_w, attn_gain_low, ffn_gain_low = (
        lax.all_gather(w_query, "dp", axis=0, tiled=True),
        lax.all_gather(w_key, "dp", axis=0, tiled=True),
        lax.all_gather(w_value, "dp", axis=0, tiled=True),
        lax.all_gather(w_out, "dp", axis=0, tiled=True),
        lax.all_gather(w_gate, "dp", axis=0, tiled=True),
        lax.all_gather(w_up, "dp", axis=0, tiled=True),
        lax.all_gather(w_down, "dp", axis=0, tiled=True),
        lax.all_gather(gain_attn, "dp", axis=0, tiled=True),
        lax.all_gather(gain_ffn, "dp", axis=0, tiled=True),
    )
    attn_gain = attn_gain_low.astype(jnp.float32)
    ffn_gain = ffn_gain_low.astype(jnp.float32)
    tok_float = tokens.astype(jnp.float32)
    factor1 = norm_factor(tok_float)
    normed1 = (tok_float * factor1 * attn_gain).astype(jnp.bfloat16)
    full1 = sequence_rows(normed1)
    query_lin = jnp.dot(full1, query_w, preferred_element_type=jnp.float32).reshape(
        seq_len, heads_here, HD
    )
    key_lin = jnp.dot(full1, key_w, preferred_element_type=jnp.float32).reshape(
        seq_len, heads_here, HD
    )
    values = (
        jnp.dot(full1, value_w, preferred_element_type=jnp.float32)
        .astype(jnp.bfloat16)
        .reshape(seq_len, heads_here, HD)
    )
    queries = rotate(query_lin, cos_table, sine_table).astype(jnp.bfloat16)
    key_rot = rotate(key_lin, cos_table, sine_table).astype(jnp.bfloat16)
    attended_heads, log_total = attention_forward(queries, key_rot, values, length, block_rows)
    out_full = lax.all_gather(out_cols, "seq", axis=1, tiled=True)
    attended_tok = lax.all_to_all(attended_heads, "seq", split_axis=0, concat_axis=1, tiled=True)
    attn_branch = contract_cols(attended_tok, out_full)
    resid = tok_float + attn_branch
    factor2 = norm_factor(resid)
    normed2 = (resid * factor2 * ffn_gain).astype(jnp.bfloat16)
    full2 = sequence_rows(normed2)
    gate_pre = jnp.dot(full2, gate_w, preferred_element_type=jnp.float32)
    up_pre = jnp.dot(full2, up_w, preferred_element_type=jnp.float32)
    sigmoid_gate = jax.nn.sigmoid(gate_pre)
    silu_gate = gate_pre * sigmoid_gate
    activation = (silu_gate * up_pre).astype(jnp.bfloat16)
    ffn_branch = lax.psum_scatter(
        contract_cols(activation, down_w).astype(jnp.bfloat16),
        "seq",
        scatter_dimension=0,
        tiled=True,
    ).astype(jnp.float32)
    output = (valid_mask * (resid + ffn_branch)).astype(jnp.bfloat16)
    grad_sum = valid_mask * cotangent.astype(jnp.float32)
    grad_ffn = grad_sum.astype(jnp.bfloat16)
    grad_full = sequence_rows(grad_ffn)
    grad_w_down = contract_rows(grad_full, activation)
    grad_act = jnp.dot(grad_full, down_w, preferred_element_type=jnp.float32)
    grad_gate = (grad_act * up_pre * sigmoid_gate * (1.0 + gate_pre * (1.0 - sigmoid_gate))).astype(
        jnp.bfloat16
    )
    grad_up = (grad_act * silu_gate).astype(jnp.bfloat16)
    grad_w_gate = contract_rows(full2, grad_gate)
    grad_w_up = contract_rows(full2, grad_up)
    grad_normed2 = lax.psum_scatter(
        contract_cols(grad_gate, gate_w) + contract_cols(grad_up, up_w),
        "seq",
        scatter_dimension=0,
        tiled=True,
    )
    grad_norm2, grad_gain_ffn = norm_back(resid, factor2, ffn_gain, grad_normed2)
    grad_resid = grad_sum + grad_norm2
    grad_attn = grad_resid.astype(jnp.bfloat16)
    grad_attended = jnp.dot(grad_attn, out_full, preferred_element_type=jnp.float32).astype(
        jnp.bfloat16
    )
    grad_heads = lax.all_to_all(grad_attended, "seq", split_axis=1, concat_axis=0, tiled=True)
    grad_out_whole = contract_rows(grad_attn, attended_tok)
    grad_w_out = lax.psum_scatter(
        grad_out_whole.astype(jnp.bfloat16), "seq", scatter_dimension=1, tiled=True
    )
    grad_queries, grad_keys, grad_values = attention_backward(
        queries,
        key_rot,
        values,
        grad_heads.reshape(seq_len, heads_here, HD),
        log_total,
        length,
        block_rows,
    )
    grad_query_lin = (
        rotate(grad_queries, cos_table, -sine_table)
        .reshape(seq_len, head_width)
        .astype(jnp.bfloat16)
    )
    grad_key_lin = (
        rotate(grad_keys, cos_table, -sine_table).reshape(seq_len, head_width).astype(jnp.bfloat16)
    )
    grad_value_lin = grad_values.reshape(seq_len, head_width).astype(jnp.bfloat16)
    grad_w_query = contract_rows(full1, grad_query_lin)
    grad_w_key = contract_rows(full1, grad_key_lin)
    grad_w_value = contract_rows(full1, grad_value_lin)
    grad_normed1 = lax.psum_scatter(
        (
            contract_cols(grad_query_lin, query_w)
            + contract_cols(grad_key_lin, key_w)
            + contract_cols(grad_value_lin, value_w)
        ).astype(jnp.bfloat16),
        "seq",
        scatter_dimension=0,
        tiled=True,
    ).astype(jnp.float32)
    grad_norm1, grad_gain_attn = norm_back(tok_float, factor1, attn_gain, grad_normed1)
    grad_tokens = grad_resid + grad_norm1
    owned_query, owned_key, owned_value, owned_out, owned_gate, owned_up, owned_down = (
        lax.psum_scatter(
            grad_w_query.astype(jnp.bfloat16), "dp", scatter_dimension=0, tiled=True
        ).astype(jnp.float32),
        lax.psum_scatter(
            grad_w_key.astype(jnp.bfloat16), "dp", scatter_dimension=0, tiled=True
        ).astype(jnp.float32),
        lax.psum_scatter(
            grad_w_value.astype(jnp.bfloat16), "dp", scatter_dimension=0, tiled=True
        ).astype(jnp.float32),
        lax.psum_scatter(grad_w_out, "dp", scatter_dimension=0, tiled=True).astype(jnp.float32),
        lax.psum_scatter(
            grad_w_gate.astype(jnp.bfloat16), "dp", scatter_dimension=0, tiled=True
        ).astype(jnp.float32),
        lax.psum_scatter(
            grad_w_up.astype(jnp.bfloat16), "dp", scatter_dimension=0, tiled=True
        ).astype(jnp.float32),
        lax.psum_scatter(
            grad_w_down.astype(jnp.bfloat16), "dp", scatter_dimension=0, tiled=True
        ).astype(jnp.float32),
    )
    owned_gain_attn, owned_gain_ffn = (
        lax.psum_scatter(grad_gain_attn, ("dp", "seq"), scatter_dimension=0, tiled=True),
        lax.psum_scatter(grad_gain_ffn, ("dp", "seq"), scatter_dimension=0, tiled=True),
    )
    return (
        output,
        grad_tokens,
        owned_query,
        owned_key,
        owned_value,
        owned_out,
        owned_gate,
        owned_up,
        owned_down,
        owned_gain_attn,
        owned_gain_ffn,
    )


def solution(mesh):
    placed = (
        P(("dp", "seq"), None),
        P("dp"),
        P(("dp", "seq"), None),
        P("dp", "seq"),
        P("dp", "seq"),
        P("dp", "seq"),
        P("dp", "seq"),
        P("dp", "seq"),
        P("dp", "seq"),
        P("dp", "seq"),
        P("dp"),
        P("dp"),
    )
    return jax.shard_map(
        body,
        mesh=mesh,
        in_specs=placed,
        out_specs=(
            P(("dp", "seq"), None),
            P(("dp", "seq"), None),
            P("dp", "seq"),
            P("dp", "seq"),
            P("dp", "seq"),
            P("dp", "seq"),
            P("dp", "seq"),
            P("dp", "seq"),
            P("dp", "seq"),
            P(("dp", "seq")),
            P(("dp", "seq")),
        ),
        check_vma=False,
    )
```

profile of v0, /device:TPU:0, one launch (start us, length us, event | category | flops | bytes accessed | tf_op | source)
XLA Modules:
  0.0 1573.2 jit_solution(5223838790335341322)
XLA Ops:
  33.7 13.7 all-gather.16.cloned.1.call-done
  47.3 101.8 %all-gather.14.cloned.1.call-done = bf16[1536,2048]{1,0:T(8,128)(2,1)} async-done(((bf16[192,2048]{1,0:T(8,128)(2,1)}), bf16[1536,2048]{1,0:T(8,128)(2,1)}) %all-gather.14.cloned.1.call-update) | async-done | bytes 6291472 | tf_op jit(solution)/shard_map/all_gather | solution.py:147
  195.6 31.1 %while.30 = (s32[]{:T(128)}, bf16[3,512,2,128]{3,2,1,0:T(2,128)(2,1)}, f32[3,2,512]{2,1,0:T(2,128)}, s32[3]{0:T(128)S(1)}, s32[]{:T(128)}, /*index=5*/bf16[1536,...) while((s32[]{:T(128)}, ...), condition=%wide.region_4.5_spmd.clone.clone, body=%wide.region_1.4_spmd.clone.clone.sunk | while | flops 828244992 | bytes 24682684 | solution.py:81
  241.1 46.2 %all-to-all-done = bf16[8,192,256]{2,1,0:T(8,128)(2,1)} async-done(((bf16[8,192,256]{2,1,0:T(8,128)(2,1)}), bf16[8,192,256]{2,1,0:T(8,128)(2,1)}, u32[]{:S(2)}, u32[]{:S(2)}) %all-to-all-start) | async-done | bytes 786464 | tf_op jit(solution)/shard_map/all_to_all | solution.py:205
  289.3 37.2 %all-gather.24.cloned.1.call-done = bf16[2048,2048]{1,0:T(8,128)(2,1)} async-done(((bf16[2048,256]{1,0:T(8,128)(2,1)}), bf16[2048,2048]{1,0:T(8,128)(2,1)}) %all-gather.24.cloned.1.call-update) | async-done | bytes 8388624 | tf_op jit(solution)/shard_map/all_gather | solution.py:204
  338.7 23.2 %all-gather.28.cloned.1.call-done = bf16[2048,1024]{1,0:T(8,128)(2,1)} async-done(((bf16[512,1024]{1,0:T(8,128)(2,1)}), bf16[2048,1024]{1,0:T(8,128)(2,1)}) %all-gather.28.cloned.1.call-update) | async-done | bytes 4194320 | tf_op jit(solution)/shard_map/all_gather | solution.py:178
  361.9 101.8 %all-gather.26.cloned.1.call-done = bf16[1536,2048]{1,0:T(8,128)(2,1)} async-done(((bf16[192,2048]{1,0:T(8,128)(2,1)}), bf16[1536,2048]{1,0:T(8,128)(2,1)}) %all-gather.26.cloned.1.call-update) | async-done | bytes 6291472 | tf_op jit(solution)/shard_map/all_gather | solution.py:147
  475.6 22.4 %all-gather.30.cloned.1.call-done = bf16[2048,1024]{1,0:T(8,128)(2,1)} async-done(((bf16[512,1024]{1,0:T(8,128)(2,1)}), bf16[2048,1024]{1,0:T(8,128)(2,1)}) %all-gather.30.cloned.1.call-update) | async-done | bytes 4194320 | tf_op jit(solution)/shard_map/all_gather | solution.py:179
  509.8 24.2 %all-gather.32.cloned.1.call-done = bf16[2048,1024]{1,0:T(8,128)(2,1)} async-done(((bf16[512,1024]{1,0:T(8,128)(2,1)}), bf16[2048,1024]{1,0:T(8,128)(2,1)}) %all-gather.32.cloned.1.call-update) | async-done | bytes 4194320 | tf_op jit(solution)/shard_map/all_gather | solution.py:180
  534.0 101.8 %all-gather.34.cloned.1.call-done = bf16[1536,2048]{1,0:T(8,128)(2,1)} async-done(((bf16[192,2048]{1,0:T(8,128)(2,1)}), bf16[1536,2048]{1,0:T(8,128)(2,1)}) %all-gather.34.cloned.1.call-update) | async-done | bytes 6291472 | tf_op jit(solution)/shard_map/all_gather | solution.py:147
  635.8 15.0 multiply_convert_fusion.1
  660.1 12.8 convolution_add_fusion
  684.0 194.7 %reduce-scatter.14.cloned.1.call-done = f32[192,2048]{1,0:T(8,128)} async-done(((f32[1536,2048]{1,0:T(8,128)}), f32[192,2048]{1,0:T(8,128)}) %reduce-scatter.14.cloned.1.call-update) | async-done | bytes 1572880 | tf_op jit(solution)/shard_map/reduce_scatter | solution.py:234
  881.1 118.2 %reduce-scatter.12.cloned.1.call-done = bf16[192,2048]{1,0:T(8,128)(2,1)} async-done(((bf16[1536,2048]{1,0:T(8,128)(2,1)}), bf16[192,2048]{1,0:T(8,128)(2,1)}) %reduce-scatter.12.cloned.1.call-update) | async-done | bytes 786448 | tf_op jit(solution)/shard_map/reduce_scatter | solution.py:216
  1052.6 29.9 %all-to-all-done.1 = bf16[192,8,256]{2,0,1:T(8,128)(2,1)S(1)} async-done(((bf16[192,8,256]{2,0,1:T(8,128)(2,1)}), bf16[192,8,256]{2,0,1:T(8,128)(2,1)S(1)}, u32[]{:S(2)}, u32[]{:S(2)}) %all-to-all-start.1) | async-done | bytes 786464 | tf_op jit(solution)/shard_map/all_to_all | solution.py:246
  1082.7 79.9 %while.31 = (s32[]{:T(128)}, f32[1536,2,128]{0,2,1:T(8,128)}, f32[1536,2,128]{0,2,1:T(8,128)}, f32[3,512,2,128]{3,1,0,2:T(8,128)}, s32[3]{0:T(128)S(1)}, /*index...) while((s32[]{:T(128)}, f32[1536,2,128]{0,2,1:T(8,128)}, ...), condition=%wide.region_11.12_spmd.clone.clone, body=%wide.region_9.11_spmd.clone.clone.sunk | while | flops 2033452032 | bytes 141324320 | solution.py:130
  1204.9 12.2 add_convert_fusion
  1223.6 44.1 %reduce-scatter.30.cloned.1.call-done = bf16[512,1024]{1,0:T(8,128)(2,1)} async-done(((bf16[2048,1024]{1,0:T(8,128)(2,1)}), bf16[512,1024]{1,0:T(8,128)(2,1)}) %reduce-scatter.30.cloned.1.call-update) | async-done | bytes 1048592 | tf_op jit(solution)/shard_map/reduce_scatter | solution.py:298
  1270.5 44.2 %reduce-scatter.32.cloned.1.call-done = bf16[512,1024]{1,0:T(8,128)(2,1)} async-done(((bf16[2048,1024]{1,0:T(8,128)(2,1)}), bf16[512,1024]{1,0:T(8,128)(2,1)}) %reduce-scatter.32.cloned.1.call-update) | async-done | bytes 1048592 | tf_op jit(solution)/shard_map/reduce_scatter | solution.py:301
  1317.5 24.5 %reduce-scatter.20.cloned.1.call-done = bf16[512,256]{1,0:T(8,128)(2,1)} async-done(((bf16[2048,256]{1,0:T(8,128)(2,1)}), bf16[512,256]{1,0:T(8,128)(2,1)}) %reduce-scatter.20.cloned.1.call-update) | async-done | bytes 262160 | tf_op jit(solution)/shard_map/reduce_scatter | solution.py:288
  1343.8 25.9 %reduce-scatter.18.cloned.1.call-done = bf16[512,256]{1,0:T(8,128)(2,1)} async-done(((bf16[2048,256]{1,0:T(8,128)(2,1)}), bf16[512,256]{1,0:T(8,128)(2,1)}) %reduce-scatter.18.cloned.1.call-update) | async-done | bytes 262160 | tf_op jit(solution)/shard_map/reduce_scatter | solution.py:285
  1371.5 25.5 %reduce-scatter.22.cloned.1.call-done = bf16[512,256]{1,0:T(8,128)(2,1)} async-done(((bf16[2048,256]{1,0:T(8,128)(2,1)}), bf16[512,256]{1,0:T(8,128)(2,1)}) %reduce-scatter.22.cloned.1.call-update) | async-done | bytes 262160 | tf_op jit(solution)/shard_map/reduce_scatter | solution.py:291
  1398.8 120.2 %reduce-scatter.16.cloned.1.call-done = bf16[192,2048]{1,0:T(8,128)(2,1)} async-done(((bf16[1536,2048]{1,0:T(8,128)(2,1)}), bf16[192,2048]{1,0:T(8,128)(2,1)}) %reduce-scatter.16.cloned.1.call-update) | async-done | bytes 786448 | tf_op jit(solution)/shard_map/reduce_scatter | solution.py:272
  1520.6 39.6 %all-reduce.2 = (f32[2048]{0:T(1024)S(1)}, f32[2048]{0:T(1024)S(1)}) all-reduce(f32[2048]{0:T(1024)S(1)} %get-tuple-element.318, f32[2048]{0:T(1024)S(1)} %copy-done.28), channel_id=13, replica_groups=mesh['dp'=4,'seq'=8] {'dp','seq'}, use_global_device_ids=true, to_apply=%region_23.24.clone | all-reduce | flops 4096 | bytes 32768
  (303 shorter events, 367.3 us)
Async XLA Ops:
  7.2 21.9 %all-gather.22.cloned.1.call-start = ((), (), s32[]{:S(2)}) async-start(), calls=%async_computation.17 | async-start | bytes 1310720 | tf_op jit(solution)/shard_map/all_gather | solution.py:177
  7.9 39.4 %all-gather.16.cloned.1.call-start = ((), (), s32[]{:S(2)}) async-start(), calls=%async_computation.14 | async-start | bytes 1310720 | tf_op jit(solution)/shard_map/all_gather | solution.py:174
  8.7 140.5 %all-gather.14.cloned.1.call-start = ((), (), s32[]{:S(2)}) async-start(), calls=%async_computation.13 | async-start | bytes 7077888 | tf_op jit(solution)/shard_map/all_gather | solution.py:147
  19.7 145.8 %all-gather.18.cloned.1.call-start = ((), (), s32[]{:S(2)}) async-start(), calls=%async_computation.15 | async-start | bytes 1310720 | tf_op jit(solution)/shard_map/all_gather | solution.py:175
  20.3 163.4 %all-gather.20.cloned.1.call-start = ((), (), s32[]{:S(2)}) async-start(), calls=%async_computation.16 | async-start | bytes 1310720 | tf_op jit(solution)/shard_map/all_gather | solution.py:176
  20.9 305.7 %all-gather.24.cloned.1.call-start = ((), (), s32[]{:S(2)}) async-start(), calls=%async_computation.18 | async-start | bytes 9437184 | tf_op jit(solution)/shard_map/all_gather | solution.py:204
  29.1 332.9 %all-gather.28.cloned.1.call-start = ((), (), s32[]{:S(2)}) async-start(), calls=%async_computation.20 | async-start | bytes 5242880 | tf_op jit(solution)/shard_map/all_gather | solution.py:178
  230.5 56.8 %all-to-all-start = ((bf16[8,192,256]{2,1,0:T(8,128)(2,1)}), bf16[8,192,256]{2,1,0:T(8,128)(2,1)}, u32[]{:S(2)}, u32[]{:S(2)}) async-start(bf16[8,192,256]{2,1,0:T(8,128)(2,1)} %all_to_all.26), calls=%async_computation | async-start | bytes 1572864 | tf_op jit(solution)/shard_map/all_to_all | solution.py:205
  235.8 227.9 %all-gather.26.cloned.1.call-start = ((), (), s32[]{:S(2)}) async-start(), calls=%async_computation.19 | async-start | bytes 7077888 | tf_op jit(solution)/shard_map/all_gather | solution.py:147
  335.5 162.5 %all-gather.30.cloned.1.call-start = ((), (), s32[]{:S(2)}) async-start(), calls=%async_computation.21 | async-start | bytes 5242880 | tf_op jit(solution)/shard_map/all_gather | solution.py:179
  336.3 197.7 %all-gather.32.cloned.1.call-start = ((), (), s32[]{:S(2)}) async-start(), calls=%async_computation.22 | async-start | bytes 5242880 | tf_op jit(solution)/shard_map/all_gather | solution.py:180
  336.8 298.9 %all-gather.34.cloned.1.call-start = ((), (), s32[]{:S(2)}) async-start(), calls=%async_computation.24 | async-start | bytes 7077888 | tf_op jit(solution)/shard_map/all_gather | solution.py:147
  338.7 540.0 %reduce-scatter.14.cloned.1.call-start = ((), (), s32[]{:S(2)}) async-start(), calls=%async_computation.25 | async-start | bytes 14155776 | tf_op jit(solution)/shard_map/reduce_scatter | solution.py:234
  673.0 326.4 %reduce-scatter.12.cloned.1.call-start = ((), (), s32[]{:S(2)}) async-start(), calls=%async_computation.23 | async-start | bytes 7077888 | tf_op jit(solution)/shard_map/reduce_scatter | solution.py:216
  684.0 533.2 %reduce-scatter.24.cloned.1.call-start = ((), (), s32[]{:S(2)}) async-start(), calls=%async_computation.30 | async-start | bytes 9437184 | tf_op jit(solution)/shard_map/reduce_scatter | solution.py:248
  1008.5 212.2 %reduce-scatter.28.cloned.1.call-start = ((), (), s32[]{:S(2)}) async-start(), calls=%async_computation.32 | async-start | bytes 5242880 | tf_op jit(solution)/shard_map/reduce_scatter | solution.py:295
  1020.0 247.7 %reduce-scatter.30.cloned.1.call-start = ((), (), s32[]{:S(2)}) async-start(), calls=%async_computation.33 | async-start | bytes 5242880 | tf_op jit(solution)/shard_map/reduce_scatter | solution.py:298
  1037.5 44.9 %all-to-all-start.1 = ((bf16[192,8,256]{2,0,1:T(8,128)(2,1)}), bf16[192,8,256]{2,0,1:T(8,128)(2,1)S(1)}, u32[]{:S(2)}, u32[]{:S(2)}) async-start(bf16[192,8,256]{2,0,1:T(8,128)(2,1)} %bitcast.90), calls=%async_computation.3 | async-start | bytes 1572864 | tf_op jit(solution)/shard_map/all_to_all | solution.py:246
  1041.2 273.5 %reduce-scatter.32.cloned.1.call-start = ((), (), s32[]{:S(2)}) async-start(), calls=%async_computation.34 | async-start | bytes 5242880 | tf_op jit(solution)/shard_map/reduce_scatter | solution.py:301
  1052.5 289.5 %reduce-scatter.20.cloned.1.call-start = ((), (), s32[]{:S(2)}) async-start(), calls=%async_computation.28 | async-start | bytes 1310720 | tf_op jit(solution)/shard_map/reduce_scatter | solution.py:288
  1175.3 194.3 %reduce-scatter.18.cloned.1.call-start = ((), (), s32[]{:S(2)}) async-start(), calls=%async_computation.27 | async-start | bytes 1310720 | tf_op jit(solution)/shard_map/reduce_scatter | solution.py:285
  1182.1 214.9 %reduce-scatter.22.cloned.1.call-start = ((), (), s32[]{:S(2)}) async-start(), calls=%async_computation.29 | async-start | bytes 1310720 | tf_op jit(solution)/shard_map/reduce_scatter | solution.py:291
  1190.4 328.6 %reduce-scatter.16.cloned.1.call-start = ((), (), s32[]{:S(2)}) async-start(), calls=%async_computation.26 | async-start | bytes 7077888 | tf_op jit(solution)/shard_map/reduce_scatter | solution.py:272
  1217.1 347.1 %reduce-scatter.26.cloned.1.call-start = ((), (), s32[]{:S(2)}) async-start(), calls=%async_computation.31 | async-start | bytes 1310720 | tf_op jit(solution)/shard_map/reduce_scatter | solution.py:294
  (55 other events, 2375.8 us)
Sparse Core Ops, SparseCore 0:
  9.6 19.4 all-gather.21
  30.6 16.6 all-gather.15
  50.1 99.0 all-gather.13
  150.6 14.8 all-gather.17
  166.9 16.7 all-gather.19
  185.6 140.9 all-gather.23
  328.1 33.7 all-gather.27
  364.7 99.0 all-gather.25
  465.3 32.6 all-gather.29
  499.4 34.4 all-gather.31
  536.7 99.0 all-gather.33
  673.1 205.5 reduce-scatter.13
  882.3 117.0 reduce-scatter.11
  1008.7 165.9 reduce-scatter.23
  1177.2 43.5 reduce-scatter.27
  1223.2 44.4 reduce-scatter.29
  1270.2 44.4 reduce-scatter.31
  1317.1 24.8 reduce-scatter.19
  1344.7 24.9 reduce-scatter.17
  1372.1 24.8 reduce-scatter.21
  1401.0 117.9 reduce-scatter.15
  1521.7 24.0 reduce-scatter.25
where the time goes:
time: 1580 us; the launch traced here: 1570 us
  waiting for transfers between devices  1130 us (72%)
  matrix products  247 us (16%)
  other arithmetic  65.4 us (4%)
  blocking collectives  50.9 us (3%)
  local copies, waits for them, and re-layouts  41.8 us (3%)
  between operations  16 us (1%)
    all_gather x3, waiting for transfers between devices, sequence_rows(): return lax.all_gather(rows, 'seq', axis=0, tiled=True)  305 us
    reduce_scatter x1, waiting for transfers between devices, body(): lax.psum_scatter(contract_cols(grad_gate, gate_w) + contract_cols(grad_up...  195 us
    reduce_scatter x1, waiting for transfers between devices, body(): lax.psum_scatter((contract_cols(grad_query_lin, query_w) + contract_cols(...  120 us
    reduce_scatter x1, waiting for transfers between devices, body(): lax.psum_scatter(contract_cols(activation, down_w).astype(jnp.bfloat16),...  118 us
    dot_general x7, matrix products, contract_cols(): lax.dot_general(left, right, (((1,), (1,)), ((), ())), preferred_element_...  66.3 us
    dot_general x7, matrix products, contract_rows(): lax.dot_general(left, right, (((0,), (0,)), ((), ())), preferred_element_...  57.6 us
    all_to_all x1, waiting for transfers between devices, body(): lax.all_to_all(attended_heads, 'seq', split_axis=0, concat_axis=1, tiled=...  46.2 us
    reduce_scatter x1, waiting for transfers between devices, body(): lax.psum_scatter(grad_w_down.astype(jnp.bfloat16), 'dp', scatter_dimensio...  44.2 us
  transfers between devices with their start and end apart: 24, of which 22 were waited for; matrix products, arithmetic and copies ran while one was open for 19% of the time, Pallas kernels for 0%

commit v1 on v0

v1 whole, which is shorter than its diff:
```python
import functools
import math

import jax
import jax.numpy as jnp
import numpy as np
from jax import lax
from jax.experimental import pallas as pl
from jax.experimental.pallas import tpu as pltpu
from jax.sharding import PartitionSpec as P

HD = 128
WINDOW = 2048
EPSILON = 1e-05
NEGATIVE = -1e30
LINE = 4
MESH = pl.DeviceIdType.MESH
VMEM_LIMIT = 60 * 1024 * 1024


def ring_index(place, count):
    columns = count // LINE
    column = place // LINE
    level = place % LINE
    odd = column % 2
    return (level + odd * (LINE - 1 - 2 * level)) * columns + column


def ring_place(index, count):
    columns = count // LINE
    level = index // columns
    column = index % columns
    odd = column % 2
    return column * LINE + level + odd * (LINE - 1 - 2 * level)


class Ring:
    def __init__(self, count):
        self.count = count
        self.half = count // 2
        self.index = lax.axis_index("seq")
        self.place = ring_place(self.index, count)
        self.next = (self.shifted(1), self.shifted(-1))

    def shifted(self, offset):
        return ring_index((self.place + offset + self.count) % self.count, self.count)

    def greet(self):
        barrier = pltpu.get_barrier_semaphore()
        for other in self.next:
            pl.semaphore_signal(barrier, inc=1, device_id={"seq": other}, device_id_type=MESH)
        pl.semaphore_wait(barrier, 2)


class RingGather:
    def __init__(self, ring, own, full, send, recv, local, parts=2):
        self.ring, self.own, self.full = ring, own, full
        self.send, self.recv, self.local = send, recv, local
        self.rows = own.shape[0]
        self.parts = parts

    @staticmethod
    def semaphores(count, parts=2):
        shape = (2, count // 2, parts)
        return [pltpu.SemaphoreType.DMA(shape), pltpu.SemaphoreType.DMA(shape), pltpu.SemaphoreType.DMA]

    def part_range(self, way, step):
        if step < self.ring.half - 1:
            return range(self.parts)
        middle = self.parts // 2
        return range(middle) if way == 0 else range(middle, self.parts)

    def copy(self, way, step, part):
        size = self.rows // self.parts
        owner = self.ring.shifted(step if way else -step)
        place = self.full.at[pl.ds(pl.multiple_of(owner * self.rows + part * size, size), size)]
        source = self.own.at[pl.ds(part * size, size)] if step == 0 else place
        return pltpu.make_async_remote_copy(
            src_ref=source,
            dst_ref=place,
            send_sem=self.send.at[way, step, part],
            recv_sem=self.recv.at[way, step, part],
            device_id={"seq": self.ring.next[way]},
            device_id_type=MESH,
        )

    def keep(self):
        place = self.full.at[pl.ds(pl.multiple_of(self.ring.index * self.rows, self.rows), self.rows)]
        return pltpu.make_async_copy(self.own, place, self.local)

    def start(self):
        for part in range(self.parts):
            for way in range(2):
                if part in self.part_range(way, 0):
                    self.copy(way, 0, part).start()
        self.keep().start()

    def advance(self, step):
        for part in range(self.parts):
            for way in range(2):
                if part in self.part_range(way, step - 1):
                    self.copy(way, step - 1, part).wait_recv()
                if step < self.ring.half and part in self.part_range(way, step):
                    self.copy(way, step, part).start()

    def finish(self):
        for step in range(self.ring.half):
            for way in range(2):
                for part in self.part_range(way, step):
                    self.copy(way, step, part).wait_send()
        self.keep().wait()


class RingReduce:
    def __init__(self, ring, own, slots, send, recv, parts=2):
        self.ring, self.own, self.slots = ring, own, slots
        self.send, self.recv = send, recv
        self.rows = slots.shape[2]
        self.parts = parts
        self.size = self.rows // parts

    @staticmethod
    def scratch(count, rows, width, parts=2):
        shape = (2, count // 2, parts)
        return [
            pltpu.VMEM((2, count // 2, rows, width), jnp.bfloat16),
            pltpu.SemaphoreType.DMA(shape),
            pltpu.SemaphoreType.DMA(shape),
        ]

    def part_range(self, way, step):
        if step > 0:
            return range(self.parts)
        middle = self.parts // 2
        return range(middle) if way == 0 else range(middle, self.parts)

    def target(self, way, step):
        left = self.ring.half - step
        return self.ring.shifted(-left if way else left)

    def mine(self, index, part):
        return pl.ds(pl.multiple_of(index * self.rows + part * self.size, self.size), self.size)

    def slot(self, way, step, part):
        return self.slots.at[way, step, pl.ds(part * self.size, self.size)]

    def copy(self, way, step, part):
        if step == 0 or (step == 1 and part not in self.part_range(way, 0)):
            source = self.own.at[self.mine(self.target(way, step), part)]
        else:
            source = self.slot(way, step - 1, part)
        return pltpu.make_async_remote_copy(
            src_ref=source,
            dst_ref=self.slot(way, step, part),
            send_sem=self.send.at[way, step, part],
            recv_sem=self.recv.at[way, step, part],
            device_id={"seq": self.ring.next[way]},
            device_id_type=MESH,
        )

    def start(self):
        for way in range(2):
            for part in self.part_range(way, 0):
                self.copy(way, 0, part).start()

    def advance(self, step):
        order = [(way, part) for part in range(self.parts) for way in range(2)]
        if step == 1:
            for way, part in order:
                if part not in self.part_range(way, 0):
                    self.copy(way, 1, part).start()
        for way, part in order:
            if part in self.part_range(way, step - 1):
                self.copy(way, step - 1, part).wait_recv()
                slot = self.slot(way, step - 1, part)
                mine = self.own[self.mine(self.target(way, step), part), :]
                slot[...] = (slot[...].astype(jnp.float32) + mine.astype(jnp.float32)).astype(slot.dtype)
                self.copy(way, step, part).start()

    def total(self, part):
        last = self.ring.half - 1
        for way in range(2):
            self.copy(way, last, part).wait_recv()
        mine = self.own[self.mine(self.ring.index, part), :].astype(jnp.float32)
        return (
            mine
            + self.slot(0, last, part)[...].astype(jnp.float32)
            + self.slot(1, last, part)[...].astype(jnp.float32)
        )

    def finish(self):
        for step in range(self.ring.half):
            for way in range(2):
                for part in self.part_range(way, step):
                    self.copy(way, step, part).wait_send()


def gather_kernel(count, own, full, *semaphores):
    ring = Ring(count)
    ring.greet()
    gather = RingGather(ring, own, full, *semaphores)
    gather.start()
    for step in range(1, ring.half + 1):
        gather.advance(step)
    gather.finish()


def ring_gather(rows, collective_id):
    count = lax.axis_size("seq")
    any_space = pl.BlockSpec(memory_space=pl.ANY)
    return pl.pallas_call(
        functools.partial(gather_kernel, count),
        out_shape=jax.ShapeDtypeStruct((count * rows.shape[0], rows.shape[1]), rows.dtype),
        in_specs=[any_space],
        out_specs=any_space,
        scratch_shapes=RingGather.semaphores(count),
        compiler_params=pltpu.CompilerParams(collective_id=collective_id, has_side_effects=True),
        cost_estimate=pl.CostEstimate(flops=0, bytes_accessed=200_000_000, transcendentals=0),
    )(rows)


def reduce_kernel(count, partial, total, own, load, *scratch):
    ring = Ring(count)
    loaded = pltpu.make_async_copy(partial, own, load)
    loaded.start()
    ring.greet()
    loaded.wait()
    reduce = RingReduce(ring, own, *scratch)
    reduce.start()
    for step in range(1, ring.half):
        reduce.advance(step)
    for part in range(reduce.parts):
        total[pl.ds(part * reduce.size, reduce.size), :] = reduce.total(part)
    reduce.finish()


def ring_reduce(partial, collective_id):
    count = lax.axis_size("seq")
    rows, width = partial.shape[0] // count, partial.shape[1]
    return pl.pallas_call(
        functools.partial(reduce_kernel, count),
        out_shape=jax.ShapeDtypeStruct((rows, width), jnp.float32),
        in_specs=[pl.BlockSpec(memory_space=pl.ANY)],
        out_specs=pl.BlockSpec(memory_space=pltpu.VMEM),
        scratch_shapes=[
            pltpu.VMEM(partial.shape, partial.dtype),
            pltpu.SemaphoreType.DMA,
            *RingReduce.scratch(count, rows, width),
        ],
        compiler_params=pltpu.CompilerParams(
            collective_id=collective_id, has_side_effects=True, vmem_limit_bytes=VMEM_LIMIT
        ),
        cost_estimate=pl.CostEstimate(flops=0, bytes_accessed=200_000_000, transcendentals=0),
    )(partial)


def rope_tables(seq_len):
    half_dim = HD // 2
    steps = np.arange(half_dim, dtype=np.float32) * np.float32(2.0 / HD)
    frequency = np.exp(np.float32(-math.log(10000.0)) * steps)
    angles = np.arange(seq_len, dtype=np.float32)[:, None] * frequency[None, :]
    cos, sin = np.cos(angles), np.sin(angles)
    return (
        np.concatenate([cos, cos], axis=1).astype(np.float32),
        np.concatenate([-sin, sin], axis=1).astype(np.float32),
    )


def turned(values, cos, sin):
    return values * cos + pltpu.roll(values, HD // 2, 1) * sin


def turned_back(values, cos, sin):
    return values * cos - pltpu.roll(values, HD // 2, 1) * sin


def dot(left, right, left_dim=1, right_dim=0):
    return lax.dot_general(
        left, right, (((left_dim,), (right_dim,)), ((), ())), preferred_element_type=jnp.float32
    )


def softmax_block(queries, keys, start, length):
    rows, count = queries.shape[0], keys.shape[0]
    scores = dot(queries, keys, 1, 1) * (1.0 / math.sqrt(HD))
    query_pos = start + lax.broadcasted_iota(jnp.int32, (rows, count), 0)
    key_pos = lax.broadcasted_iota(jnp.int32, (rows, count), 1)
    allowed = (key_pos <= query_pos) & (key_pos < length)
    if start + rows > WINDOW:
        allowed = allowed & (query_pos - key_pos < WINDOW)
    scores = jnp.where(allowed, scores, NEGATIVE)
    exponent = jnp.exp(scores - jnp.max(scores, axis=-1, keepdims=True))
    return exponent * (1.0 / jnp.sum(exponent, axis=-1, keepdims=True))


def attend_kernel(block, length, queries, keys, values, attended):
    seq_len, width = queries.shape
    limit = length[0]

    def one_head(head, carry):
        lanes = pl.ds(pl.multiple_of(head * HD, HD), HD)
        for start in range(0, seq_len, block):
            rows, upto = pl.ds(start, block), pl.ds(0, start + block)
            probs = softmax_block(queries[rows, lanes], keys[upto, lanes], start, limit)
            out = dot(probs.astype(jnp.bfloat16), values[upto, lanes])
            attended[rows, lanes] = out.astype(jnp.bfloat16)
        return carry

    lax.fori_loop(0, width // HD, one_head, 0)


def attend(length, queries, keys, values):
    vmem = pl.BlockSpec(memory_space=pltpu.VMEM)
    return pl.pallas_call(
        functools.partial(attend_kernel, 256),
        out_shape=jax.ShapeDtypeStruct(queries.shape, jnp.bfloat16),
        in_specs=[pl.BlockSpec(memory_space=pltpu.SMEM)] + [vmem] * 3,
        out_specs=vmem,
        compiler_params=pltpu.CompilerParams(vmem_limit_bytes=VMEM_LIMIT),
        cost_estimate=pl.CostEstimate(flops=8_000_000_000, bytes_accessed=4_000_000, transcendentals=0),
    )(length, queries, keys, values)


def attend_back_kernel(block, length, queries, keys, values, grad_out, cos, sin, out_q, out_k, out_v, sum_k, sum_v):
    seq_len, width = queries.shape
    limit = length[0]
    scale = 1.0 / math.sqrt(HD)

    def one_head(head, carry):
        lanes = pl.ds(pl.multiple_of(head * HD, HD), HD)
        sum_k[...] = jnp.zeros_like(sum_k)
        sum_v[...] = jnp.zeros_like(sum_v)
        for start in range(0, seq_len, block):
            rows, upto = pl.ds(start, block), pl.ds(0, start + block)
            query_part, grad_part = queries[rows, lanes], grad_out[rows, lanes]
            probs = softmax_block(query_part, keys[upto, lanes], start, limit)
            grad_probs = dot(grad_part, values[upto, lanes], 1, 1)
            inner = jnp.sum(probs * grad_probs, axis=-1, keepdims=True)
            grad_scores = (probs * (grad_probs - inner)).astype(jnp.bfloat16)
            sum_v[upto, :] += dot(probs.astype(jnp.bfloat16), grad_part, 0, 0)
            sum_k[upto, :] += dot(grad_scores, query_part, 0, 0)
            grad_query = dot(grad_scores, keys[upto, lanes]) * scale
            out_q[rows, lanes] = turned_back(grad_query, cos[rows, :], sin[rows, :]).astype(jnp.bfloat16)
        out_k[:, lanes] = turned_back(sum_k[...] * scale, cos[...], sin[...]).astype(jnp.bfloat16)
        out_v[:, lanes] = sum_v[...].astype(jnp.bfloat16)
        return carry

    lax.fori_loop(0, width // HD, one_head, 0)


def attend_back(length, queries, keys, values, grad_out, cos, sin):
    vmem = pl.BlockSpec(memory_space=pltpu.VMEM)
    seq_len = queries.shape[0]
    return pl.pallas_call(
        functools.partial(attend_back_kernel, 256),
        out_shape=[jax.ShapeDtypeStruct(queries.shape, jnp.bfloat16)] * 3,
        in_specs=[pl.BlockSpec(memory_space=pltpu.SMEM)] + [vmem] * 6,
        out_specs=[vmem] * 3,
        scratch_shapes=[pltpu.VMEM((seq_len, HD), jnp.float32)] * 2,
        compiler_params=pltpu.CompilerParams(vmem_limit_bytes=VMEM_LIMIT),
        cost_estimate=pl.CostEstimate(flops=20_000_000_000, bytes_accessed=8_000_000, transcendentals=0),
    )(length, queries, keys, values, grad_out, cos, sin)


def norm_factor(values):
    return lax.rsqrt(jnp.mean(values * values, axis=-1, keepdims=True) + EPSILON)


def norm_back(values, factor, gain, grad_normed):
    weighted = grad_normed * gain
    grad_values = factor * (
        weighted - values * factor * factor * jnp.mean(weighted * values, axis=-1, keepdims=True)
    )
    grad_gain = jnp.sum(grad_normed * values * factor, axis=0)
    return (grad_values, grad_gain)


def contract_rows(left, right):
    return lax.dot_general(
        left, right, (((0,), (0,)), ((), ())), preferred_element_type=jnp.float32
    )


def contract_cols(left, right):
    return lax.dot_general(
        left, right, (((1,), (1,)), ((), ())), preferred_element_type=jnp.float32
    )


def body(
    tokens,
    lengths,
    cotangent,
    w_query,
    w_key,
    w_value,
    w_out,
    w_gate,
    w_up,
    w_down,
    gain_attn,
    gain_ffn,
):
    tok_rows = tokens.shape[0]
    seq_len = tok_rows * lax.axis_size("seq")
    head_width = w_query.shape[1]
    heads_here = head_width // HD
    length = lengths[0]
    local_pos = lax.axis_index("seq") * tok_rows + jnp.arange(tok_rows, dtype=jnp.int32)
    valid_mask = (local_pos < length).astype(jnp.float32)[:, None]
    cos_table, sine_table = rope_tables(seq_len)
    cos_heads, sine_heads = np.tile(cos_table, (1, heads_here)), np.tile(sine_table, (1, heads_here))
    query_w, key_w, value_w, out_cols, gate_w, up_w, down_w, attn_gain_low, ffn_gain_low = (
        lax.all_gather(w_query, "dp", axis=0, tiled=True),
        lax.all_gather(w_key, "dp", axis=0, tiled=True),
        lax.all_gather(w_value, "dp", axis=0, tiled=True),
        lax.all_gather(w_out, "dp", axis=0, tiled=True),
        lax.all_gather(w_gate, "dp", axis=0, tiled=True),
        lax.all_gather(w_up, "dp", axis=0, tiled=True),
        lax.all_gather(w_down, "dp", axis=0, tiled=True),
        lax.all_gather(gain_attn, "dp", axis=0, tiled=True),
        lax.all_gather(gain_ffn, "dp", axis=0, tiled=True),
    )
    attn_gain = attn_gain_low.astype(jnp.float32)
    ffn_gain = ffn_gain_low.astype(jnp.float32)
    tok_float = tokens.astype(jnp.float32)
    factor1 = norm_factor(tok_float)
    normed1 = (tok_float * factor1 * attn_gain).astype(jnp.bfloat16)
    full1 = ring_gather(normed1, 1)
    query_lin = jnp.dot(full1, query_w, preferred_element_type=jnp.float32)
    key_lin = jnp.dot(full1, key_w, preferred_element_type=jnp.float32)
    values = jnp.dot(full1, value_w, preferred_element_type=jnp.float32).astype(jnp.bfloat16)

    def rotate(lin):
        halves = lin.reshape(seq_len, heads_here, 2, HD // 2)[:, :, ::-1].reshape(seq_len, head_width)
        return (lin * cos_heads + halves * sine_heads).astype(jnp.bfloat16)

    queries, key_rot = rotate(query_lin), rotate(key_lin)
    attended_heads = attend(lengths, queries, key_rot, values)
    out_full = lax.all_gather(out_cols, "seq", axis=1, tiled=True)
    attended_tok = lax.all_to_all(attended_heads, "seq", split_axis=0, concat_axis=1, tiled=True)
    attn_branch = contract_cols(attended_tok, out_full)
    resid = tok_float + attn_branch
    factor2 = norm_factor(resid)
    normed2 = (resid * factor2 * ffn_gain).astype(jnp.bfloat16)
    full2 = ring_gather(normed2, 2)
    gate_pre = jnp.dot(full2, gate_w, preferred_element_type=jnp.float32)
    up_pre = jnp.dot(full2, up_w, preferred_element_type=jnp.float32)
    sigmoid_gate = jax.nn.sigmoid(gate_pre)
    silu_gate = gate_pre * sigmoid_gate
    activation = (silu_gate * up_pre).astype(jnp.bfloat16)
    ffn_branch = ring_reduce(contract_cols(activation, down_w).astype(jnp.bfloat16), 4)
    output = (valid_mask * (resid + ffn_branch)).astype(jnp.bfloat16)
    grad_sum = valid_mask * cotangent.astype(jnp.float32)
    grad_ffn = grad_sum.astype(jnp.bfloat16)
    grad_full = ring_gather(grad_ffn, 3)
    grad_w_down = contract_rows(grad_full, activation)
    grad_act = jnp.dot(grad_full, down_w, preferred_element_type=jnp.float32)
    grad_gate = (grad_act * up_pre * sigmoid_gate * (1.0 + gate_pre * (1.0 - sigmoid_gate))).astype(
        jnp.bfloat16
    )
    grad_up = (grad_act * silu_gate).astype(jnp.bfloat16)
    grad_w_gate = contract_rows(full2, grad_gate)
    grad_w_up = contract_rows(full2, grad_up)
    grad_normed2 = ring_reduce(
        (contract_cols(grad_gate, gate_w) + contract_cols(grad_up, up_w)).astype(jnp.bfloat16), 5
    )
    grad_norm2, grad_gain_ffn = norm_back(resid, factor2, ffn_gain, grad_normed2)
    grad_resid = grad_sum + grad_norm2
    grad_attn = grad_resid.astype(jnp.bfloat16)
    grad_attended = jnp.dot(grad_attn, out_full, preferred_element_type=jnp.float32).astype(
        jnp.bfloat16
    )
    grad_heads = lax.all_to_all(grad_attended, "seq", split_axis=1, concat_axis=0, tiled=True)
    grad_out_whole = contract_rows(grad_attn, attended_tok)
    grad_w_out = lax.psum_scatter(
        grad_out_whole.astype(jnp.bfloat16), "seq", scatter_dimension=1, tiled=True
    )
    grad_query_lin, grad_key_lin, grad_value_lin = attend_back(
        lengths, queries, key_rot, values, grad_heads, cos_table, sine_table
    )
    grad_w_query = contract_rows(full1, grad_query_lin)
    grad_w_key = contract_rows(full1, grad_key_lin)
    grad_w_value = contract_rows(full1, grad_value_lin)
    grad_normed1 = ring_reduce(
        (
            contract_cols(grad_query_lin, query_w)
            + contract_cols(grad_key_lin, key_w)
            + contract_cols(grad_value_lin, value_w)
        ).astype(jnp.bfloat16),
        6,
    )
    grad_norm1, grad_gain_attn = norm_back(tok_float, factor1, attn_gain, grad_normed1)
    grad_tokens = grad_resid + grad_norm1
    owned_query, owned_key, owned_value, owned_out, owned_gate, owned_up, owned_down = (
        lax.psum_scatter(
            grad_w_query.astype(jnp.bfloat16), "dp", scatter_dimension=0, tiled=True
        ).astype(jnp.float32),
        lax.psum_scatter(
            grad_w_key.astype(jnp.bfloat16), "dp", scatter_dimension=0, tiled=True
        ).astype(jnp.float32),
        lax.psum_scatter(
            grad_w_value.astype(jnp.bfloat16), "dp", scatter_dimension=0, tiled=True
        ).astype(jnp.float32),
        lax.psum_scatter(grad_w_out, "dp", scatter_dimension=0, tiled=True).astype(jnp.float32),
        lax.psum_scatter(
            grad_w_gate.astype(jnp.bfloat16), "dp", scatter_dimension=0, tiled=True
        ).astype(jnp.float32),
        lax.psum_scatter(
            grad_w_up.astype(jnp.bfloat16), "dp", scatter_dimension=0, tiled=True
        ).astype(jnp.float32),
        lax.psum_scatter(
            grad_w_down.astype(jnp.bfloat16), "dp", scatter_dimension=0, tiled=True
        ).astype(jnp.float32),
    )
    owned_gain_attn, owned_gain_ffn = (
        lax.psum_scatter(grad_gain_attn, ("dp", "seq"), scatter_dimension=0, tiled=True),
        lax.psum_scatter(grad_gain_ffn, ("dp", "seq"), scatter_dimension=0, tiled=True),
    )
    return (
        output,
        grad_tokens,
        owned_query,
        owned_key,
        owned_value,
        owned_out,
        owned_gate,
        owned_up,
        owned_down,
        owned_gain_attn,
        owned_gain_ffn,
    )


def solution(mesh):
    placed = (
        P(("dp", "seq"), None),
        P("dp"),
        P(("dp", "seq"), None),
        P("dp", "seq"),
        P("dp", "seq"),
        P("dp", "seq"),
        P("dp", "seq"),
        P("dp", "seq"),
        P("dp", "seq"),
        P("dp", "seq"),
        P("dp"),
        P("dp"),
    )
    return jax.shard_map(
        body,
        mesh=mesh,
        in_specs=placed,
        out_specs=(
            P(("dp", "seq"), None),
            P(("dp", "seq"), None),
            P("dp", "seq"),
            P("dp", "seq"),
            P("dp", "seq"),
            P("dp", "seq"),
            P("dp", "seq"),
            P("dp", "seq"),
            P("dp", "seq"),
            P(("dp", "seq")),
            P(("dp", "seq")),
        ),
        check_vma=False,
    )
```

time: 1580 us -> 1000 us (0.63)
  waiting for transfers between devices: 1130 us -> 171 us
  Pallas kernels: 0 us -> 475 us
  matrix products: 247 us -> 185 us
  blocking collectives: 50.9 us -> 93 us
  other arithmetic: 65.4 us -> 34.8 us
  local copies, waits for them, and re-layouts: 41.8 us -> 15.8 us
    pallas_call x0 -> x8, Pallas kernels: none -> 475 us  [the longest x3 257 us: ring_gather(): pl.pallas_call(functools.partial(gather_kernel, count), out_shape=jax.Sha...]
    reduce_scatter x3 -> x0, waiting for transfers between devices: 433 us -> none  [the longest x1 195 us: body(): lax.psum_scatter(contract_cols(grad_gate, gate_w) + contract_cols(grad_up...]
    all_gather x3 -> x0, waiting for transfers between devices: 305 us -> none  [sequence_rows(): return lax.all_gather(rows, 'seq', axis=0, tiled=True)]
    dot_general x23 -> x2, matrix products: 73.8 us -> 12.1 us  [the longest x1 6.06 us: body(): query_lin = jnp.dot(full1, query_w, preferred_element_type=jnp.float32)]
    all_to_all x1, waiting for transfers between devices: 46.2 us -> 0.01 us  [body(): lax.all_to_all(attended_heads, 'seq', split_axis=0, concat_axis=1, tiled=...]
    reduce_scatter x1, waiting for transfers between devices: 44.2 us -> 0.71 us  [body(): lax.psum_scatter(grad_w_down.astype(jnp.bfloat16), 'dp', scatter_dimensio...]
    all_to_all x0 -> x1, blocking collectives: none -> 42.8 us  [body(): lax.all_to_all(grad_attended, 'seq', split_axis=1, concat_axis=0, tiled=T...]
    reduce_scatter x1, waiting for transfers between devices: 2.92 us -> 44.1 us  [body(): lax.psum_scatter(grad_w_gate.astype(jnp.bfloat16), 'dp', scatter_dimensio...]
  transfers between devices with their start and end apart: 24 -> 17, of which waited for: 22 -> 6; matrix products, arithmetic and copies ran while one was open for 19% -> 17% of each run, Pallas kernels for 0% -> 35%
where the time goes in v1:
time: 1000 us; the launch traced here: 994 us
  Pallas kernels  475 us (48%)
  matrix products  185 us (18%)
  waiting for transfers between devices  171 us (17%)
  blocking collectives  93 us (9%)
  other arithmetic  34.8 us (3%)
  local copies, waits for them, and re-layouts  15.8 us (2%)
  between operations  15.3 us (2%)
    pallas_call x3, Pallas kernels, ring_gather(): pl.pallas_call(functools.partial(gather_kernel, count), out_shape=jax.Sha...  257 us
    pallas_call x3, Pallas kernels, ring_reduce(): pl.pallas_call(functools.partial(reduce_kernel, count), out_shape=jax.Sha...  190 us
    dot_general x7, matrix products, contract_cols(): lax.dot_general(left, right, (((1,), (1,)), ((), ())), preferred_element_...  64.4 us
    dot_general x7, matrix products, contract_rows(): lax.dot_general(left, right, (((0,), (0,)), ((), ())), preferred_element_...  57 us
    reduce_scatter x1, waiting for transfers between devices, body(): lax.psum_scatter(grad_w_up.astype(jnp.bfloat16), 'dp', scatter_dimension=...  44.2 us
    reduce_scatter x1, waiting for transfers between devices, body(): lax.psum_scatter(grad_w_gate.astype(jnp.bfloat16), 'dp', scatter_dimensio...  44.1 us
    all_to_all x1, blocking collectives, body(): lax.all_to_all(grad_attended, 'seq', split_axis=1, concat_axis=0, tiled=T...  42.8 us
    unnamed x1, blocking collectives  39.9 us
  transfers between devices with their start and end apart: 17, of which 6 were waited for; matrix products, arithmetic and copies ran while one was open for 17% of the time, Pallas kernels for 35%

profile of v1, /device:TPU:0, one launch (start us, length us, event | category | flops | bytes accessed | tf_op | source)
XLA Modules:
  0.0 994.5 jit_solution(17105038826507161330)
XLA Ops:
  10.0 19.0 %all-gather.17.cloned.1.call-done = bf16[2048,256]{1,0:T(8,128)(2,1)} async-done(((bf16[512,256]{1,0:T(8,128)(2,1)}), bf16[2048,256]{1,0:T(8,128)(2,1)}) %all-gather.17.cloned.1.call-update) | async-done | bytes 1048592 | tf_op jit(solution)/shard_map/all_gather | solution.py:417
  38.2 78.4 %shard_map.239 = bf16[1536,2048]{1,0:T(8,128)(2,1)} custom-call(bf16[192,2048]{1,0:T(8,128)(2,1)} %fusion.3.own), custom_call_target="tpu_custom_call" | custom-call | bytes 200000000 | tf_op jit(solution)/shard_map/pallas_call | solution.py:211
  152.1 10.6 %shard_map.240 = bf16[1536,256]{1,0:T(8,128)(2,1)} custom-call(s32[1]{0:T(128)} %copy.48.length, bf16[1536,256]{1,0:T(8,128)(2,1)} %get-tuple-element.29.queries, bf16[1536,256]{1,0:T(8,128)(2,1)} %get-tuple-element.28.keys, bf16[1536,256]{1,0:T(8,128)(2,1)} %convolution_convert_fusion.8.values), custom_call_target="tpu_custom_call" | custom-call | flops 8000000000 | bytes 4000000 | tf_op jit(solution)/shard_map/pallas_call | solution.py:314
  173.6 116.7 %shard_map.243 = bf16[1536,2048]{1,0:T(8,128)(2,1)} custom-call(bf16[192,2048]{1,0:T(8,128)(2,1)} %fusion.12.own), custom_call_target="tpu_custom_call" | custom-call | bytes 200000000 | tf_op jit(solution)/shard_map/pallas_call | solution.py:211
  298.3 61.5 %shard_map.241 = bf16[1536,2048]{1,0:T(8,128)(2,1)} custom-call(bf16[192,2048]{1,0:T(8,128)(2,1)} %multiply_convert_fusion.4.own), custom_call_target="tpu_custom_call" | custom-call | bytes 200000000 | tf_op jit(solution)/shard_map/pallas_call | solution.py:211
  359.8 12.1 %fusion.18 = f32[1536,1024]{1,0:T(8,128)} fusion(bf16[1536,2048]{1,0:T(8,128)(2,1)} %shard_map.241, bf16[2048,1024]{1,0:T(8,128)(2,1)} %all-gather.23.cloned.1.call-done), kind=kOutput, calls=%fused_computation.56 | convolution fusion | flops 6442450944 | bytes 16777216 | tf_op jit(solution)/shard_map/dot_general | solution.py:448
  371.9 11.7 %fusion.17 = f32[1536,1024]{1,0:T(8,128)} fusion(bf16[1536,2048]{1,0:T(8,128)(2,1)} %shard_map.241, bf16[2048,1024]{1,0:T(8,128)(2,1)} %all-gather.21.cloned.1.call-done), kind=kOutput, calls=%fused_computation.55 | convolution fusion | flops 6442450944 | bytes 16777216 | tf_op jit(solution)/shard_map/dot_general | solution.py:447
  383.6 16.7 %multiply_convert_fusion = (bf16[1536,1024]{1,0:T(8,128)(2,1)}, bf16[1536,1024]{1,0:T(8,128)(2,1)}, bf16[1536,1024]{1,0:T(8,128)(2,1)S(1)}) fusion(f32[1536,1024]{1,0:T(8,128)} %fusion.17, f32[1536,1024]{1,0:T(8,128)} %fusion.18, bf16[1536,2048]{1,0:T(8,128)(2,1)} %shard_map.243, bf16[2048,1024]{1,0:T(8,128)(2,1)} %all-gather.25.cloned.1.call-done), kind=kOutput, calls=%fused_computation.4 | convolution fusion | flops 6466043904 | bytes 32505856 | tf_op jit(solution)/shard_map/dot_general | solution.py:458
  410.9 60.4 %shard_map.242 = f32[192,2048]{1,0:T(8,128)} custom-call(bf16[1536,2048]{1,0:T(8,128)(2,1)} %convolution_convert_fusion.partial), custom_call_target="tpu_custom_call" | custom-call | bytes 200000000 | tf_op jit(solution)/shard_map/pallas_call | solution.py:240
  471.3 12.4 %fusion.19 = f32[1536,2048]{1,0:T(8,128)} fusion(bf16[1536,1024]{1,0:T(8,128)(2,1)} %get-tuple-element.24, bf16[2048,1024]{1,0:T(8,128)(2,1)} %all-gather.21.cloned.1.call-done), kind=kOutput, calls=%fused_computation.57 | convolution fusion | flops 6442450944 | bytes 19922944 | tf_op jit(solution)/shard_map/dot_general | solution.py:385
  483.7 11.5 %add_convert_fusion.1.partial = bf16[1536,2048]{1,0:T(8,128)(2,1)} fusion(f32[1536,2048]{1,0:T(8,128)} %fusion.19, bf16[1536,1024]{1,0:T(8,128)(2,1)S(1)} %copy-done.26, bf16[2048,1024]{1,0:T(8,128)(2,1)S(1)} %copy-done.24), kind=kOutput, calls=%fused_computation.1 | convolution fusion | flops 6448742400 | bytes 26214400 | tf_op jit(solution)/shard_map/dot_general | solution.py:385
  495.2 62.8 %shard_map.244 = f32[192,2048]{1,0:T(8,128)} custom-call(bf16[1536,2048]{1,0:T(8,128)(2,1)} %add_convert_fusion.1.partial), custom_call_target="tpu_custom_call" | custom-call | bytes 200000000 | tf_op jit(solution)/shard_map/pallas_call | solution.py:240
  574.0 42.8 %all_to_all.38 = bf16[192,8,256]{2,0,1:T(8,128)(2,1)} all-to-all(bf16[192,8,256]{2,0,1:T(8,128)(2,1)S(1)} %bitcast.66), channel_id=1, replica_groups=mesh['dp'=4,'seq'=8] {'seq'}, dimensions={1} | all-to-all | bytes 1572864 | tf_op jit(solution)/shard_map/all_to_all | solution.py:474
  616.8 17.7 %shard_map.245 = (bf16[1536,256]{1,0:T(8,128)(2,1)}, bf16[1536,256]{1,0:T(8,128)(2,1)}, bf16[1536,256]{1,0:T(8,128)(2,1)}) custom-call(s32[1]{0:T(128)} %copy.48.length, bf16[1536,256]{1,0:T(8,128)(2,1)} %get-tuple-element.29.queries, bf16[1536,256]{1,0:T(8,128)(2,1)} %get-tuple-element.28.keys, bf16[1536,256]{1,0:T(8,128)(2,1)} %convolution_convert_fusion.8.values, ...), custom_call_target="tpu_custom_call" | custom-call | flops 20000000000 | bytes 8000000 | tf_op jit(solution)/shard_map/pallas_call | solution.py:354
  652.3 11.3 %convolution_convert_fusion.2 = bf16[2048,1024]{1,0:T(8,128)(2,1)} fusion(bf16[1536,2048]{1,0:T(8,128)(2,1)} %shard_map.243, bf16[1536,1024]{1,0:T(8,128)(2,1)} %copy-done.27), kind=kOutput, calls=%fused_computation.9 | convolution fusion | flops 6444548096 | bytes 13631488 | tf_op jit(solution)/shard_map/dot_general | solution.py:379
  663.7 11.2 %convolution_convert_fusion.3 = bf16[2048,1024]{1,0:T(8,128)(2,1)} fusion(bf16[1536,2048]{1,0:T(8,128)(2,1)} %shard_map.241, bf16[1536,1024]{1,0:T(8,128)(2,1)} %get-tuple-element.23), kind=kOutput, calls=%fused_computation.10 | convolution fusion | flops 6444548096 | bytes 13631488 | tf_op jit(solution)/shard_map/dot_general | solution.py:379
  675.0 11.4 %convolution_convert_fusion.4 = bf16[2048,1024]{1,0:T(8,128)(2,1)} fusion(bf16[1536,2048]{1,0:T(8,128)(2,1)} %shard_map.241, bf16[1536,1024]{1,0:T(8,128)(2,1)} %get-tuple-element.24), kind=kOutput, calls=%fused_computation.11 | convolution fusion | flops 6444548096 | bytes 13631488 | tf_op jit(solution)/shard_map/dot_general | solution.py:379
  700.3 33.3 %reduce-scatter.15.cloned.1.call-done = bf16[2048,256]{1,0:T(8,128)(2,1)} async-done(((bf16[2048,2048]{1,0:T(8,128)(2,1)}), bf16[2048,256]{1,0:T(8,128)(2,1)}) %reduce-scatter.15.cloned.1.call-update) | async-done | bytes 1048592 | tf_op jit(solution)/shard_map/reduce_scatter | solution.py:476
  733.7 12.1 %add_convert_fusion.partial = bf16[1536,2048]{1,0:T(8,128)(2,1)} fusion(f32[1536,2048]{1,0:T(8,128)} %fusion.20, f32[1536,2048]{1,0:T(8,128)} %fusion.21, bf16[1536,256]{1,0:T(8,128)(2,1)S(1)} %copy-done.17, bf16[2048,256]{1,0:T(8,128)(2,1)S(1)} %copy-done.14), kind=kOutput, calls=%fused_computation | convolution fusion | flops 1620049920 | bytes 33292288 | tf_op jit(solution)/shard_map/dot_general | solution.py:385
  745.8 66.6 %shard_map.246 = f32[192,2048]{1,0:T(8,128)} custom-call(bf16[1536,2048]{1,0:T(8,128)(2,1)} %add_convert_fusion.partial), custom_call_target="tpu_custom_call" | custom-call | bytes 200000000 | tf_op jit(solution)/shard_map/pallas_call | solution.py:240
  814.6 39.9 %all-reduce.2 = (f32[2048]{0:T(1024)S(1)}, f32[2048]{0:T(1024)S(1)}) all-reduce(f32[2048]{0:T(1024)S(1)} %get-tuple-element.19, f32[2048]{0:T(1024)S(1)} %get-tuple-element.17), channel_id=10, replica_groups=mesh['dp'=4,'seq'=8] {'dp','seq'}, use_global_device_ids=true, to_apply=%region_13.0.clone | all-reduce | flops 4096 | bytes 32768
  867.3 44.2 %reduce-scatter.21.cloned.1.call-done = bf16[512,1024]{1,0:T(8,128)(2,1)} async-done(((bf16[2048,1024]{1,0:T(8,128)(2,1)}), bf16[512,1024]{1,0:T(8,128)(2,1)}) %reduce-scatter.21.cloned.1.call-update) | async-done | bytes 1048592 | tf_op jit(solution)/shard_map/reduce_scatter | solution.py:509
  914.3 44.1 %reduce-scatter.19.cloned.1.call-done = bf16[512,1024]{1,0:T(8,128)(2,1)} async-done(((bf16[2048,1024]{1,0:T(8,128)(2,1)}), bf16[512,1024]{1,0:T(8,128)(2,1)}) %reduce-scatter.19.cloned.1.call-update) | async-done | bytes 1048592 | tf_op jit(solution)/shard_map/reduce_scatter | solution.py:506
  961.2 24.7 %reduce-scatter.17.cloned.1.call-done = bf16[512,256]{1,0:T(8,128)(2,1)} async-done(((bf16[2048,256]{1,0:T(8,128)(2,1)}), bf16[512,256]{1,0:T(8,128)(2,1)}) %reduce-scatter.17.cloned.1.call-update) | async-done | bytes 262160 | tf_op jit(solution)/shard_map/reduce_scatter | solution.py:505
  (149 shorter events, 146.1 us)
Async XLA Ops:
  7.2 23.9 %copy-start.22 = (bf16[512]{0:T(512)(128)(2,1)S(1)}, bf16[512]{0:T(512)(128)(2,1)}, u32[]{:S(2)}) copy-start(bf16[512]{0:T(512)(128)(2,1)} %param.26) | copy-start | bytes 3076
  7.2 29.1 %copy-start.2 = (bf16[192,2048]{1,0:T(8,128)(2,1)S(1)}, bf16[192,2048]{1,0:T(8,128)(2,1)}, u32[]{:S(2)}) copy-start(bf16[192,2048]{1,0:T(8,128)(2,1)} %param.16) | copy-start | bytes 2359300
  7.2 21.8 %all-gather.17.cloned.1.call-start = ((), (), s32[]{:S(2)}) async-start(), calls=%async_computation.13 | async-start | bytes 1310720 | tf_op jit(solution)/shard_map/all_gather | solution.py:417
  7.9 108.7 %all-gather.11.cloned.1.call-start = ((), (), s32[]{:S(2)}) async-start(), calls=%async_computation.10 | async-start | bytes 1310720 | tf_op jit(solution)/shard_map/all_gather | solution.py:414
  8.7 116.0 %all-gather.13.cloned.1.call-start = ((), (), s32[]{:S(2)}) async-start(), calls=%async_computation.11 | async-start | bytes 1310720 | tf_op jit(solution)/shard_map/all_gather | solution.py:415
  9.4 134.8 %all-gather.15.cloned.1.call-start = ((), (), s32[]{:S(2)}) async-start(), calls=%async_computation.12 | async-start | bytes 1310720 | tf_op jit(solution)/shard_map/all_gather | solution.py:416
  10.0 280.5 %all-gather.19.cloned.1.call-start = ((), (), s32[]{:S(2)}) async-start(), calls=%async_computation.14 | async-start | bytes 9437184 | tf_op jit(solution)/shard_map/all_gather | solution.py:440
  29.1 330.7 %all-gather.23.cloned.1.call-start = ((), (), s32[]{:S(2)}) async-start(), calls=%async_computation.16 | async-start | bytes 5242880 | tf_op jit(solution)/shard_map/all_gather | solution.py:419
  29.6 342.3 %all-gather.21.cloned.1.call-start = ((), (), s32[]{:S(2)}) async-start(), calls=%async_computation.15 | async-start | bytes 5242880 | tf_op jit(solution)/shard_map/all_gather | solution.py:418
  162.8 127.6 %all-to-all-start = ((bf16[8,192,256]{2,1,0:T(8,128)(2,1)}), bf16[8,192,256]{2,1,0:T(8,128)(2,1)S(1)}, u32[]{:S(2)}, u32[]{:S(2)}) async-start(bf16[8,192,256]{2,1,0:T(8,128)(2,1)} %bitcast.67), calls=%async_computation | async-start | bytes 1572864 | tf_op jit(solution)/shard_map/all_to_all | solution.py:441
  166.5 217.2 %all-gather.25.cloned.1.call-start = ((), (), s32[]{:S(2)}) async-start(), calls=%async_computation.17 | async-start | bytes 5242880 | tf_op jit(solution)/shard_map/all_gather | solution.py:420
  167.2 566.4 %reduce-scatter.15.cloned.1.call-start = ((), (), s32[]{:S(2)}) async-start(), calls=%async_computation.21 | async-start | bytes 9437184 | tf_op jit(solution)/shard_map/reduce_scatter | solution.py:476
  568.7 289.8 %reduce-scatter.9.cloned.1.call-start = ((), (), s32[]{:S(2)}) async-start(), calls=%async_computation.18 | async-start | bytes 1310720 | tf_op jit(solution)/shard_map/reduce_scatter | solution.py:496
  640.4 219.9 %reduce-scatter.11.cloned.1.call-start = ((), (), s32[]{:S(2)}) async-start(), calls=%async_computation.19 | async-start | bytes 1310720 | tf_op jit(solution)/shard_map/reduce_scatter | solution.py:499
  646.3 215.8 %reduce-scatter.13.cloned.1.call-start = ((), (), s32[]{:S(2)}) async-start(), calls=%async_computation.20 | async-start | bytes 1310720 | tf_op jit(solution)/shard_map/reduce_scatter | solution.py:502
  652.3 212.3 %reduce-scatter.23.cloned.1.call-start = ((), (), s32[]{:S(2)}) async-start(), calls=%async_computation.25 | async-start | bytes 5242880 | tf_op jit(solution)/shard_map/reduce_scatter | solution.py:512
  663.6 248.0 %reduce-scatter.21.cloned.1.call-start = ((), (), s32[]{:S(2)}) async-start(), calls=%async_computation.24 | async-start | bytes 5242880 | tf_op jit(solution)/shard_map/reduce_scatter | solution.py:509
  674.9 283.5 %reduce-scatter.19.cloned.1.call-start = ((), (), s32[]{:S(2)}) async-start(), calls=%async_computation.23 | async-start | bytes 5242880 | tf_op jit(solution)/shard_map/reduce_scatter | solution.py:506
  686.4 299.5 %reduce-scatter.17.cloned.1.call-start = ((), (), s32[]{:S(2)}) async-start(), calls=%async_computation.22 | async-start | bytes 1310720 | tf_op jit(solution)/shard_map/reduce_scatter | solution.py:505
  694.0 39.7 %copy-start.14 = (bf16[2048,256]{1,0:T(8,128)(2,1)S(1)}, bf16[2048,256]{1,0:T(8,128)(2,1)}, u32[]{:S(2)}) copy-start(bf16[2048,256]{1,0:T(8,128)(2,1)} %all-gather.15.cloned.1.call-done) | copy-start | bytes 3145732
  694.0 39.7 %copy-start.17 = (bf16[1536,256]{1,0:T(8,128)(2,1)S(1)}, bf16[1536,256]{1,0:T(8,128)(2,1)}, u32[]{:S(2)}) copy-start(bf16[1536,256]{1,0:T(8,128)(2,1)} %get-tuple-element.16) | copy-start | bytes 2359300
  745.8 66.6 %copy-start.19 = (f32[4,1,512]{2,1,0:T(1,128)S(1)}, f32[4,1,512]{2,1,0:T(1,128)}, u32[]{:S(2)}) copy-start(f32[4,1,512]{2,1,0:T(1,128)} %copy-done.18) | copy-start | bytes 24580
  745.8 66.6 %copy-start.21 = (f32[192]{0:T(256)S(1)}, f32[192]{0:T(256)}, u32[]{:S(2)}) copy-start(f32[192]{0:T(256)} %copy-done.20) | copy-start | bytes 2308
  812.5 43.3 %copy-start = (f32[192,2048]{1,0:T(8,128)S(1)}, f32[192,2048]{1,0:T(8,128)}, u32[]{:S(2)}) copy-start(f32[192,2048]{1,0:T(8,128)} %shard_map.246) | copy-start | bytes 4718596
  (21 other events, 135.4 us)
Sparse Core Ops, SparseCore 0:
  9.6 19.4 all-gather.16
  30.6 16.7 all-gather.10
  48.9 16.7 all-gather.12
  67.1 16.7 all-gather.14
  85.8 175.9 all-gather.18
  263.1 38.0 all-gather.22
  302.8 34.4 all-gather.20
  338.9 34.4 all-gather.24
  568.8 164.7 reduce-scatter.14
  736.8 23.8 reduce-scatter.8
  763.8 24.9 reduce-scatter.10
  791.8 24.8 reduce-scatter.12
  819.3 45.1 reduce-scatter.22
  867.1 44.4 reduce-scatter.20
  913.9 44.4 reduce-scatter.18
  961.0 24.8 reduce-scatter.16

commit v2 on v1

v2 whole, which is shorter than its diff:
```python
import functools
import math

import jax
import jax.numpy as jnp
import numpy as np
from jax import lax
from jax.experimental import pallas as pl
from jax.experimental.pallas import tpu as pltpu
from jax.sharding import PartitionSpec as P

HD = 128
WINDOW = 2048
EPSILON = 1e-05
NEGATIVE = -1e30
LINE = 4
CORES = 2
PARTS = 2
MESH = pl.DeviceIdType.MESH
VMEM_LIMIT = 60 * 1024 * 1024

ANY = pl.BlockSpec(memory_space=pl.ANY)
VMEM = pl.BlockSpec(memory_space=pltpu.VMEM)
SMEM = pl.BlockSpec(memory_space=pltpu.SMEM)
low = jnp.bfloat16
full = jnp.float32


def shape_of(shape, dtype):
    return jax.ShapeDtypeStruct(shape, dtype)


def span(start, size):
    if isinstance(start, int):
        return pl.ds(start, size)
    return pl.ds(pl.multiple_of(start, size), size)


def dot(left, right, left_dim=1, right_dim=0):
    return lax.dot_general(
        left, right, (((left_dim,), (right_dim,)), ((), ())), preferred_element_type=jnp.float32
    )


def greet(targets):
    barrier = pltpu.get_barrier_semaphore()
    for target in targets:
        pl.semaphore_signal(barrier, inc=1, device_id=target, device_id_type=MESH)
    pl.semaphore_wait(barrier, len(targets))


def send_to(target, source, place, send, recv):
    return pltpu.make_async_remote_copy(
        src_ref=source, dst_ref=place, send_sem=send, recv_sem=recv, device_id=target, device_id_type=MESH
    )


def weave(tasks, events):
    done = 0
    for number, task in enumerate(tasks):
        task()
        upto = (number + 1) * len(events) // len(tasks)
        for event in events[done:upto]:
            event()
        done = upto


def ring_index(place, count):
    columns = count // LINE
    column = place // LINE
    level = place % LINE
    odd = column % 2
    return (level + odd * (LINE - 1 - 2 * level)) * columns + column


def ring_place(index, count):
    columns = count // LINE
    level = index // columns
    column = index % columns
    odd = column % 2
    return column * LINE + level + odd * (LINE - 1 - 2 * level)


class Ring:
    def __init__(self, count):
        self.count = count
        self.half = count // 2
        self.index = lax.axis_index("seq")
        self.place = ring_place(self.index, count)
        self.next = ({"seq": self.shifted(1)}, {"seq": self.shifted(-1)})

    def shifted(self, offset):
        return ring_index((self.place + offset + self.count) % self.count, self.count)


def ring_semaphores(count):
    return [pltpu.SemaphoreType.DMA((2, count // 2, PARTS))] * 2


class RingGather:
    def __init__(self, ring, source, place, send, recv):
        self.ring, self.source, self.place = ring, source, place
        self.send, self.recv = send, recv

    def pieces(self, way, step):
        if step < self.ring.half - 1:
            return range(PARTS)
        return range(PARTS // 2) if way == 0 else range(PARTS // 2, PARTS)

    def copy(self, way, step, part):
        place = self.place(self.ring.shifted(step if way else -step), part)
        return send_to(
            self.ring.next[way],
            self.source(part) if step == 0 else place,
            place,
            self.send.at[way, step, part],
            self.recv.at[way, step, part],
        )

    def start(self):
        for part in range(PARTS):
            for way in range(2):
                if part in self.pieces(way, 0):
                    self.copy(way, 0, part).start()

    def advance(self, step):
        for part in range(PARTS):
            for way in range(2):
                if part in self.pieces(way, step - 1):
                    self.copy(way, step - 1, part).wait_recv()
                if step < self.ring.half and part in self.pieces(way, step):
                    self.copy(way, step, part).start()

    def finish(self):
        for step in range(self.ring.half):
            for way in range(2):
                for part in self.pieces(way, step):
                    self.copy(way, step, part).wait_send()

    def steps(self):
        return [functools.partial(self.advance, step) for step in range(1, self.ring.half + 1)]


class RingReduce:
    def __init__(self, ring, mine, slots, terms, send, recv, load):
        self.ring, self.mine, self.slots, self.terms = ring, mine, slots, terms
        self.send, self.recv, self.load = send, recv, load
        self.size = slots.shape[2] // PARTS

    @staticmethod
    def scratch(count, rows, width):
        return [
            pltpu.VMEM((2, count // 2, rows, width), low),
            pltpu.VMEM((2, 2, rows, width), low),
            *ring_semaphores(count),
            pltpu.SemaphoreType.DMA((2, 2, PARTS)),
        ]

    def pieces(self, way, step):
        if step > 0:
            return range(PARTS)
        return range(PARTS // 2) if way == 0 else range(PARTS // 2, PARTS)

    def summed(self, way, step):
        return self.pieces(way, 0) if step == 1 else range(PARTS)

    def target(self, way, step):
        left = self.ring.half - step
        return self.ring.shifted(-left if way else left)

    def slot(self, way, step, part):
        return self.slots.at[way, step, pl.ds(part * self.size, self.size)]

    def term(self, way, step, part):
        return self.terms.at[step % 2, way, pl.ds(part * self.size, self.size)]

    def fetch(self, way, step, part):
        return pltpu.make_async_copy(
            self.mine(self.target(way, step), part), self.term(way, step, part), self.load.at[step % 2, way, part]
        )

    def fetch_all(self, step):
        for part in range(PARTS):
            for way in range(2 if step < self.ring.half else 1):
                if part in self.summed(way, step):
                    self.fetch(way, step, part).start()

    def copy(self, way, step, part):
        alone = step == 0 or part not in self.summed(way, step)
        source = self.mine(self.target(way, step), part) if alone else self.slot(way, step - 1, part)
        return send_to(
            self.ring.next[way],
            source,
            self.slot(way, step, part),
            self.send.at[way, step, part],
            self.recv.at[way, step, part],
        )

    def start(self):
        for way in range(2):
            for part in self.pieces(way, 0):
                self.copy(way, 0, part).start()
        self.fetch_all(1)

    def advance(self, step):
        self.fetch_all(step + 1)
        order = [(way, part) for part in range(PARTS) for way in range(2)]
        for way, part in order:
            if part not in self.summed(way, step):
                self.copy(way, step, part).start()
        for way, part in order:
            if part in self.summed(way, step):
                self.fetch(way, step, part).wait()
                self.copy(way, step - 1, part).wait_recv()
                slot = self.slot(way, step - 1, part)
                total = slot[...].astype(full) + self.term(way, step, part)[...].astype(full)
                slot[...] = total.astype(slot.dtype)
                self.copy(way, step, part).start()

    def steps(self):
        return [functools.partial(self.advance, step) for step in range(1, self.ring.half)]

    def total(self, part):
        last = self.ring.half - 1
        self.fetch(0, last + 1, part).wait()
        for way in range(2):
            self.copy(way, last, part).wait_recv()
        return (
            self.term(0, last + 1, part)[...].astype(full)
            + self.slot(0, last, part)[...].astype(full)
            + self.slot(1, last, part)[...].astype(full)
        )

    def finish(self):
        for step in range(self.ring.half):
            for way in range(2):
                for part in self.pieces(way, step):
                    self.copy(way, step, part).wait_send()


def row_piece(ref, rows):
    size = rows // PARTS
    return lambda index, part: ref.at[span(index * rows + part * size, size)]


class Shards:
    def __init__(self, count):
        self.count = count
        self.chips = count // CORES
        self.index = lax.axis_index("dp")
        self.chip = self.index // CORES
        self.core = self.index % CORES
        self.sibling = {"dp": self.chip * CORES + 1 - self.core}

    def chip_at(self, offset):
        return (self.chip + offset) % self.chips

    def device(self, chip, core):
        return chip * CORES + core

    def others(self):
        return [{"dp": (self.index + offset) % self.count} for offset in range(1, self.count)]

    def greeted(self):
        return [self.sibling] + [
            {"dp": self.device(self.chip_at(offset), self.core)} for offset in range(1, self.chips)
        ]


class ShardGather:
    def __init__(self, shards, own, whole, send, recv, local):
        self.shards, self.own, self.whole = shards, own, whole
        self.send, self.recv, self.local = send, recv, local
        self.rows = own.shape[0]
        self.size = self.rows // PARTS

    @staticmethod
    def semaphores(count):
        shape = (2, count // CORES, PARTS)
        return [pltpu.SemaphoreType.DMA(shape), pltpu.SemaphoreType.DMA(shape), pltpu.SemaphoreType.DMA]

    def source(self, part):
        return self.own.at[pl.ds(part * self.size, self.size)]

    def place(self, shard, part):
        return self.whole.at[span(shard * self.rows + part * self.size, self.size)]

    def across(self, offset, part):
        shards = self.shards
        target = {"dp": shards.device(shards.chip_at(offset), shards.core)}
        return send_to(
            target,
            self.source(part),
            self.place(shards.index, part),
            self.send.at[0, offset, part],
            self.recv.at[0, offset, part],
        )

    def beside(self, offset, part):
        shards = self.shards
        place = self.place(shards.device(shards.chip_at(shards.chips - offset), shards.core), part)
        return send_to(
            shards.sibling,
            place if offset else self.source(part),
            place,
            self.send.at[1, offset, part],
            self.recv.at[1, offset, part],
        )

    def keep(self):
        return pltpu.make_async_copy(
            self.own, self.whole.at[span(self.shards.index * self.rows, self.rows)], self.local
        )

    def start(self):
        for part in range(PARTS):
            for offset in range(1, self.shards.chips):
                self.across(offset, part).start()
            self.beside(0, part).start()
        self.keep().start()

    def pass_on(self):
        for part in range(PARTS):
            for offset in range(1, self.shards.chips):
                self.across(offset, part).wait_recv()
                self.beside(offset, part).start()

    def finish(self):
        for part in range(PARTS):
            for offset in range(self.shards.chips):
                self.beside(offset, part).wait_recv()
                self.beside(offset, part).wait_send()
                if offset:
                    self.across(offset, part).wait_send()
        self.keep().wait()


class ShardReduce:
    def __init__(self, shards, whole, own, beside_slots, across_slots, loads, beside_sems, across_sems):
        self.shards, self.whole = shards, whole
        self.own, self.beside_slots, self.across_slots = own, beside_slots, across_slots
        self.loads, self.beside_sems, self.across_sems = loads, beside_sems, across_sems
        self.rows = own.shape[1]
        self.offsets = [*range(1, shards.chips), 0]

    @staticmethod
    def scratch(count, rows, width):
        chips = count // CORES
        return [
            pltpu.VMEM((chips, rows, width), low),
            pltpu.VMEM((chips, rows, width), low),
            pltpu.VMEM((chips - 1, rows, width), low),
            pltpu.SemaphoreType.DMA((chips,)),
            pltpu.SemaphoreType.DMA((2, chips)),
            pltpu.SemaphoreType.DMA((2, chips)),
        ]

    def block(self, offset, core):
        shard = self.shards.device(self.shards.chip_at(offset), core)
        return self.whole.at[span(shard * self.rows, self.rows)]

    def beside(self, offset):
        return send_to(
            self.shards.sibling,
            self.block(offset, 1 - self.shards.core),
            self.beside_slots.at[offset],
            self.beside_sems.at[0, offset],
            self.beside_sems.at[1, offset],
        )

    def load(self, offset):
        return pltpu.make_async_copy(
            self.block(offset, self.shards.core), self.own.at[offset], self.loads.at[offset]
        )

    def across(self, offset):
        return send_to(
            {"dp": self.shards.device(self.shards.chip_at(offset), self.shards.core)},
            self.beside_slots.at[offset],
            self.across_slots.at[offset - 1],
            self.across_sems.at[0, offset],
            self.across_sems.at[1, offset],
        )

    def start(self):
        for offset in self.offsets:
            self.beside(offset).start()
            self.load(offset).start()

    def spread(self):
        for offset in self.offsets:
            self.beside(offset).wait_recv()
            self.load(offset).wait()
            total = self.beside_slots[offset].astype(full) + self.own[offset].astype(full)
            self.beside_slots[offset] = total.astype(low)
            if offset:
                self.across(offset).start()

    def total(self):
        total = self.beside_slots[0].astype(full)
        for offset in range(1, self.shards.chips):
            self.across(offset).wait_recv()
            total += self.across_slots[offset - 1].astype(full)
        return total

    def finish(self):
        for offset in self.offsets:
            self.beside(offset).wait_send()
            if offset:
                self.across(offset).wait_send()


def grouped(refs, size):
    return [refs[number : number + size] for number in range(0, len(refs), size)]


def norm_gather_kernel(count, shard_count, weights, *refs):
    tokens, gains, *shard_refs = refs[: 2 + weights]
    all_rows, gain_rows, *whole_refs = refs[2 + weights : 4 + 2 * weights]
    own, all_gains, send, recv, local, ring_send, ring_recv, *shard_sems = refs[4 + 2 * weights :]
    ring, shards = Ring(count), Shards(shard_count)
    greet([*ring.next, *shards.others()])
    copies = [
        send_to(target, gains, all_gains.at[shards.index], send.at[offset], recv.at[offset])
        for offset, target in enumerate(shards.others())
    ]
    for copy in copies:
        copy.start()
    gathers = [
        ShardGather(shards, shard, whole, *sems)
        for shard, whole, sems in zip(shard_refs, whole_refs, grouped(shard_sems, 3))
    ]
    early, late = gathers[:-1], gathers[-1]
    for gather in early:
        gather.start()
    all_gains[shards.index] = gains[...]
    rows = tokens[...].astype(full)
    factor = lax.rsqrt(jnp.mean(rows * rows, axis=-1, keepdims=True) + EPSILON)
    rows = rows * factor
    for copy in copies:
        copy.wait_recv()
    width = gains.shape[1]
    for shard in range(shard_count):
        gain_rows[:, shard * width : (shard + 1) * width] = all_gains[shard, :8, :].astype(full)
    own[...] = (rows * gain_rows[0:1, :]).astype(low)
    place = row_piece(all_rows, own.shape[0])
    size = own.shape[0] // PARTS
    gather = RingGather(ring, lambda part: own.at[pl.ds(part * size, size)], place, ring_send, ring_recv)
    gather.start()
    kept = pltpu.make_async_copy(own, all_rows.at[span(ring.index * own.shape[0], own.shape[0])], local)
    kept.start()
    for number, step in enumerate(gather.steps()):
        step()
        if number == 0:
            late.start()
        elif number == 1:
            for other in early[:-1]:
                other.pass_on()
        elif number == 2:
            early[-1].pass_on()
    late.pass_on()
    gather.finish()
    for other in gathers:
        other.finish()
    kept.wait()
    for copy in copies:
        copy.wait_send()


def norm_gather(tokens, gains, weights, collective_id):
    count, shard_count = lax.axis_size("seq"), lax.axis_size("dp")
    rows, width = tokens.shape
    return pl.pallas_call(
        functools.partial(norm_gather_kernel, count, shard_count, len(weights)),
        out_shape=[
            shape_of((count * rows, width), low),
            shape_of((8, width), full),
            *[shape_of((shard_count * weight.shape[0], weight.shape[1]), low) for weight in weights],
        ],
        in_specs=[VMEM, VMEM] + [ANY] * len(weights),
        out_specs=[ANY, VMEM] + [ANY] * len(weights),
        scratch_shapes=[
            pltpu.VMEM((rows, width), low),
            pltpu.VMEM((shard_count, *gains.shape), low),
            pltpu.SemaphoreType.DMA((shard_count - 1,)),
            pltpu.SemaphoreType.DMA((shard_count - 1,)),
            pltpu.SemaphoreType.DMA,
            *ring_semaphores(count),
            *ShardGather.semaphores(shard_count) * len(weights),
        ],
        compiler_params=pltpu.CompilerParams(
            collective_id=collective_id, has_side_effects=True, vmem_limit_bytes=VMEM_LIMIT
        ),
        cost_estimate=pl.CostEstimate(flops=0, bytes_accessed=200_000_000, transcendentals=0),
    )(tokens, gains, *weights)


def rope_tables(seq_len):
    half_dim = HD // 2
    steps = np.arange(half_dim, dtype=np.float32) * np.float32(2.0 / HD)
    frequency = np.exp(np.float32(-math.log(10000.0)) * steps)
    angles = np.arange(seq_len, dtype=np.float32)[:, None] * frequency[None, :]
    cos, sin = np.cos(angles), np.sin(angles)
    return (
        np.concatenate([cos, cos], axis=1).astype(np.float32),
        np.concatenate([-sin, sin], axis=1).astype(np.float32),
    )


def turned(values, cos, sin):
    return values * cos + pltpu.roll(values, HD // 2, 1) * sin


def turned_back(values, cos, sin):
    return values * cos - pltpu.roll(values, HD // 2, 1) * sin


def softmax_block(queries, keys, start, length):
    rows, count = queries.shape[0], keys.shape[0]
    scores = dot(queries, keys, 1, 1) * (1.0 / math.sqrt(HD))
    query_pos = start + lax.broadcasted_iota(jnp.int32, (rows, count), 0)
    key_pos = lax.broadcasted_iota(jnp.int32, (rows, count), 1)
    allowed = (key_pos <= query_pos) & (key_pos < length)
    if start + rows > WINDOW:
        allowed = allowed & (query_pos - key_pos < WINDOW)
    scores = jnp.where(allowed, scores, NEGATIVE)
    exponent = jnp.exp(scores - jnp.max(scores, axis=-1, keepdims=True))
    return exponent * (1.0 / jnp.sum(exponent, axis=-1, keepdims=True))


BLOCK = 256


def attend_kernel(
    count,
    shard_count,
    length,
    rows_in,
    query_w,
    key_w,
    value_w,
    cos_in,
    sin_in,
    grad_own,
    out_own,
    down_own,
    queries,
    keys,
    values,
    attended,
    grad_rows,
    down_all,
    out_all,
    out_mine,
    rows,
    weights,
    cos,
    sin,
    loads,
    local,
    grad_send,
    grad_recv,
    out_send,
    out_recv,
    *shard_sems,
):
    ring, shards = Ring(count), Shards(shard_count)
    seq_len, width = queries.shape
    own_rows = grad_own.shape[0]
    out_rows, out_width = out_own.shape
    blocks = seq_len // BLOCK
    weight_loads = [
        pltpu.make_async_copy(source, weights.at[number], loads.at[blocks + number])
        for number, source in enumerate((query_w, key_w, value_w))
    ]
    table_loads = [
        pltpu.make_async_copy(cos_in, cos, loads.at[blocks + 3]),
        pltpu.make_async_copy(sin_in, sin, loads.at[blocks + 4]),
    ]
    row_loads = [
        pltpu.make_async_copy(rows_in.at[pl.ds(n * BLOCK, BLOCK)], rows.at[pl.ds(n * BLOCK, BLOCK)], loads.at[n])
        for n in range(blocks)
    ]
    for load in (*weight_loads, row_loads[0], *table_loads, *row_loads[1:]):
        load.start()
    greet([*ring.next, *shards.greeted()])

    out_size, grad_size = out_rows // PARTS, own_rows // PARTS
    out_gather = RingGather(
        ring,
        lambda part: out_own.at[pl.ds(part * out_size, out_size)],
        lambda index, part: out_mine.at[pl.ds(part * out_size, out_size), span(index * out_width, out_width)],
        out_send,
        out_recv,
    )
    grad_gather = RingGather(
        ring,
        lambda part: grad_own.at[pl.ds(part * grad_size, grad_size)],
        row_piece(grad_rows, own_rows),
        grad_send,
        grad_recv,
    )
    out_gather.start()
    grad_gather.start()
    kept = [
        pltpu.make_async_copy(
            out_own, out_mine.at[:, span(ring.index * out_width, out_width)], local.at[0]
        ),
        pltpu.make_async_copy(grad_own, grad_rows.at[span(ring.index * own_rows, own_rows)], local.at[1]),
    ]
    for copy in kept:
        copy.start()
    down_sems, out_sems = grouped(shard_sems, 3)
    down_gather = ShardGather(shards, down_own, down_all, *down_sems)
    shard_gather = ShardGather(shards, out_mine, out_all, *out_sems)
    down_gather.start()

    def spread_out():
        kept[0].wait()
        out_gather.finish()
        shard_gather.start()

    grad_steps = grad_gather.steps()
    events = [*out_gather.steps(), spread_out, *grad_steps[:2], down_gather.pass_on, *grad_steps[2:-1]]
    events += [shard_gather.pass_on, grad_steps[-1]]

    def project(n):
        if n == 0:
            for load in (*weight_loads, *table_loads):
                load.wait()
        row_loads[n].wait()
        here = pl.ds(n * BLOCK, BLOCK)
        block = rows[here, :]
        for number, place in enumerate((queries, keys, values)):
            linear = dot(block, weights[number])
            for head in range(width // HD):
                lanes = slice(head * HD, (head + 1) * HD)
                one = linear[:, lanes]
                if number < 2:
                    one = turned(one, cos[here, :], sin[here, :])
                place[here, lanes] = one.astype(low)

    limit = length[0]

    def attend(head, n):
        lanes = slice(head * HD, (head + 1) * HD)
        here, upto = pl.ds(n * BLOCK, BLOCK), pl.ds(0, (n + 1) * BLOCK)
        probs = softmax_block(queries[here, lanes], keys[upto, lanes], n * BLOCK, limit)
        attended[here, lanes] = dot(probs.astype(low), values[upto, lanes]).astype(low)

    tasks = [functools.partial(project, n) for n in range(blocks)]
    tasks += [functools.partial(attend, head, n) for head in range(width // HD) for n in range(blocks)]
    weave(tasks, events)
    grad_gather.finish()
    down_gather.finish()
    shard_gather.finish()
    kept[1].wait()


def attend(length, rows, query_w, key_w, value_w, tables, grad_own, out_own, down_own, collective_id):
    count, shard_count = lax.axis_size("seq"), lax.axis_size("dp")
    seq_len, model = rows.shape
    heads = shape_of((seq_len, query_w.shape[1]), low)
    out_rows = out_own.shape[0]
    return pl.pallas_call(
        functools.partial(attend_kernel, count, shard_count),
        out_shape=[heads] * 4
        + [
            shape_of(rows.shape, low),
            shape_of((model, down_own.shape[1]), low),
            shape_of((model, model), low),
        ],
        in_specs=[SMEM] + [ANY] * 9,
        out_specs=[VMEM] * 4 + [ANY] * 3,
        scratch_shapes=[
            pltpu.VMEM((out_rows, model), low),
            pltpu.VMEM(rows.shape, low),
            pltpu.VMEM((3, *query_w.shape), low),
            pltpu.VMEM((seq_len, HD), full),
            pltpu.VMEM((seq_len, HD), full),
            pltpu.SemaphoreType.DMA((seq_len // BLOCK + 5,)),
            pltpu.SemaphoreType.DMA((2,)),
            *ring_semaphores(count),
            *ring_semaphores(count),
            *ShardGather.semaphores(shard_count) * 2,
        ],
        compiler_params=pltpu.CompilerParams(
            collective_id=collective_id, has_side_effects=True, vmem_limit_bytes=VMEM_LIMIT
        ),
        cost_estimate=pl.CostEstimate(flops=0, bytes_accessed=250_000_000, transcendentals=0),
    )(length, rows, query_w, key_w, value_w, *tables, grad_own, out_own, down_own)


TILE = 256


def ffn_kernel(
    count,
    attended,
    out_in,
    tokens,
    gain_rows,
    gate_in,
    up_in,
    down_in,
    grad_rows,
    attended_own,
    resid,
    normed_rows,
    act_out,
    grad_gate_out,
    grad_up_out,
    partial,
    out_w,
    gate_w,
    up_w,
    down_w,
    own,
    normed,
    grads,
    hidden,
    back,
    loads,
    row_loads,
    stores,
    swap_send,
    swap_recv,
    ring_send,
    ring_recv,
    local,
):
    ring = Ring(count)
    size, model = tokens.shape
    heads = attended.shape[1]
    units = gate_w.shape[1]
    weight_loads = [
        pltpu.make_async_copy(source, place, loads.at[number])
        for number, (source, place) in enumerate(
            ((out_in, out_w), (gate_in, gate_w), (up_in, up_w), (down_in, down_w))
        )
    ]
    others = [{"seq": (ring.index + offset) % count} for offset in range(1, count)]
    weight_loads[0].start()
    greet(others)
    place = attended_own.at[:, span(ring.index * heads, heads)]
    swaps = [
        send_to(
            other, attended.at[span(other["seq"] * size, size)], place, swap_send.at[number], swap_recv.at[number]
        )
        for number, other in enumerate(others)
    ]
    for swap in swaps:
        swap.start()
    kept = pltpu.make_async_copy(attended.at[span(ring.index * size, size)], place, local.at[0])
    kept.start()
    for load in weight_loads[1:]:
        load.start()
    weight_loads[0].wait()
    kept.wait()
    for swap in swaps:
        swap.wait_recv()

    def project(tile, carry):
        lanes = span(tile * TILE, TILE)
        resid[:, lanes] = tokens[:, lanes].astype(full) + dot(attended_own[...], out_w[lanes, :], 1, 1)
        return carry

    lax.fori_loop(0, model // TILE, project, 0)
    rows = resid[...]
    factor = lax.rsqrt(jnp.mean(rows * rows, axis=-1, keepdims=True) + EPSILON)
    own[...] = (rows * factor * gain_rows[1:2, :]).astype(low)
    piece = size // PARTS
    gather = RingGather(
        ring, lambda part: own.at[pl.ds(part * piece, piece)], row_piece(normed_rows, size), ring_send, ring_recv
    )
    gather.start()
    kept = pltpu.make_async_copy(own, normed_rows.at[span(ring.index * size, size)], local.at[1])
    kept.start()

    def owners(step):
        if step in (0, ring.half):
            return [ring.shifted(step)]
        return [ring.shifted(-step), ring.shifted(step)]

    def grad_loads(step):
        return [
            pltpu.make_async_copy(
                grad_rows.at[span(owner * size, size)],
                grads.at[step % 2, pl.ds(side * size, size)],
                row_loads.at[step % 2, side],
            )
            for side, owner in enumerate(owners(step))
        ]

    def normed_loads(step):
        return [
            pltpu.make_async_copy(
                own if step == 0 else normed_rows.at[span(owner * size, size)],
                normed.at[pl.ds(side * size, size)],
                row_loads.at[2, side],
            )
            for side, owner in enumerate(owners(step))
        ]

    def result_stores(step):
        results = []
        for side, owner in enumerate(owners(step)):
            here, there = pl.ds(side * size, size), span(owner * size, size)
            for number, place in enumerate((act_out, grad_gate_out, grad_up_out)):
                results.append(
                    pltpu.make_async_copy(hidden.at[number, here], place.at[there], stores.at[side, number])
                )
            results.append(pltpu.make_async_copy(back.at[here], partial.at[there], stores.at[side, 3]))
        return results

    def block(step):
        for load in normed_loads(step):
            load.start()
        if step < ring.half:
            for load in grad_loads(step + 1):
                load.start()
        if step > 0:
            for store in result_stores(step - 1):
                store.wait()
        if step == 0:
            for load in weight_loads[1:]:
                load.wait()
        for load in (*normed_loads(step), *grad_loads(step)):
            load.wait()
        rows = pl.ds(0, size * len(owners(step)))
        slot = step % 2

        def forward(tile, carry):
            lanes = span(tile * TILE, TILE)
            gate = dot(normed[rows, :], gate_w[:, lanes])
            up = dot(normed[rows, :], up_w[:, lanes])
            grad_act = dot(grads[slot, rows, :], down_w[:, lanes])
            sigmoid = 1.0 / (1.0 + jnp.exp(-gate))
            silu = gate * sigmoid
            hidden[0, rows, lanes] = (silu * up).astype(low)
            hidden[1, rows, lanes] = (grad_act * up * sigmoid * (1.0 + gate * (1.0 - sigmoid))).astype(low)
            hidden[2, rows, lanes] = (grad_act * silu).astype(low)
            return carry

        lax.fori_loop(0, units // TILE, forward, 0)

        def backward(tile, carry):
            lanes = span(tile * TILE, TILE)
            total = dot(hidden[1, rows, :], gate_w[lanes, :], 1, 1) + dot(hidden[2, rows, :], up_w[lanes, :], 1, 1)
            back[rows, lanes] = total.astype(low)
            return carry

        lax.fori_loop(0, model // TILE, backward, 0)
        for store in result_stores(step):
            store.start()

    for load in grad_loads(0):
        load.start()
    block(0)
    for step in range(1, ring.half + 1):
        gather.advance(step)
        block(step)
    for store in result_stores(ring.half):
        store.wait()
    gather.finish()
    kept.wait()
    for swap in swaps:
        swap.wait_send()


def ffn(attended, out_w, tokens, gain_rows, gate_w, up_w, down_w, grad_rows, collective_id):
    count = lax.axis_size("seq")
    size, model = tokens.shape
    seq_len, units = grad_rows.shape[0], gate_w.shape[1]
    hidden = shape_of((seq_len, units), low)
    return pl.pallas_call(
        functools.partial(ffn_kernel, count),
        out_shape=[
            shape_of((size, model), low),
            shape_of((size, model), full),
            shape_of((seq_len, model), low),
            hidden,
            hidden,
            hidden,
            shape_of((seq_len, model), low),
        ],
        in_specs=[ANY, ANY, VMEM, VMEM, ANY, ANY, ANY, ANY],
        out_specs=[VMEM, VMEM, ANY, ANY, ANY, ANY, ANY],
        scratch_shapes=[
            pltpu.VMEM(out_w.shape, low),
            pltpu.VMEM(gate_w.shape, low),
            pltpu.VMEM(up_w.shape, low),
            pltpu.VMEM(down_w.shape, low),
            pltpu.VMEM((size, model), low),
            pltpu.VMEM((2 * size, model), low),
            pltpu.VMEM((2, 2 * size, model), low),
            pltpu.VMEM((3, 2 * size, units), low),
            pltpu.VMEM((2 * size, model), low),
            pltpu.SemaphoreType.DMA((4,)),
            pltpu.SemaphoreType.DMA((3, 2)),
            pltpu.SemaphoreType.DMA((2, 4)),
            pltpu.SemaphoreType.DMA((count - 1,)),
            pltpu.SemaphoreType.DMA((count - 1,)),
            *ring_semaphores(count),
            pltpu.SemaphoreType.DMA((2,)),
        ],
        compiler_params=pltpu.CompilerParams(
            collective_id=collective_id, has_side_effects=True, vmem_limit_bytes=VMEM_LIMIT
        ),
        cost_estimate=pl.CostEstimate(flops=0, bytes_accessed=300_000_000, transcendentals=0),
    )(attended, out_w, tokens, gain_rows, gate_w, up_w, down_w, grad_rows)


def ffn_back_kernel(
    count,
    partial,
    normed_rows,
    grad_rows,
    act_in,
    grad_gate_in,
    grad_up_in,
    down_in,
    out_in,
    resid,
    grad_own,
    gain_rows,
    grad_gate_w,
    grad_up_w,
    grad_down_w,
    branch,
    grad_resid,
    grad_attn,
    gain_sum,
    grad_heads,
    hidden,
    down_w,
    out_w,
    tiles,
    staged,
    branch_tile,
    attended,
    loads,
    tile_loads,
    stores,
    swap_send,
    swap_recv,
    local,
    slots,
    terms,
    ring_send,
    ring_recv,
    term_loads,
):
    ring = Ring(count)
    size, model = resid.shape
    heads = grad_heads.shape[1]
    others = [{"seq": (ring.index + offset) % count} for offset in range(1, count)]
    inputs = [
        pltpu.make_async_copy(source, place, loads.at[number])
        for number, (source, place) in enumerate(
            (
                (grad_gate_in, hidden.at[1]),
                (grad_up_in, hidden.at[2]),
                (act_in, hidden.at[0]),
                (down_in, down_w),
                (out_in, out_w),
            )
        )
    ]
    greet(others)
    reduce = RingReduce(ring, row_piece(partial, size), slots, terms, ring_send, ring_recv, term_loads)
    reduce.start()

    def fetch(tile):
        lanes = span(tile * TILE, TILE)
        return [
            pltpu.make_async_copy(source.at[:, lanes], tiles.at[tile % 2, number], tile_loads.at[tile % 2, number])
            for number, source in enumerate((normed_rows, grad_rows))
        ]

    def store(tile):
        lanes, slot = span(tile * TILE, TILE), tile % 2
        copies = [
            pltpu.make_async_copy(staged.at[slot, number], place.at[lanes], stores.at[slot, number])
            for number, place in enumerate((grad_gate_w, grad_up_w, grad_down_w))
        ]
        copies.append(pltpu.make_async_copy(branch_tile.at[slot], branch.at[:, lanes], stores.at[slot, 3]))
        return copies

    count_tiles = model // TILE
    for copy in (inputs[0], *fetch(0), *inputs[1:]):
        copy.start()

    def weights(tile):
        slot = tile % 2
        if tile == 0:
            for copy in inputs[:4]:
                copy.wait()
        if tile + 1 < count_tiles:
            for copy in fetch(tile + 1):
                copy.start()
        if tile >= 2:
            for copy in store(tile - 2):
                copy.wait()
        for copy in fetch(tile):
            copy.wait()
        staged[slot, 0] = dot(tiles[slot, 0], hidden[1], 0, 0).astype(low)
        staged[slot, 1] = dot(tiles[slot, 0], hidden[2], 0, 0).astype(low)
        staged[slot, 2] = dot(tiles[slot, 1], hidden[0], 0, 0).astype(low)
        branch_tile[slot] = dot(hidden[0], down_w[pl.ds(tile * TILE, TILE), :], 1, 1).astype(low)
        for copy in store(tile):
            copy.start()

    tasks = [functools.partial(weights, tile) for tile in range(count_tiles)]
    weave(tasks, [*reduce.steps(), lambda: None])
    inputs[4].wait()
    gain_total = jnp.zeros((1, model), full)
    for part in range(PARTS):
        here = pl.ds(part * reduce.size, reduce.size)
        grad_normed, rows = reduce.total(part), resid[here, :]
        factor = lax.rsqrt(jnp.mean(rows * rows, axis=-1, keepdims=True) + EPSILON)
        weighted = grad_normed * gain_rows[1:2, :]
        inner = jnp.mean(weighted * rows, axis=-1, keepdims=True)
        grad = grad_own[here, :].astype(full) + factor * (weighted - rows * (factor * factor * inner))
        grad_resid[here, :] = grad
        grad_attn[here, :] = grad.astype(low)
        gain_total += jnp.sum(grad_normed * rows * factor, axis=0, keepdims=True)
    gain_sum[...] = jnp.broadcast_to(gain_total, gain_sum.shape)
    place = grad_heads.at[span(ring.index * size, size)]
    swaps = []
    for number, index in enumerate([other["seq"] for other in others] + [ring.index]):
        lanes = span(index * heads, heads)
        attended[:, lanes] = dot(grad_attn[...], out_w[:, lanes]).astype(low)
        if number < count - 1:
            swap = send_to(others[number], attended.at[:, lanes], place, swap_send.at[number], swap_recv.at[number])
        else:
            swap = pltpu.make_async_copy(attended.at[:, lanes], place, local)
        swap.start()
        swaps.append(swap)
    reduce.finish()
    for tile in (count_tiles - 2, count_tiles - 1):
        for copy in store(tile):
            copy.wait()
    for swap in swaps:
        swap.wait()


def ffn_back(partial, normed_rows, grad_rows, hidden, down_w, out_w, resid, grad_own, gain_rows, heads, collective_id):
    count = lax.axis_size("seq")
    size, model = resid.shape
    seq_len, units = hidden[0].shape
    grad_w = shape_of((model, units), low)
    return pl.pallas_call(
        functools.partial(ffn_back_kernel, count),
        out_shape=[
            grad_w,
            grad_w,
            grad_w,
            shape_of((seq_len, model), low),
            shape_of((size, model), full),
            shape_of((size, model), low),
            shape_of((8, model), full),
            shape_of((seq_len, heads), low),
        ],
        in_specs=[ANY] * 8 + [VMEM] * 3,
        out_specs=[ANY] * 4 + [VMEM] * 3 + [ANY],
        scratch_shapes=[
            pltpu.VMEM((3, seq_len, units), low),
            pltpu.VMEM(down_w.shape, low),
            pltpu.VMEM(out_w.shape, low),
            pltpu.VMEM((2, 2, seq_len, TILE), low),
            pltpu.VMEM((2, 3, TILE, units), low),
            pltpu.VMEM((2, seq_len, TILE), low),
            pltpu.VMEM((size, model), low),
            pltpu.SemaphoreType.DMA((5,)),
            pltpu.SemaphoreType.DMA((2, 2)),
            pltpu.SemaphoreType.DMA((2, 4)),
            pltpu.SemaphoreType.DMA((count - 1,)),
            pltpu.SemaphoreType.DMA((count - 1,)),
            pltpu.SemaphoreType.DMA,
            *RingReduce.scratch(count, size, model),
        ],
        compiler_params=pltpu.CompilerParams(
            collective_id=collective_id, has_side_effects=True, vmem_limit_bytes=VMEM_LIMIT
        ),
        cost_estimate=pl.CostEstimate(flops=0, bytes_accessed=300_000_000, transcendentals=0),
    )(partial, normed_rows, grad_rows, *hidden, down_w, out_w, resid, grad_own, gain_rows)


def attend_back_kernel(
    count,
    shard_count,
    length,
    grad_heads,
    queries,
    keys,
    values,
    cos_in,
    sin_in,
    rows_in,
    query_w,
    key_w,
    value_w,
    branch,
    resid,
    grad_attn,
    attended_own,
    unit_grad_w,
    output,
    partial,
    grad_w,
    gain_sum,
    out_sum,
    owned_w,
    cos,
    sin,
    weights,
    grads,
    sum_k,
    sum_v,
    row_tiles,
    staged,
    grad_staged,
    out_staged,
    out_beside,
    out_across,
    loads,
    tile_loads,
    stores,
    grad_stores,
    beside_sems,
    across_sems,
    slots,
    terms,
    ring_send,
    ring_recv,
    term_loads,
    *shard_scratch,
):
    ring, shards = Ring(count), Shards(shard_count)
    seq_len, width = queries.shape
    size, model = resid.shape
    blocks, tiles = seq_len // BLOCK, model // TILE
    scale = 1.0 / math.sqrt(HD)
    limit = length[0]
    inputs = [
        pltpu.make_async_copy(source, place, loads.at[number])
        for number, (source, place) in enumerate(
            (
                (cos_in, cos),
                (sin_in, sin),
                (query_w, weights.at[:, pl.ds(0, width)]),
                (key_w, weights.at[:, pl.ds(width, width)]),
                (value_w, weights.at[:, pl.ds(2 * width, width)]),
            )
        )
    ]
    greet([*ring.next, *shards.greeted()])
    reduce = RingReduce(ring, row_piece(branch, size), slots, terms, ring_send, ring_recv, term_loads)
    reduce.start()
    shard_reduce = ShardReduce(shards, unit_grad_w, *shard_scratch)
    shard_reduce.start()
    for load in inputs:
        load.start()

    out_rows = model // shard_count

    def out_term(shard, lanes):
        return dot(grad_attn[:, span(shard * out_rows, out_rows)], attended_own[:, lanes], 0, 0)

    def beside(offset):
        return send_to(
            shards.sibling,
            out_staged.at[offset],
            out_beside.at[offset],
            beside_sems.at[0, offset],
            beside_sems.at[1, offset],
        )

    def across(offset):
        return send_to(
            {"dp": shards.device(shards.chip_at(offset), shards.core)},
            out_beside.at[offset],
            out_across.at[offset - 1],
            across_sems.at[0, offset],
            across_sems.at[1, offset],
        )

    offsets = [*range(1, shards.chips), 0]
    out_tile = 512

    def out_start(offset):
        shard = shards.device(shards.chip_at(offset), 1 - shards.core)

        def tile(number, carry):
            lanes = span(number * out_tile, out_tile)
            out_staged[offset, :, lanes] = out_term(shard, lanes).astype(low)
            return carry

        lax.fori_loop(0, model // out_tile, tile, 0)
        beside(offset).start()

    def out_middle(offset):
        shard = shards.device(shards.chip_at(offset), shards.core)
        beside(offset).wait_recv()

        def tile(number, carry):
            lanes = span(number * out_tile, out_tile)
            total = out_beside[offset, :, lanes].astype(full) + out_term(shard, lanes)
            out_beside[offset, :, lanes] = total.astype(low)
            return carry

        lax.fori_loop(0, model // out_tile, tile, 0)
        if offset:
            across(offset).start()

    def out_finish():
        for offset in range(1, shards.chips):
            across(offset).wait_recv()

        def tile(number, carry):
            lanes = span(number * out_tile, out_tile)
            total = out_beside[0, :, lanes].astype(full)
            for offset in range(1, shards.chips):
                total += out_across[offset - 1, :, lanes].astype(full)
            out_sum[:, lanes] = total.astype(low)
            return carry

        lax.fori_loop(0, model // out_tile, tile, 0)
        for offset in offsets:
            beside(offset).wait_send()
            if offset:
                across(offset).wait_send()

    def attend_block(head, number):
        lanes = slice(head * HD, (head + 1) * HD)
        here, upto = pl.ds(number * BLOCK, BLOCK), pl.ds(0, (number + 1) * BLOCK)
        if number == 0:
            sum_k[...] = jnp.zeros_like(sum_k)
            sum_v[...] = jnp.zeros_like(sum_v)
            if head == 0:
                for load in inputs[:2]:
                    load.wait()
        query_part, grad_part = queries[here, lanes], grad_heads[here, lanes]
        probs = softmax_block(query_part, keys[upto, lanes], number * BLOCK, limit)
        grad_probs = dot(grad_part, values[upto, lanes], 1, 1)
        inner = jnp.sum(probs * grad_probs, axis=-1, keepdims=True)
        grad_scores = (probs * (grad_probs - inner)).astype(low)
        sum_v[upto, :] += dot(probs.astype(low), grad_part, 0, 0)
        sum_k[upto, :] += dot(grad_scores, query_part, 0, 0)
        grad_query = dot(grad_scores, keys[upto, lanes]) * scale
        grads[here, lanes] = turned_back(grad_query, cos[here, :], sin[here, :]).astype(low)
        if number == blocks - 1:
            key_lanes = slice(width + head * HD, width + (head + 1) * HD)
            value_lanes = slice(2 * width + head * HD, 2 * width + (head + 1) * HD)
            grads[:, key_lanes] = turned_back(sum_k[...] * scale, cos[...], sin[...]).astype(low)
            grads[:, value_lanes] = sum_v[...].astype(low)

    def fetch(tile):
        return pltpu.make_async_copy(
            rows_in.at[:, pl.ds(tile * TILE, TILE)], row_tiles.at[tile % 2], tile_loads.at[tile % 2]
        )

    def store(number):
        return pltpu.make_async_copy(
            staged.at[number % 2], partial.at[pl.ds(number * BLOCK, BLOCK)], stores.at[number % 2]
        )

    def grad_store(tile):
        return pltpu.make_async_copy(
            grad_staged.at[tile % 2], grad_w.at[pl.ds(tile * TILE, TILE)], grad_stores.at[tile % 2]
        )

    def rows_back(number):
        if number == 0:
            for load in inputs[2:]:
                load.wait()
            fetch(0).start()
        if number >= 2:
            store(number - 2).wait()
        staged[number % 2] = dot(grads[pl.ds(number * BLOCK, BLOCK), :], weights[...], 1, 1).astype(low)
        store(number).start()

    def weights_back(tile):
        if tile + 1 < tiles:
            fetch(tile + 1).start()
        if tile >= 2:
            grad_store(tile - 2).wait()
        fetch(tile).wait()
        grad = dot(row_tiles[tile % 2], grads[...], 0, 0)
        grad_staged[tile % 2] = grad.astype(low)
        grad_store(tile).start()
        shared = grad * weights[pl.ds(tile * TILE, TILE), :].astype(full)
        gain_sum[:, pl.ds(tile * TILE, TILE)] = lax.dot_general(
            jnp.ones((8, shared.shape[1]), full),
            shared,
            (((1,), (1,)), ((), ())),
            precision=lax.Precision.HIGHEST,
            preferred_element_type=full,
        )

    def finish_output():
        for part in range(PARTS):
            here = pl.ds(part * reduce.size, reduce.size)
            position = (
                ring.index * size + part * reduce.size + lax.broadcasted_iota(jnp.int32, (reduce.size, model), 0)
            )
            total = resid[here, :] + reduce.total(part)
            output[here, :] = jnp.where(position < limit, total, 0.0).astype(low)

    tasks = [functools.partial(out_start, offset) for offset in offsets] + [shard_reduce.spread]
    attention = [
        functools.partial(attend_block, head, number) for head in range(width // HD) for number in range(blocks)
    ]
    tasks += attention[:2] + [functools.partial(out_middle, offset) for offset in offsets] + attention[2:]
    tasks += [functools.partial(rows_back, number) for number in range(blocks)]
    tasks += [functools.partial(weights_back, tile) for tile in range(tiles)]
    weave(tasks, [*reduce.steps(), lambda: None])
    for number in (blocks - 2, blocks - 1):
        store(number).wait()
    for tile in (tiles - 2, tiles - 1):
        grad_store(tile).wait()
    owned_w[...] = shard_reduce.total()
    out_finish()
    finish_output()
    reduce.finish()
    shard_reduce.finish()


def attend_back(
    length,
    grad_heads,
    queries,
    keys,
    values,
    tables,
    rows,
    query_w,
    key_w,
    value_w,
    branch,
    resid,
    grad_attn,
    attended_own,
    unit_grad_w,
    collective_id,
):
    count, shard_count = lax.axis_size("seq"), lax.axis_size("dp")
    seq_len, width = queries.shape
    size, model = resid.shape
    chips, out_rows, units = shard_count // CORES, model // shard_count, unit_grad_w.shape[1]
    return pl.pallas_call(
        functools.partial(attend_back_kernel, count, shard_count),
        out_shape=[
            shape_of((size, model), low),
            shape_of((seq_len, model), low),
            shape_of((model, 3 * width), low),
            shape_of((8, model), full),
            shape_of((out_rows, model), low),
            shape_of((out_rows, units), full),
        ],
        in_specs=[SMEM] + [VMEM] * 4 + [ANY] * 7 + [VMEM] * 3 + [ANY],
        out_specs=[VMEM, ANY, ANY, VMEM, VMEM, VMEM],
        scratch_shapes=[
            pltpu.VMEM((seq_len, HD), full),
            pltpu.VMEM((seq_len, HD), full),
            pltpu.VMEM((model, 3 * width), low),
            pltpu.VMEM((seq_len, 3 * width), low),
            pltpu.VMEM((seq_len, HD), full),
            pltpu.VMEM((seq_len, HD), full),
            pltpu.VMEM((2, seq_len, TILE), low),
            pltpu.VMEM((2, BLOCK, model), low),
            pltpu.VMEM((2, TILE, 3 * width), low),
            pltpu.VMEM((chips, out_rows, model), low),
            pltpu.VMEM((chips, out_rows, model), low),
            pltpu.VMEM((chips - 1, out_rows, model), low),
            pltpu.SemaphoreType.DMA((5,)),
            pltpu.SemaphoreType.DMA((2,)),
            pltpu.SemaphoreType.DMA((2,)),
            pltpu.SemaphoreType.DMA((2,)),
            pltpu.SemaphoreType.DMA((2, chips)),
            pltpu.SemaphoreType.DMA((2, chips)),
            *RingReduce.scratch(count, size, model),
            *ShardReduce.scratch(shard_count, out_rows, units),
        ],
        compiler_params=pltpu.CompilerParams(
            collective_id=collective_id, has_side_effects=True, vmem_limit_bytes=VMEM_LIMIT
        ),
        cost_estimate=pl.CostEstimate(flops=0, bytes_accessed=250_000_000, transcendentals=0),
    )(
        length,
        grad_heads,
        queries,
        keys,
        values,
        *tables,
        rows,
        query_w,
        key_w,
        value_w,
        branch,
        resid,
        grad_attn,
        attended_own,
        unit_grad_w,
    )


def last_kernel(
    count,
    shard_count,
    partial,
    grad_w,
    up_grad_w,
    down_grad_w,
    out_sum,
    tokens,
    gain_rows,
    grad_resid,
    gain_blocks,
    grad_tokens,
    grad_query_w,
    grad_key_w,
    grad_value_w,
    grad_out_w,
    grad_up_w,
    grad_down_w,
    gains,
    gain_slots,
    gain_sum,
    gain_shards,
    gain_sems,
    shard_gain_sems,
    *scratch,
):
    out_scratch, ring_scratch = scratch[:5], scratch[5:10]
    shard_scratch = grouped(scratch[10:], 6)
    ring, shards = Ring(count), Shards(shard_count)
    size = tokens.shape[0]
    rows, width = grad_out_w.shape
    others = [{"seq": (ring.index + offset) % count} for offset in range(1, count)]
    greet([*others, *shards.others()])

    def out_piece(index, part):
        piece = rows // PARTS
        return out_sum.at[pl.ds(part * piece, piece), span(index * width, width)]

    reduce = RingReduce(ring, row_piece(partial, size), *ring_scratch)
    out_reduce = RingReduce(ring, out_piece, *out_scratch)
    reduce.start()
    out_reduce.start()
    weights = [
        ShardReduce(shards, whole, *one) for whole, one in zip((up_grad_w, down_grad_w, grad_w), shard_scratch)
    ]
    gain_copies = [
        send_to(
            other,
            gain_blocks.at[other["seq"]],
            gain_slots.at[ring.index],
            gain_sems.at[0, number],
            gain_sems.at[1, number],
        )
        for number, other in enumerate(others)
    ]
    shard_gain_copies = [
        send_to(
            other, gain_sum, gain_shards.at[shards.index], shard_gain_sems.at[0, number], shard_gain_sems.at[1, number]
        )
        for number, other in enumerate(shards.others())
    ]
    for copy in gain_copies:
        copy.start()
    for weight in weights:
        weight.start()
    for weight in weights:
        weight.spread()
    gain_slots[ring.index] = gain_blocks[ring.index]
    for copy in gain_copies:
        copy.wait_recv()
    gain_sum[...] = jnp.sum(gain_slots[...], axis=0)
    for copy in shard_gain_copies:
        copy.start()

    def finish_gains():
        gain_shards[shards.index] = gain_sum[...]
        for copy in shard_gain_copies:
            copy.wait_recv()
        gains[...] = jnp.sum(gain_shards[...], axis=0)

    def finish_qkv():
        total = weights[2].total()
        for number, place in enumerate((grad_query_w, grad_key_w, grad_value_w)):
            place[...] = total[:, number * width : (number + 1) * width]

    def finish_up():
        grad_up_w[...] = weights[0].total()

    def finish_down():
        grad_down_w[...] = weights[1].total()

    out_steps, steps = out_reduce.steps(), reduce.steps()
    finals = [finish_gains, finish_up, finish_down]
    for number, step in enumerate(steps):
        out_steps[number]()
        step()
        if number < len(finals):
            finals[number]()
    finish_qkv()
    for part in range(PARTS):
        grad_out_w[pl.ds(part * out_reduce.size, out_reduce.size), :] = out_reduce.total(part)
    for part in range(PARTS):
        here = pl.ds(part * reduce.size, reduce.size)
        grad_normed, values = reduce.total(part), tokens[here, :].astype(full)
        factor = lax.rsqrt(jnp.mean(values * values, axis=-1, keepdims=True) + EPSILON)
        weighted = grad_normed * gain_rows[0:1, :]
        inner = jnp.mean(weighted * values, axis=-1, keepdims=True)
        grad_tokens[here, :] = grad_resid[here, :] + factor * (weighted - values * (factor * factor * inner))
    reduce.finish()
    out_reduce.finish()
    for weight in weights:
        weight.finish()
    for copy in (*gain_copies, *shard_gain_copies):
        copy.wait_send()


def last(partial, grad_w, up_grad_w, down_grad_w, out_sum, tokens, gain_rows, grad_resid, gain_blocks, collective_id):
    count, shard_count = lax.axis_size("seq"), lax.axis_size("dp")
    size = tokens.shape[0]
    rows, model = out_sum.shape
    width, units = model // count, up_grad_w.shape[1]
    block = gain_blocks.shape[1:]
    return pl.pallas_call(
        functools.partial(last_kernel, count, shard_count),
        out_shape=[
            shape_of(tokens.shape, full),
            *[shape_of((rows, width), full)] * 4,
            *[shape_of((rows, units), full)] * 2,
            shape_of(block, full),
        ],
        in_specs=[ANY] * 5 + [VMEM] * 4,
        out_specs=[VMEM] * 8,
        scratch_shapes=[
            pltpu.VMEM((count, *block), full),
            pltpu.VMEM(block, full),
            pltpu.VMEM((shard_count, *block), full),
            pltpu.SemaphoreType.DMA((2, count - 1)),
            pltpu.SemaphoreType.DMA((2, shard_count - 1)),
            *RingReduce.scratch(count, rows, width),
            *RingReduce.scratch(count, size, model),
            *ShardReduce.scratch(shard_count, rows, units),
            *ShardReduce.scratch(shard_count, rows, units),
            *ShardReduce.scratch(shard_count, rows, 3 * width),
        ],
        compiler_params=pltpu.CompilerParams(
            collective_id=collective_id, has_side_effects=True, vmem_limit_bytes=VMEM_LIMIT
        ),
        cost_estimate=pl.CostEstimate(flops=0, bytes_accessed=200_000_000, transcendentals=0),
    )(partial, grad_w, up_grad_w, down_grad_w, out_sum, tokens, gain_rows, grad_resid, gain_blocks)


def body(
    tokens,
    lengths,
    cotangent,
    w_query,
    w_key,
    w_value,
    w_out,
    w_gate,
    w_up,
    w_down,
    gain_attn,
    gain_ffn,
):
    tok_rows = tokens.shape[0]
    seq_len = tok_rows * lax.axis_size("seq")
    head_width = w_query.shape[1]
    length = lengths[0]
    local_pos = lax.axis_index("seq") * tok_rows + jnp.arange(tok_rows, dtype=jnp.int32)
    valid_mask = (local_pos < length).astype(jnp.float32)[:, None]
    tables = rope_tables(seq_len)
    gains = jnp.concatenate(
        [gain_attn[None], gain_ffn[None], jnp.zeros((14, gain_attn.shape[0]), gain_attn.dtype)], axis=0
    )
    grad_ffn = jnp.where(valid_mask > 0, cotangent, jnp.zeros_like(cotangent))

    full1, gain_rows, query_w, key_w, value_w, gate_w, up_w = norm_gather(
        tokens, gains, (w_query, w_key, w_value, w_gate, w_up), 1
    )
    queries, key_rot, values, attended_heads, grad_full, down_w, out_full = attend(
        lengths, full1, query_w, key_w, value_w, tables, grad_ffn, w_out, w_down, 2
    )
    attended_tok, resid, full2, activation, grad_gate, grad_up, partial2 = ffn(
        attended_heads, out_full, tokens, gain_rows, gate_w, up_w, down_w, grad_full, 3
    )
    grad_w_gate, grad_w_up, grad_w_down, branch, grad_resid, grad_attn, gain_ffn_sum, grad_heads = ffn_back(
        partial2,
        full2,
        grad_full,
        (activation, grad_gate, grad_up),
        down_w,
        out_full,
        resid,
        grad_ffn,
        gain_rows,
        head_width,
        4,
    )
    output, partial1, grad_w, gain_attn_sum, out_sum, owned_gate = attend_back(
        lengths,
        grad_heads,
        queries,
        key_rot,
        values,
        tables,
        full1,
        query_w,
        key_w,
        value_w,
        branch,
        resid,
        grad_attn,
        attended_tok,
        grad_w_gate,
        5,
    )
    count, shard_count = lax.axis_size("seq"), lax.axis_size("dp")
    gain_sums = jnp.stack([gain_attn_sum[0] / gain_rows[0], gain_ffn_sum[0]])
    piece = gain_sums.shape[1] // (count * shard_count)
    gain_blocks = gain_sums.reshape(2, shard_count, count, piece).transpose(2, 1, 0, 3)
    gain_blocks = gain_blocks.reshape(count, shard_count, 2 * piece)
    gain_blocks = jnp.pad(gain_blocks, ((0, 0), (0, 8 - shard_count), (0, 128 - 2 * piece)))
    grad_tokens, owned_query, owned_key, owned_value, owned_out, owned_up, owned_down, owned_gains = last(
        partial1, grad_w, grad_w_up, grad_w_down, out_sum, tokens, gain_rows, grad_resid, gain_blocks, 6
    )
    owned_gains = lax.dynamic_index_in_dim(owned_gains, lax.axis_index("dp"), 0, keepdims=False)
    owned_gain_attn, owned_gain_ffn = owned_gains[:piece], owned_gains[piece : 2 * piece]
    return (
        output,
        grad_tokens,
        owned_query,
        owned_key,
        owned_value,
        owned_out,
        owned_gate,
        owned_up,
        owned_down,
        owned_gain_attn,
        owned_gain_ffn,
    )


def solution(mesh):
    rows, shard = P(("dp", "seq"), None), P("dp", "seq")
    gains = P(("dp", "seq"))
    return jax.shard_map(
        body,
        mesh=mesh,
        in_specs=(rows, P("dp"), rows, *[shard] * 7, P("dp"), P("dp")),
        out_specs=(rows, rows, *[shard] * 7, gains, gains),
        check_vma=False,
    )
```

time: 1000 us -> 614 us (0.61)
  matrix products: 185 us -> 0 us
  waiting for transfers between devices: 171 us -> 0 us
  Pallas kernels: 475 us -> 584 us
  blocking collectives: 93 us -> 0 us
  other arithmetic: 34.8 us -> 3.81 us
  between operations: 15.3 us -> 1.85 us
    dot_general x21 -> x0, matrix products: 185 us -> none  [the longest x7 64.4 us: contract_cols(): lax.dot_general(left, right, (((1,), (1,)), ((), ())), preferred_element_...]
    reduce_scatter x8 -> x0, waiting for transfers between devices: 147 us -> none  [the longest x1 44.2 us: body(): lax.psum_scatter(grad_w_up.astype(jnp.bfloat16), 'dp', scatter_dimension=...]
    pallas_call x8 -> x6, Pallas kernels: 475 us -> 584 us  [the longest x1 125 us: last(): pl.pallas_call(functools.partial(last_kernel, count, shard_count), out_sh...]
    all_to_all x1 -> x0, blocking collectives: 42.8 us -> none  [body(): lax.all_to_all(grad_attended, 'seq', split_axis=1, concat_axis=0, tiled=T...]
    unnamed x1 -> x0, blocking collectives: 39.9 us -> none
    convert_element_type x14 -> x0, other arithmetic: 20.5 us -> none  [the longest x6 13.7 us: body(): owned_query, owned_key, owned_value, owned_out, owned_gate, owned_up, own...]
    all_gather x8 -> x0, waiting for transfers between devices: 19.1 us -> none  [the longest x1 19 us: body(): lax.all_gather(w_out, 'dp', axis=0, tiled=True)]
    all_gather x2 -> x0, blocking collectives: 10.3 us -> none  [the longest x1 5.16 us: body(): lax.all_gather(gain_ffn, 'dp', axis=0, tiled=True)]
  transfers between devices with their start and end apart: 17 -> 0, of which waited for: 6 -> 0; matrix products, arithmetic and copies ran while one was open for 17% -> 0% of each run, Pallas kernels for 35% -> 0%
where the time goes in v2:
time: 614 us; the launch traced here: 605 us
  Pallas kernels  584 us (95%)
  local copies, waits for them, and re-layouts  15.6 us (3%)
    pallas_call x1, Pallas kernels, last(): pl.pallas_call(functools.partial(last_kernel, count, shard_count), out_sh...  125 us
    pallas_call x1, Pallas kernels, ffn(): pl.pallas_call(functools.partial(ffn_kernel, count), out_shape=[shape_of(...  103 us
    pallas_call x1, Pallas kernels, norm_gather(): pl.pallas_call(functools.partial(norm_gather_kernel, count, shard_count,...  94.3 us
    pallas_call x1, Pallas kernels, attend(): pl.pallas_call(functools.partial(attend_kernel, count, shard_count), out_...  94 us
    pallas_call x1, Pallas kernels, ffn_back(): pl.pallas_call(functools.partial(ffn_back_kernel, count), out_shape=[grad...  84.2 us
    pallas_call x1, Pallas kernels, attend_back(): pl.pallas_call(functools.partial(attend_back_kernel, count, shard_count),...  83.3 us

profile of v2, /device:TPU:0, one launch (start us, length us, event | category | flops | bytes accessed | tf_op | source)
XLA Modules:
  0.0 605.0 jit_solution(8636702136711283580)
XLA Ops:
  1.4 0.7 broadcast_in_dim.21
  2.1 0.7 broadcast_in_dim.22
  2.8 0.7 maximum_maximum_fusion.refs_1_
  3.4 2.1 broadcast_select_fusion.grad_own
  5.6 94.3 %shard_map.221 = (bf16[1536,2048]{1,0:T(8,128)(2,1)}, f32[8,2048]{1,0:T(8,128)}, bf16[2048,256]{1,0:T(8,128)(2,1)}, bf16[2048,256]{1,0:T(8,128)(2,1)}, bf16[2048...) custom-call(bf16[192,2048]{1,0:T(8,128)(2,1)} %tokens.3, ...), custom_call_target="tpu_custom_call" | custom-call | bytes 200000000 | tf_op jit(solution)/shard_map/pallas_call | solution.py:473
  99.9 94.0 %shard_map.222 = (bf16[1536,256]{1,0:T(8,128)(2,1)}, bf16[1536,256]{1,0:T(8,128)(2,1)}, bf16[1536,256]{1,0:T(8,128)(2,1)}, bf16[1536,256]{1,0:T(8,128)(2,1)}, bf...) custom-call(s32[1]{0:T(128)} %copy.36.length, ...), custom_call_target="tpu_custom_call" | custom-call | bytes 250000000 | tf_op jit(solution)/shard_map/pallas_call | solution.py:665
  193.9 102.9 %shard_map.223 = (bf16[192,2048]{1,0:T(8,128)(2,1)}, f32[192,2048]{1,0:T(8,128)}, bf16[1536,2048]{1,0:T(8,128)(2,1)}, bf16[1536,1024]{1,0:T(8,128)(2,1)}, bf16[1...) custom-call(bf16[1536,256]{1,0:T(8,128)(2,1)} %get-tuple-element.58.attended, ...), custom_call_target="tpu_custom_call" | custom-call | bytes 300000000 | tf_op jit(solution)/shard_map/pallas_call | solution.py:876
  296.9 84.2 %shard_map.224 = (bf16[2048,1024]{1,0:T(8,128)(2,1)}, bf16[2048,1024]{1,0:T(8,128)(2,1)}, bf16[2048,1024]{1,0:T(8,128)(2,1)}, bf16[1536,2048]{1,0:T(8,128)(2,1)}...) custom-call(bf16[1536,2048]{1,0:T(8,128)(2,1)} %get-tuple-element.65.partial, ...), custom_call_target="tpu_custom_call" | custom-call | bytes 300000000 | tf_op jit(solution)/shard_map/pallas_call | solution.py:1053
  381.1 83.3 %shard_map.225 = (bf16[192,2048]{1,0:T(8,128)(2,1)}, bf16[1536,2048]{1,0:T(8,128)(2,1)}, bf16[2048,768]{1,0:T(8,128)(2,1)}, f32[8,2048]{1,0:T(8,128)}, bf16[512,2048]{1,0:T(8,128)(2,1)}, /*index=5*/f32[512,1024]{1,0:T(8,128)}) custom-call(s32[1]{0:T(128)} %copy.36.length, bf16[1536,256]{1,0:T(8,128)(2,1)} %get-tuple-element.71.grad_heads, ...), custom_call_target="tpu_custom_call" | custom-call | bytes 250000000 | tf_op jit(solution)/shard_map/pallas_call | solution.py:1352
  464.4 1.0 slice_reduce_fusion
  465.7 0.6 pad.4.gain_blocks
  466.4 124.9 %shard_map.226 = (f32[192,2048]{1,0:T(8,128)}, f32[512,256]{1,0:T(8,128)}, f32[512,256]{1,0:T(8,128)}, f32[512,256]{1,0:T(8,128)}, f32[512,256]{1,0:T(8,128)}, /...) custom-call(bf16[1536,2048]{1,0:T(8,128)(2,1)} %get-tuple-element.80.partial, ...), custom_call_target="tpu_custom_call" | custom-call | bytes 200000000 | tf_op jit(solution)/shard_map/pallas_call | solution.py:1532
  591.3 0.8 constant_dynamic-slice_fusion
  592.1 0.6 slice_bitcast_fusion
  592.7 0.9 copy.37
  593.5 2.9 copy.38
  596.4 0.8 copy.39
  597.2 0.8 copy.40
  598.0 0.8 copy.41
  598.8 0.8 copy.42
  599.6 1.3 copy.43
  600.9 1.3 copy.44
  602.2 1.0 copy-done.1
  603.3 1.3 copy.45
  (24 shorter events, 0.4 us)
Async XLA Ops:
  466.4 126.3 %copy-start.3 = (bf16[192,2048]{1,0:T(8,128)(2,1)S(1)}, bf16[192,2048]{1,0:T(8,128)(2,1)}, u32[]{:S(2)}) copy-start(bf16[192,2048]{1,0:T(8,128)(2,1)} %get-tuple-element.112) | copy-start | bytes 2359300
  591.3 5.1 copy-start.7
  591.3 5.9 copy-start.6
  592.7 5.3 copy-start.5
  593.5 5.2 copy-start.4
  593.5 6.0 copy-start
  598.0 2.9 copy-start.2
  600.9 2.3 copy-start.1

commit v3 on v2

--- a/solution.py
+++ b/solution.py
@@ -13,6 +13,8 @@
 WINDOW = 2048
 EPSILON = 1e-05
 NEGATIVE = -1e30
+BLOCK = 256
+TILE = 256
 LINE = 4
 CORES = 2
 PARTS = 2
@@ -271,7 +273,7 @@
     def __init__(self, shards, own, whole, send, recv, local):
         self.shards, self.own, self.whole = shards, own, whole
         self.send, self.recv, self.local = send, recv, local
-        self.rows = own.shape[0]
+        self.rows = whole.shape[0] // shards.count
         self.size = self.rows // PARTS
 
     @staticmethod
@@ -280,6 +282,8 @@
         return [pltpu.SemaphoreType.DMA(shape), pltpu.SemaphoreType.DMA(shape), pltpu.SemaphoreType.DMA]
 
     def source(self, part):
+        if self.own is None:
+            return self.place(self.shards.index, part)
         return self.own.at[pl.ds(part * self.size, self.size)]
 
     def place(self, shard, part):
@@ -308,16 +312,16 @@
         )
 
     def keep(self):
-        return pltpu.make_async_copy(
-            self.own, self.whole.at[span(self.shards.index * self.rows, self.rows)], self.local
-        )
+        place = self.whole.at[span(self.shards.index * self.rows, self.rows)]
+        return pltpu.make_async_copy(self.own, place, self.local)
 
     def start(self):
         for part in range(PARTS):
             for offset in range(1, self.shards.chips):
                 self.across(offset, part).start()
             self.beside(0, part).start()
-        self.keep().start()
+        if self.own is not None:
+            self.keep().start()
 
     def pass_on(self):
         for part in range(PARTS):
@@ -325,14 +329,19 @@
                 self.across(offset, part).wait_recv()
                 self.beside(offset, part).start()
 
+    def arrive(self):
+        for part in range(PARTS):
+            for offset in range(self.shards.chips):
+                self.beside(offset, part).wait_recv()
+        if self.own is not None:
+            self.keep().wait()
+
     def finish(self):
         for part in range(PARTS):
             for offset in range(self.shards.chips):
-                self.beside(offset, part).wait_recv()
                 self.beside(offset, part).wait_send()
                 if offset:
                     self.across(offset, part).wait_send()
-        self.keep().wait()
 
 
 class ShardReduce:
@@ -414,87 +423,6 @@
     return [refs[number : number + size] for number in range(0, len(refs), size)]
 
 
-def norm_gather_kernel(count, shard_count, weights, *refs):
-    tokens, gains, *shard_refs = refs[: 2 + weights]
-    all_rows, gain_rows, *whole_refs = refs[2 + weights : 4 + 2 * weights]
-    own, all_gains, send, recv, local, ring_send, ring_recv, *shard_sems = refs[4 + 2 * weights :]
-    ring, shards = Ring(count), Shards(shard_count)
-    greet([*ring.next, *shards.others()])
-    copies = [
-        send_to(target, gains, all_gains.at[shards.index], send.at[offset], recv.at[offset])
-        for offset, target in enumerate(shards.others())
-    ]
-    for copy in copies:
-        copy.start()
-    gathers = [
-        ShardGather(shards, shard, whole, *sems)
-        for shard, whole, sems in zip(shard_refs, whole_refs, grouped(shard_sems, 3))
-    ]
-    early, late = gathers[:-1], gathers[-1]
-    for gather in early:
-        gather.start()
-    all_gains[shards.index] = gains[...]
-    rows = tokens[...].astype(full)
-    factor = lax.rsqrt(jnp.mean(rows * rows, axis=-1, keepdims=True) + EPSILON)
-    rows = rows * factor
-    for copy in copies:
-        copy.wait_recv()
-    width = gains.shape[1]
-    for shard in range(shard_count):
-        gain_rows[:, shard * width : (shard + 1) * width] = all_gains[shard, :8, :].astype(full)
-    own[...] = (rows * gain_rows[0:1, :]).astype(low)
-    place = row_piece(all_rows, own.shape[0])
-    size = own.shape[0] // PARTS
-    gather = RingGather(ring, lambda part: own.at[pl.ds(part * size, size)], place, ring_send, ring_recv)
-    gather.start()
-    kept = pltpu.make_async_copy(own, all_rows.at[span(ring.index * own.shape[0], own.shape[0])], local)
-    kept.start()
-    for number, step in enumerate(gather.steps()):
-        step()
-        if number == 0:
-            late.start()
-        elif number == 1:
-            for other in early[:-1]:
-                other.pass_on()
-        elif number == 2:
-            early[-1].pass_on()
-    late.pass_on()
-    gather.finish()
-    for other in gathers:
-        other.finish()
-    kept.wait()
-    for copy in copies:
-        copy.wait_send()
-
-
-def norm_gather(tokens, gains, weights, collective_id):
-    count, shard_count = lax.axis_size("seq"), lax.axis_size("dp")
-    rows, width = tokens.shape
-    return pl.pallas_call(
-        functools.partial(norm_gather_kernel, count, shard_count, len(weights)),
-        out_shape=[
-            shape_of((count * rows, width), low),
-            shape_of((8, width), full),
-            *[shape_of((shard_count * weight.shape[0], weight.shape[1]), low) for weight in weights],
-        ],
-        in_specs=[VMEM, VMEM] + [ANY] * len(weights),
-        out_specs=[ANY, VMEM] + [ANY] * len(weights),
-        scratch_shapes=[
-            pltpu.VMEM((rows, width), low),
-            pltpu.VMEM((shard_count, *gains.shape), low),
-            pltpu.SemaphoreType.DMA((shard_count - 1,)),
-            pltpu.SemaphoreType.DMA((shard_count - 1,)),
-            pltpu.SemaphoreType.DMA,
-            *ring_semaphores(count),
-            *ShardGather.semaphores(shard_count) * len(weights),
-        ],
-        compiler_params=pltpu.CompilerParams(
-            collective_id=collective_id, has_side_effects=True, vmem_limit_bytes=VMEM_LIMIT
-        ),
-        cost_estimate=pl.CostEstimate(flops=0, bytes_accessed=200_000_000, transcendentals=0),
-    )(tokens, gains, *weights)
-
-
 def rope_tables(seq_len):
     half_dim = HD // 2
     steps = np.arange(half_dim, dtype=np.float32) * np.float32(2.0 / HD)
@@ -528,276 +456,208 @@
     return exponent * (1.0 / jnp.sum(exponent, axis=-1, keepdims=True))
 
 
-BLOCK = 256
-
-
-def attend_kernel(
-    count,
-    shard_count,
-    length,
-    rows_in,
-    query_w,
-    key_w,
-    value_w,
-    cos_in,
-    sin_in,
-    grad_own,
-    out_own,
-    down_own,
-    queries,
-    keys,
-    values,
-    attended,
-    grad_rows,
-    down_all,
-    out_all,
-    out_mine,
-    rows,
-    weights,
-    cos,
-    sin,
-    loads,
-    local,
-    grad_send,
-    grad_recv,
-    out_send,
-    out_recv,
-    *shard_sems,
-):
+def forward_kernel(count, shard_count, *refs):
+    (length, tokens, gains, cotangent, query_in, key_in, value_in, out_in, gate_in, up_in, down_in, cos_in, sin_in) = (
+        refs[:13]
+    )
+    (gain_rows, queries, keys, values, grad_own, attended_own, resid) = refs[13:20]
+    (all_rows, grad_rows, normed_rows, qkv_out, out_out, down_out, act_out, grad_gate_out, grad_up_out, partial) = (
+        refs[20:30]
+    )
+    (all_gains, qkv_w, out_w, gate_w, up_w, down_w, cos, sin, own, attended, normed, grads, hidden, back) = refs[30:44]
+    (gain_sems, local, row_loads, stores, weight_stores, swap_sems) = refs[44:50]
+    sems = refs[50:]
+    out_sems, row_sems, grad_sems, normed_sems = grouped(sems[:8], 2)
+    shard_sems = grouped(sems[8:], 3)
+
     ring, shards = Ring(count), Shards(shard_count)
+    size, model = tokens.shape
     seq_len, width = queries.shape
-    own_rows = grad_own.shape[0]
-    out_rows, out_width = out_own.shape
-    blocks = seq_len // BLOCK
-    weight_loads = [
-        pltpu.make_async_copy(source, weights.at[number], loads.at[blocks + number])
-        for number, source in enumerate((query_w, key_w, value_w))
-    ]
-    table_loads = [
-        pltpu.make_async_copy(cos_in, cos, loads.at[blocks + 3]),
-        pltpu.make_async_copy(sin_in, sin, loads.at[blocks + 4]),
-    ]
-    row_loads = [
-        pltpu.make_async_copy(rows_in.at[pl.ds(n * BLOCK, BLOCK)], rows.at[pl.ds(n * BLOCK, BLOCK)], loads.at[n])
-        for n in range(blocks)
-    ]
-    for load in (*weight_loads, row_loads[0], *table_loads, *row_loads[1:]):
-        load.start()
-    greet([*ring.next, *shards.greeted()])
-
-    out_size, grad_size = out_rows // PARTS, own_rows // PARTS
+    units = gate_w.shape[1]
+    limit = length[0]
+    others = [{"seq": (ring.index + offset) % count} for offset in range(1, count)]
+    tables = [pltpu.make_async_copy(cos_in, cos, local.at[0]), pltpu.make_async_copy(sin_in, sin, local.at[1])]
+    for table in tables:
+        table.start()
+    greet([*others, *shards.others()])
+
+    out_rows, out_width = out_in.shape
+    out_mine = out_w.at[span(shards.index * out_rows, out_rows)]
+    out_piece = out_rows // PARTS
     out_gather = RingGather(
         ring,
-        lambda part: out_own.at[pl.ds(part * out_size, out_size)],
-        lambda index, part: out_mine.at[pl.ds(part * out_size, out_size), span(index * out_width, out_width)],
-        out_send,
-        out_recv,
+        lambda part: out_in.at[pl.ds(part * out_piece, out_piece)],
+        lambda index, part: out_w.at[
+            span(shards.index * out_rows + part * out_piece, out_piece), span(index * out_width, out_width)
+        ],
+        *out_sems,
     )
-    grad_gather = RingGather(
-        ring,
-        lambda part: grad_own.at[pl.ds(part * grad_size, grad_size)],
-        row_piece(grad_rows, own_rows),
-        grad_send,
-        grad_recv,
+    out_kept = pltpu.make_async_copy(out_in, out_mine.at[:, span(ring.index * out_width, out_width)], local.at[2])
+    out_gather.start()
+    out_kept.start()
+    gain_copies = [
+        send_to(target, gains, all_gains.at[shards.index], gain_sems.at[0, number], gain_sems.at[1, number])
+        for number, target in enumerate(shards.others())
+    ]
+    for copy in gain_copies:
+        copy.start()
+    qkv_gathers = [
+        ShardGather(shards, source, qkv_w.at[:, pl.ds(number * width, width)], *shard_sems[number])
+        for number, source in enumerate((query_in, key_in, value_in))
+    ]
+    out_shards = ShardGather(shards, None, out_w, *shard_sems[3])
+    gate_gather, up_gather, down_gather = (
+        ShardGather(shards, source, whole, *shard_sems[4 + number])
+        for number, (source, whole) in enumerate(((gate_in, gate_w), (up_in, up_w), (down_in, down_w)))
     )
-    out_gather.start()
-    grad_gather.start()
-    kept = [
-        pltpu.make_async_copy(
-            out_own, out_mine.at[:, span(ring.index * out_width, out_width)], local.at[0]
-        ),
-        pltpu.make_async_copy(grad_own, grad_rows.at[span(ring.index * own_rows, own_rows)], local.at[1]),
-    ]
-    for copy in kept:
-        copy.start()
-    down_sems, out_sems = grouped(shard_sems, 3)
-    down_gather = ShardGather(shards, down_own, down_all, *down_sems)
-    shard_gather = ShardGather(shards, out_mine, out_all, *out_sems)
-    down_gather.start()
-
-    def spread_out():
-        kept[0].wait()
-        out_gather.finish()
-        shard_gather.start()
-
-    grad_steps = grad_gather.steps()
-    events = [*out_gather.steps(), spread_out, *grad_steps[:2], down_gather.pass_on, *grad_steps[2:-1]]
-    events += [shard_gather.pass_on, grad_steps[-1]]
-
-    def project(n):
-        if n == 0:
-            for load in (*weight_loads, *table_loads):
-                load.wait()
-        row_loads[n].wait()
-        here = pl.ds(n * BLOCK, BLOCK)
-        block = rows[here, :]
-        for number, place in enumerate((queries, keys, values)):
-            linear = dot(block, weights[number])
-            for head in range(width // HD):
-                lanes = slice(head * HD, (head + 1) * HD)
-                one = linear[:, lanes]
-                if number < 2:
-                    one = turned(one, cos[here, :], sin[here, :])
-                place[here, lanes] = one.astype(low)
-
-    limit = length[0]
-
-    def attend(head, n):
-        lanes = slice(head * HD, (head + 1) * HD)
-        here, upto = pl.ds(n * BLOCK, BLOCK), pl.ds(0, (n + 1) * BLOCK)
-        probs = softmax_block(queries[here, lanes], keys[upto, lanes], n * BLOCK, limit)
-        attended[here, lanes] = dot(probs.astype(low), values[upto, lanes]).astype(low)
-
-    tasks = [functools.partial(project, n) for n in range(blocks)]
-    tasks += [functools.partial(attend, head, n) for head in range(width // HD) for n in range(blocks)]
-    weave(tasks, events)
-    grad_gather.finish()
-    down_gather.finish()
-    shard_gather.finish()
-    kept[1].wait()
-
-
-def attend(length, rows, query_w, key_w, value_w, tables, grad_own, out_own, down_own, collective_id):
-    count, shard_count = lax.axis_size("seq"), lax.axis_size("dp")
-    seq_len, model = rows.shape
-    heads = shape_of((seq_len, query_w.shape[1]), low)
-    out_rows = out_own.shape[0]
-    return pl.pallas_call(
-        functools.partial(attend_kernel, count, shard_count),
-        out_shape=[heads] * 4
-        + [
-            shape_of(rows.shape, low),
-            shape_of((model, down_own.shape[1]), low),
-            shape_of((model, model), low),
-        ],
-        in_specs=[SMEM] + [ANY] * 9,
-        out_specs=[VMEM] * 4 + [ANY] * 3,
-        scratch_shapes=[
-            pltpu.VMEM((out_rows, model), low),
-            pltpu.VMEM(rows.shape, low),
-            pltpu.VMEM((3, *query_w.shape), low),
-            pltpu.VMEM((seq_len, HD), full),
-            pltpu.VMEM((seq_len, HD), full),
-            pltpu.SemaphoreType.DMA((seq_len // BLOCK + 5,)),
-            pltpu.SemaphoreType.DMA((2,)),
-            *ring_semaphores(count),
-            *ring_semaphores(count),
-            *ShardGather.semaphores(shard_count) * 2,
-        ],
-        compiler_params=pltpu.CompilerParams(
-            collective_id=collective_id, has_side_effects=True, vmem_limit_bytes=VMEM_LIMIT
-        ),
-        cost_estimate=pl.CostEstimate(flops=0, bytes_accessed=250_000_000, transcendentals=0),
-    )(length, rows, query_w, key_w, value_w, *tables, grad_own, out_own, down_own)
-
-
-TILE = 256
-
-
-def ffn_kernel(
-    count,
-    attended,
-    out_in,
-    tokens,
-    gain_rows,
-    gate_in,
-    up_in,
-    down_in,
-    grad_rows,
-    attended_own,
-    resid,
-    normed_rows,
-    act_out,
-    grad_gate_out,
-    grad_up_out,
-    partial,
-    out_w,
-    gate_w,
-    up_w,
-    down_w,
-    own,
-    normed,
-    grads,
-    hidden,
-    back,
-    loads,
-    row_loads,
-    stores,
-    swap_send,
-    swap_recv,
-    ring_send,
-    ring_recv,
-    local,
-):
-    ring = Ring(count)
-    size, model = tokens.shape
-    heads = attended.shape[1]
-    units = gate_w.shape[1]
-    weight_loads = [
-        pltpu.make_async_copy(source, place, loads.at[number])
-        for number, (source, place) in enumerate(
-            ((out_in, out_w), (gate_in, gate_w), (up_in, up_w), (down_in, down_w))
-        )
-    ]
-    others = [{"seq": (ring.index + offset) % count} for offset in range(1, count)]
-    weight_loads[0].start()
-    greet(others)
-    place = attended_own.at[:, span(ring.index * heads, heads)]
-    swaps = [
-        send_to(
-            other, attended.at[span(other["seq"] * size, size)], place, swap_send.at[number], swap_recv.at[number]
-        )
-        for number, other in enumerate(others)
-    ]
-    for swap in swaps:
-        swap.start()
-    kept = pltpu.make_async_copy(attended.at[span(ring.index * size, size)], place, local.at[0])
-    kept.start()
-    for load in weight_loads[1:]:
-        load.start()
-    weight_loads[0].wait()
-    kept.wait()
-    for swap in swaps:
-        swap.wait_recv()
-
-    def project(tile, carry):
-        lanes = span(tile * TILE, TILE)
-        resid[:, lanes] = tokens[:, lanes].astype(full) + dot(attended_own[...], out_w[lanes, :], 1, 1)
-        return carry
-
-    lax.fori_loop(0, model // TILE, project, 0)
-    rows = resid[...]
-    factor = lax.rsqrt(jnp.mean(rows * rows, axis=-1, keepdims=True) + EPSILON)
-    own[...] = (rows * factor * gain_rows[1:2, :]).astype(low)
+    for gather in qkv_gathers:
+        gather.start()
+
     piece = size // PARTS
-    gather = RingGather(
-        ring, lambda part: own.at[pl.ds(part * piece, piece)], row_piece(normed_rows, size), ring_send, ring_recv
-    )
-    gather.start()
-    kept = pltpu.make_async_copy(own, normed_rows.at[span(ring.index * size, size)], local.at[1])
-    kept.start()
+    rows = tokens[...].astype(full)
+    rows = rows * lax.rsqrt(jnp.mean(rows * rows, axis=-1, keepdims=True) + EPSILON)
+    all_gains[shards.index] = gains[...]
+    for copy in gain_copies:
+        copy.wait_recv()
+    gain_width = gains.shape[1]
+    for shard in range(shard_count):
+        gain_rows[:, shard * gain_width : (shard + 1) * gain_width] = all_gains[shard, :8, :].astype(full)
+    own[0] = (rows * gain_rows[0:1, :]).astype(low)
+
+    def own_gather(source, whole, pair):
+        return RingGather(ring, lambda part: source.at[pl.ds(part * piece, piece)], row_piece(whole, size), *pair)
+
+    def own_kept(source, whole, number):
+        return pltpu.make_async_copy(source, whole.at[span(ring.index * size, size)], local.at[number])
+
+    row_gather = own_gather(own.at[0], all_rows, row_sems)
+    row_gather.start()
+    row_kept = own_kept(own.at[0], all_rows, 3)
+    row_kept.start()
+    gate_gather.start()
+    position = ring.index * size + lax.broadcasted_iota(jnp.int32, (size, model), 0)
+    grad_own[...] = jnp.where(position < limit, cotangent[...].astype(full), 0.0).astype(low)
+    grad_gather = own_gather(grad_own, grad_rows, grad_sems)
+    grad_kept = own_kept(grad_own, grad_rows, 4)
+    grad_kept.start()
 
     def owners(step):
         if step in (0, ring.half):
             return [ring.shifted(step)]
         return [ring.shifted(-step), ring.shifted(step)]
 
+    def normed_loads(step, mine, whole):
+        return [
+            pltpu.make_async_copy(
+                mine if step == 0 else whole.at[span(owner * size, size)],
+                normed.at[pl.ds(side * size, size)],
+                row_loads.at[2, side],
+            )
+            for side, owner in enumerate(owners(step))
+        ]
+
+    def project(step):
+        loads = normed_loads(step, own.at[0], all_rows)
+        for load in loads:
+            load.start()
+        for load in loads:
+            load.wait()
+        linear = dot(normed[pl.ds(0, size * len(loads)), :], qkv_w[...])
+        for side, owner in enumerate(owners(step)):
+            here = span(owner * size, size)
+            side_cos, side_sin = cos[here, :], sin[here, :]
+            for number, place in enumerate((queries, keys, values)):
+                for head in range(width // HD):
+                    lanes = slice(head * HD, (head + 1) * HD)
+                    first = number * width + head * HD
+                    one = linear[side * size : (side + 1) * size, first : first + HD]
+                    if number < 2:
+                        one = turned(one, side_cos, side_sin)
+                    place[here, lanes] = one.astype(low)
+
+    for step in out_gather.steps():
+        step()
+    out_kept.wait()
+    for gather in qkv_gathers:
+        gather.pass_on()
+    out_shards.start()
+    row_gather.advance(1)
+    up_gather.start()
+    for table in tables:
+        table.wait()
+    for gather in qkv_gathers:
+        gather.arrive()
+    qkv_store = pltpu.make_async_copy(qkv_w, qkv_out, weight_stores.at[0])
+    qkv_store.start()
+    project(0)
+    project(1)
+    for step in range(2, ring.half + 1):
+        row_gather.advance(step)
+        if step == 2:
+            gate_gather.pass_on()
+        if step == ring.half:
+            grad_gather.start()
+            down_gather.start()
+        project(step)
+
+    blocks = seq_len // BLOCK
+
+    def swap(head, number):
+        other = others[number]
+        lanes = pl.ds(head * HD, HD)
+        return send_to(
+            other,
+            attended.at[span(other["seq"] * size, size), lanes],
+            attended_own.at[:, span(ring.index * width + head * HD, HD)],
+            swap_sems.at[0, head, number],
+            swap_sems.at[1, head, number],
+        )
+
+    swap_kept = pltpu.make_async_copy(
+        attended.at[span(ring.index * size, size)],
+        attended_own.at[:, span(ring.index * width, width)],
+        local.at[5],
+    )
+    for head in range(width // HD):
+        lanes = slice(head * HD, (head + 1) * HD)
+        for number in range(blocks):
+            here, upto = pl.ds(number * BLOCK, BLOCK), pl.ds(0, (number + 1) * BLOCK)
+            probs = softmax_block(queries[here, lanes], keys[upto, lanes], number * BLOCK, limit)
+            attended[here, lanes] = dot(probs.astype(low), values[upto, lanes]).astype(low)
+        for number in range(count - 1):
+            swap(head, number).start()
+    swap_kept.start()
+    up_gather.pass_on()
+    grad_gather.advance(1)
+    out_shards.pass_on()
+    out_shards.arrive()
+    out_store = pltpu.make_async_copy(out_w, out_out, weight_stores.at[1])
+    out_store.start()
+    swap_kept.wait()
+    for head in range(width // HD):
+        for number in range(count - 1):
+            swap(head, number).wait_recv()
+
+    def out_project(tile, carry):
+        lanes = span(tile * TILE, TILE)
+        resid[:, lanes] = tokens[:, lanes].astype(full) + dot(attended_own[...], out_w[lanes, :], 1, 1)
+        return carry
+
+    lax.fori_loop(0, model // TILE, out_project, 0)
+    rows = resid[...]
+    factor = lax.rsqrt(jnp.mean(rows * rows, axis=-1, keepdims=True) + EPSILON)
+    own[1] = (rows * factor * gain_rows[1:2, :]).astype(low)
+    normed_gather = own_gather(own.at[1], normed_rows, normed_sems)
+    normed_gather.start()
+    normed_kept = own_kept(own.at[1], normed_rows, 6)
+    normed_kept.start()
+
     def grad_loads(step):
         return [
             pltpu.make_async_copy(
-                grad_rows.at[span(owner * size, size)],
+                grad_own if step == 0 else grad_rows.at[span(owner * size, size)],
                 grads.at[step % 2, pl.ds(side * size, size)],
                 row_loads.at[step % 2, side],
-            )
-            for side, owner in enumerate(owners(step))
-        ]
-
-    def normed_loads(step):
-        return [
-            pltpu.make_async_copy(
-                own if step == 0 else normed_rows.at[span(owner * size, size)],
-                normed.at[pl.ds(side * size, size)],
-                row_loads.at[2, side],
             )
             for side, owner in enumerate(owners(step))
         ]
@@ -813,19 +673,13 @@
             results.append(pltpu.make_async_copy(back.at[here], partial.at[there], stores.at[side, 3]))
         return results
 
-    def block(step):
-        for load in normed_loads(step):
+    def feed(step):
+        for load in (*normed_loads(step, own.at[1], normed_rows), *grad_loads(step)):
             load.start()
-        if step < ring.half:
-            for load in grad_loads(step + 1):
-                load.start()
         if step > 0:
             for store in result_stores(step - 1):
                 store.wait()
-        if step == 0:
-            for load in weight_loads[1:]:
-                load.wait()
-        for load in (*normed_loads(step), *grad_loads(step)):
+        for load in (*normed_loads(step, own.at[1], normed_rows), *grad_loads(step)):
             load.wait()
         rows = pl.ds(0, size * len(owners(step)))
         slot = step % 2
@@ -854,61 +708,90 @@
         for store in result_stores(step):
             store.start()
 
-    for load in grad_loads(0):
-        load.start()
-    block(0)
+    grad_gather.advance(2)
+    down_gather.pass_on()
+    gate_gather.arrive()
+    up_gather.arrive()
+    down_gather.arrive()
+    down_store = pltpu.make_async_copy(down_w, down_out, weight_stores.at[2])
+    down_store.start()
+    feed(0)
+    for step in range(3, ring.half + 1):
+        grad_gather.advance(step)
     for step in range(1, ring.half + 1):
-        gather.advance(step)
-        block(step)
+        normed_gather.advance(step)
+        feed(step)
     for store in result_stores(ring.half):
         store.wait()
-    gather.finish()
-    kept.wait()
-    for swap in swaps:
-        swap.wait_send()
-
-
-def ffn(attended, out_w, tokens, gain_rows, gate_w, up_w, down_w, grad_rows, collective_id):
-    count = lax.axis_size("seq")
+    for gather in (out_gather, row_gather, grad_gather, normed_gather):
+        gather.finish()
+    for gather in (*qkv_gathers, out_shards, gate_gather, up_gather, down_gather):
+        gather.finish()
+    for copy in (row_kept, grad_kept, normed_kept, qkv_store, out_store, down_store):
+        copy.wait()
+    for copy in gain_copies:
+        copy.wait_send()
+    for head in range(width // HD):
+        for number in range(count - 1):
+            swap(head, number).wait_send()
+
+
+def forward(length, tokens, gains, cotangent, weights, tables, collective_id):
+    count, shard_count = lax.axis_size("seq"), lax.axis_size("dp")
     size, model = tokens.shape
-    seq_len, units = grad_rows.shape[0], gate_w.shape[1]
-    hidden = shape_of((seq_len, units), low)
+    seq_len, width, units = size * count, weights[0].shape[1], weights[4].shape[1]
+    heads, hidden, rows = shape_of((seq_len, width), low), shape_of((seq_len, units), low), shape_of((size, model), low)
+    all_rows = shape_of((seq_len, model), low)
+    dma = pltpu.SemaphoreType.DMA
     return pl.pallas_call(
-        functools.partial(ffn_kernel, count),
+        functools.partial(forward_kernel, count, shard_count),
         out_shape=[
-            shape_of((size, model), low),
+            shape_of((8, model), full),
+            heads,
+            heads,
+            heads,
+            rows,
+            rows,
             shape_of((size, model), full),
-            shape_of((seq_len, model), low),
+            all_rows,
+            all_rows,
+            all_rows,
+            shape_of((model, 3 * width), low),
+            shape_of((model, model), low),
+            shape_of((model, units), low),
             hidden,
             hidden,
             hidden,
-            shape_of((seq_len, model), low),
+            all_rows,
         ],
-        in_specs=[ANY, ANY, VMEM, VMEM, ANY, ANY, ANY, ANY],
-        out_specs=[VMEM, VMEM, ANY, ANY, ANY, ANY, ANY],
+        in_specs=[SMEM] + [VMEM] * 3 + [ANY] * 9,
+        out_specs=[VMEM] * 7 + [ANY] * 10,
         scratch_shapes=[
-            pltpu.VMEM(out_w.shape, low),
-            pltpu.VMEM(gate_w.shape, low),
-            pltpu.VMEM(up_w.shape, low),
-            pltpu.VMEM(down_w.shape, low),
-            pltpu.VMEM((size, model), low),
+            pltpu.VMEM((shard_count, *gains.shape), low),
+            pltpu.VMEM((model, 3 * width), low),
+            pltpu.VMEM((model, model), low),
+            *[pltpu.VMEM((model, units), low)] * 3,
+            *[pltpu.VMEM((seq_len, HD), full)] * 2,
+            pltpu.VMEM((2, size, model), low),
+            pltpu.VMEM((seq_len, width), low),
             pltpu.VMEM((2 * size, model), low),
             pltpu.VMEM((2, 2 * size, model), low),
             pltpu.VMEM((3, 2 * size, units), low),
             pltpu.VMEM((2 * size, model), low),
-            pltpu.SemaphoreType.DMA((4,)),
-            pltpu.SemaphoreType.DMA((3, 2)),
-            pltpu.SemaphoreType.DMA((2, 4)),
-            pltpu.SemaphoreType.DMA((count - 1,)),
-            pltpu.SemaphoreType.DMA((count - 1,)),
-            *ring_semaphores(count),
-            pltpu.SemaphoreType.DMA((2,)),
+            dma((2, shard_count - 1)),
+            dma((7,)),
+            dma((3, 2)),
+            dma((2, 4)),
+            dma((3,)),
+            dma((2, width // HD, count - 1)),
+            *ring_semaphores(count) * 4,
+            *ShardGather.semaphores(shard_count) * 7,
         ],
         compiler_params=pltpu.CompilerParams(
             collective_id=collective_id, has_side_effects=True, vmem_limit_bytes=VMEM_LIMIT
         ),
-        cost_estimate=pl.CostEstimate(flops=0, bytes_accessed=300_000_000, transcendentals=0),
-    )(attended, out_w, tokens, gain_rows, gate_w, up_w, down_w, grad_rows)
+        cost_estimate=pl.CostEstimate(flops=0, bytes_accessed=600_000_000, transcendentals=0),
+    )(length, tokens, gains, cotangent, *weights, *tables)
 
 
 def ffn_back_kernel(
@@ -1098,9 +981,7 @@
     cos_in,
     sin_in,
     rows_in,
-    query_w,
-    key_w,
-    value_w,
+    qkv_w,
     branch,
     resid,
     grad_attn,
@@ -1149,9 +1030,7 @@
             (
                 (cos_in, cos),
                 (sin_in, sin),
-                (query_w, weights.at[:, pl.ds(0, width)]),
-                (key_w, weights.at[:, pl.ds(width, width)]),
-                (value_w, weights.at[:, pl.ds(2 * width, width)]),
+                (qkv_w, weights),
             )
         )
     ]
@@ -1335,9 +1214,7 @@
     values,
     tables,
     rows,
-    query_w,
-    key_w,
-    value_w,
+    qkv_w,
     branch,
     resid,
     grad_attn,
@@ -1359,7 +1236,7 @@
             shape_of((out_rows, model), low),
             shape_of((out_rows, units), full),
         ],
-        in_specs=[SMEM] + [VMEM] * 4 + [ANY] * 7 + [VMEM] * 3 + [ANY],
+        in_specs=[SMEM] + [VMEM] * 4 + [ANY] * 5 + [VMEM] * 3 + [ANY],
         out_specs=[VMEM, ANY, ANY, VMEM, VMEM, VMEM],
         scratch_shapes=[
             pltpu.VMEM((seq_len, HD), full),
@@ -1374,7 +1251,7 @@
             pltpu.VMEM((chips, out_rows, model), low),
             pltpu.VMEM((chips, out_rows, model), low),
             pltpu.VMEM((chips - 1, out_rows, model), low),
-            pltpu.SemaphoreType.DMA((5,)),
+            pltpu.SemaphoreType.DMA((3,)),
             pltpu.SemaphoreType.DMA((2,)),
             pltpu.SemaphoreType.DMA((2,)),
             pltpu.SemaphoreType.DMA((2,)),
@@ -1395,9 +1272,7 @@
         values,
         *tables,
         rows,
-        query_w,
-        key_w,
-        value_w,
+        qkv_w,
         branch,
         resid,
         grad_attn,
@@ -1499,12 +1374,12 @@
         grad_down_w[...] = weights[1].total()
 
     out_steps, steps = out_reduce.steps(), reduce.steps()
-    finals = [finish_gains, finish_up, finish_down]
     for number, step in enumerate(steps):
         out_steps[number]()
         step()
-        if number < len(finals):
-            finals[number]()
+    finish_gains()
+    finish_up()
+    finish_down()
     finish_qkv()
     for part in range(PARTS):
         grad_out_w[pl.ds(part * out_reduce.size, out_reduce.size), :] = out_reduce.total(part)
@@ -1572,26 +1447,32 @@
     gain_attn,
     gain_ffn,
 ):
-    tok_rows = tokens.shape[0]
-    seq_len = tok_rows * lax.axis_size("seq")
+    seq_len = tokens.shape[0] * lax.axis_size("seq")
     head_width = w_query.shape[1]
-    length = lengths[0]
-    local_pos = lax.axis_index("seq") * tok_rows + jnp.arange(tok_rows, dtype=jnp.int32)
-    valid_mask = (local_pos < length).astype(jnp.float32)[:, None]
     tables = rope_tables(seq_len)
     gains = jnp.concatenate(
         [gain_attn[None], gain_ffn[None], jnp.zeros((14, gain_attn.shape[0]), gain_attn.dtype)], axis=0
     )
-    grad_ffn = jnp.where(valid_mask > 0, cotangent, jnp.zeros_like(cotangent))
-
-    full1, gain_rows, query_w, key_w, value_w, gate_w, up_w = norm_gather(
-        tokens, gains, (w_query, w_key, w_value, w_gate, w_up), 1
-    )
-    queries, key_rot, values, attended_heads, grad_full, down_w, out_full = attend(
-        lengths, full1, query_w, key_w, value_w, tables, grad_ffn, w_out, w_down, 2
-    )
-    attended_tok, resid, full2, activation, grad_gate, grad_up, partial2 = ffn(
-        attended_heads, out_full, tokens, gain_rows, gate_w, up_w, down_w, grad_full, 3
+    (
+        gain_rows,
+        queries,
+        keys,
+        values,
+        grad_ffn,
+        attended_tok,
+        resid,
+        full1,
+        grad_full,
+        full2,
+        qkv_w,
+        out_full,
+        down_w,
+        activation,
+        grad_gate,
+        grad_up,
+        partial2,
+    ) = forward(
+        lengths, tokens, gains, cotangent, (w_query, w_key, w_value, w_out, w_gate, w_up, w_down), tables, 1
     )
     grad_w_gate, grad_w_up, grad_w_down, branch, grad_resid, grad_attn, gain_ffn_sum, grad_heads = ffn_back(
         partial2,
@@ -1610,13 +1491,11 @@
         lengths,
         grad_heads,
         queries,
-        key_rot,
+        keys,
         values,
         tables,
         full1,
-        query_w,
-        key_w,
-        value_w,
+        qkv_w,
         branch,
         resid,
         grad_attn,

time: 614 us -> 539 us (0.88)
  Pallas kernels: 584 us -> 510 us
    pallas_call x3 -> x1, Pallas kernels: 291 us -> 253 us  [forward(): pl.pallas_call(functools.partial(forward_kernel, count, shard_count), out...]
    pallas_call x1, Pallas kernels: 125 us -> 93.8 us  [last(): pl.pallas_call(functools.partial(last_kernel, count, shard_count), out_sh...]
where the time goes in v3:
time: 539 us; the launch traced here: 529 us
  Pallas kernels  510 us (95%)
  local copies, waits for them, and re-layouts  15.6 us (3%)
    pallas_call x1, Pallas kernels, forward(): pl.pallas_call(functools.partial(forward_kernel, count, shard_count), out...  253 us
    pallas_call x1, Pallas kernels, last(): pl.pallas_call(functools.partial(last_kernel, count, shard_count), out_sh...  93.8 us
    pallas_call x1, Pallas kernels, attend_back(): pl.pallas_call(functools.partial(attend_back_kernel, count, shard_count),...  81.8 us
    pallas_call x1, Pallas kernels, ffn_back(): pl.pallas_call(functools.partial(ffn_back_kernel, count), out_shape=[grad...  81.5 us
    unnamed x25, local copies, waits for them, and re-layouts  11.9 us

profile of v3, /device:TPU:0, one launch (start us, length us, event | category | flops | bytes accessed | tf_op | source)
XLA Modules:
  0.0 529.1 jit_solution(5107617455752053037)
XLA Ops:
  1.3 0.7 broadcast_in_dim.10
  2.0 0.7 broadcast_in_dim.9
  2.7 0.1 pad.9.clone
  2.7 0.7 maximum_maximum_fusion.refs_2_
  3.4 252.9 %shard_map.221 = (f32[8,2048]{1,0:T(8,128)}, bf16[1536,256]{1,0:T(8,128)(2,1)}, bf16[1536,256]{1,0:T(8,128)(2,1)}, bf16[1536,256]{1,0:T(8,128)(2,1)}, bf16[192,2...) custom-call(s32[1]{0:T(128)S(6)} %copy.36.refs_0_.length, ...), custom_call_target="tpu_custom_call" | custom-call | bytes 600000000 | tf_op jit(solution)/shard_map/pallas_call | solution.py:746
  256.4 81.5 %shard_map.222 = (bf16[2048,1024]{1,0:T(8,128)(2,1)}, bf16[2048,1024]{1,0:T(8,128)(2,1)}, bf16[2048,1024]{1,0:T(8,128)(2,1)}, bf16[1536,2048]{1,0:T(8,128)(2,1)}...) custom-call(bf16[1536,2048]{1,0:T(8,128)(2,1)} %get-tuple-element.50.partial, ...), custom_call_target="tpu_custom_call" | custom-call | bytes 300000000 | tf_op jit(solution)/shard_map/pallas_call | solution.py:936
  337.9 81.8 %shard_map.223 = (bf16[192,2048]{1,0:T(8,128)(2,1)}, bf16[1536,2048]{1,0:T(8,128)(2,1)}, bf16[2048,768]{1,0:T(8,128)(2,1)}, f32[8,2048]{1,0:T(8,128)}, bf16[512,2048]{1,0:T(8,128)(2,1)}, /*index=5*/f32[512,1024]{1,0:T(8,128)}) custom-call(s32[1]{0:T(128)S(6)} %copy.36.refs_0_.length, bf16[1536,256]{1,0:T(8,128)(2,1)} %get-tuple-element.61.grad_heads, ...), custom_call_target="tpu_custom_call" | custom-call | bytes 250000000 | tf_op jit(solution)/shard_map/pallas_call | solution.py:1229
  419.7 1.0 slice_reduce_fusion
  420.6 0.1 stack.8
  420.9 0.1 reshape.30
  421.0 0.6 pad.4.gain_blocks
  421.6 93.8 %shard_map.224 = (f32[192,2048]{1,0:T(8,128)}, f32[512,256]{1,0:T(8,128)}, f32[512,256]{1,0:T(8,128)}, f32[512,256]{1,0:T(8,128)}, f32[512,256]{1,0:T(8,128)}, /...) custom-call(bf16[1536,2048]{1,0:T(8,128)(2,1)} %get-tuple-element.72.partial, ...), custom_call_target="tpu_custom_call" | custom-call | bytes 200000000 | tf_op jit(solution)/shard_map/pallas_call | solution.py:1407
  515.4 0.8 constant_dynamic-slice_fusion
  516.2 0.6 slice_bitcast_fusion
  516.8 0.9 copy.37
  517.6 2.9 copy.38
  520.5 0.8 copy.39
  521.3 0.8 copy.40
  522.1 0.8 copy.41
  522.9 0.8 copy.42
  523.7 1.3 copy.43
  525.0 1.3 copy.44
  526.3 1.0 copy-done.1
  527.4 1.3 copy.45
  (20 shorter events, 0.2 us)
Async XLA Ops:
  421.6 95.2 %copy-start.3 = (bf16[192,2048]{1,0:T(8,128)(2,1)S(1)}, bf16[192,2048]{1,0:T(8,128)(2,1)}, u32[]{:S(2)}) copy-start(bf16[192,2048]{1,0:T(8,128)(2,1)} %get-tuple-element.104) | copy-start | bytes 2359300
  515.4 5.1 copy-start.7
  515.4 5.9 %copy-start.6 = (f32[512,256]{1,0:T(8,128)S(1)}, f32[512,256]{1,0:T(8,128)}, u32[]{:S(2)}) copy-start(f32[512,256]{1,0:T(8,128)} %get-tuple-element.107) | copy-start | bytes 1572868
  516.8 5.3 %copy-start.5 = (f32[512,256]{1,0:T(8,128)S(1)}, f32[512,256]{1,0:T(8,128)}, u32[]{:S(2)}) copy-start(f32[512,256]{1,0:T(8,128)} %get-tuple-element.108) | copy-start | bytes 1572868
  517.6 5.2 copy-start.4
  517.6 6.0 %copy-start = (f32[512,1024]{1,0:T(8,128)S(1)}, f32[512,1024]{1,0:T(8,128)}, u32[]{:S(2)}) copy-start(f32[512,1024]{1,0:T(8,128)} %get-tuple-element.110) | copy-start | bytes 6291460
  522.1 2.9 copy-start.2
  525.0 2.3 copy-start.1

commit v4 on v3

--- a/solution.py
+++ b/solution.py
@@ -239,6 +239,14 @@
                 for part in self.pieces(way, step):
                     self.copy(way, step, part).wait_send()
 
+    def free(self, sems):
+        for way in range(2):
+            pl.semaphore_signal(sems.at[way], inc=1, device_id=self.ring.next[way], device_id_type=MESH)
+
+    def wait_free(self, sems):
+        for way in range(2):
+            pl.semaphore_wait(sems.at[way], 1)
+
 
 def row_piece(ref, rows):
     size = rows // PARTS
@@ -345,24 +353,14 @@
 
 
 class ShardReduce:
-    def __init__(self, shards, whole, own, beside_slots, across_slots, loads, beside_sems, across_sems):
+    def __init__(self, shards, whole, beside_slots, across_slots, work, loads, stores, beside_sems, across_sems):
         self.shards, self.whole = shards, whole
-        self.own, self.beside_slots, self.across_slots = own, beside_slots, across_slots
-        self.loads, self.beside_sems, self.across_sems = loads, beside_sems, across_sems
-        self.rows = own.shape[1]
+        self.beside_slots, self.across_slots = beside_slots, across_slots
+        self.work, self.loads, self.stores = work, loads, stores
+        self.beside_sems, self.across_sems = beside_sems, across_sems
+        self.rows = whole.shape[0] // shards.count
+        self.lanes = pl.ds(0, whole.shape[1])
         self.offsets = [*range(1, shards.chips), 0]
-
-    @staticmethod
-    def scratch(count, rows, width):
-        chips = count // CORES
-        return [
-            pltpu.VMEM((chips, rows, width), low),
-            pltpu.VMEM((chips, rows, width), low),
-            pltpu.VMEM((chips - 1, rows, width), low),
-            pltpu.SemaphoreType.DMA((chips,)),
-            pltpu.SemaphoreType.DMA((2, chips)),
-            pltpu.SemaphoreType.DMA((2, chips)),
-        ]
 
     def block(self, offset, core):
         shard = self.shards.device(self.shards.chip_at(offset), core)
@@ -377,11 +375,6 @@
             self.beside_sems.at[1, offset],
         )
 
-    def load(self, offset):
-        return pltpu.make_async_copy(
-            self.block(offset, self.shards.core), self.own.at[offset], self.loads.at[offset]
-        )
-
     def across(self, offset):
         return send_to(
             {"dp": self.shards.device(self.shards.chip_at(offset), self.shards.core)},
@@ -391,26 +384,51 @@
             self.across_sems.at[1, offset],
         )
 
+    def fetches(self, offset):
+        sources = (self.beside_slots.at[offset], self.block(offset, self.shards.core))
+        return [
+            pltpu.make_async_copy(source, self.work.at[offset, number, :, self.lanes], self.loads.at[offset, number])
+            for number, source in enumerate(sources)
+        ]
+
+    def keep(self, offset):
+        return pltpu.make_async_copy(
+            self.work.at[offset, 0, :, self.lanes], self.beside_slots.at[offset], self.stores.at[offset]
+        )
+
     def start(self):
         for offset in self.offsets:
             self.beside(offset).start()
-            self.load(offset).start()
-
-    def spread(self):
+
+    def load(self):
         for offset in self.offsets:
             self.beside(offset).wait_recv()
-            self.load(offset).wait()
-            total = self.beside_slots[offset].astype(full) + self.own[offset].astype(full)
-            self.beside_slots[offset] = total.astype(low)
-            if offset:
-                self.across(offset).start()
-
-    def total(self):
-        total = self.beside_slots[0].astype(full)
-        for offset in range(1, self.shards.chips):
+            for fetch in self.fetches(offset):
+                fetch.start()
+
+    def add(self):
+        for offset in self.offsets:
+            for fetch in self.fetches(offset):
+                fetch.wait()
+            total = self.work[offset, 0, :, self.lanes].astype(full) + self.work[offset, 1, :, self.lanes].astype(full)
+            self.work[offset, 0, :, self.lanes] = total.astype(low)
+            self.keep(offset).start()
+
+    def stored(self):
+        for offset in self.offsets:
+            self.keep(offset).wait()
+
+    def cross(self):
+        for offset in self.offsets[:-1]:
+            self.across(offset).start()
+
+    def pass_on(self):
+        self.stored()
+        self.cross()
+
+    def arrive(self):
+        for offset in self.offsets[:-1]:
             self.across(offset).wait_recv()
-            total += self.across_slots[offset - 1].astype(full)
-        return total
 
     def finish(self):
         for offset in self.offsets:
@@ -460,13 +478,20 @@
     (length, tokens, gains, cotangent, query_in, key_in, value_in, out_in, gate_in, up_in, down_in, cos_in, sin_in) = (
         refs[:13]
     )
-    (gain_rows, queries, keys, values, grad_own, attended_own, resid) = refs[13:20]
+    gain_rows, *results = refs[13:20]
     (all_rows, grad_rows, normed_rows, qkv_out, out_out, down_out, act_out, grad_gate_out, grad_up_out, partial) = (
         refs[20:30]
     )
     (all_gains, qkv_w, out_w, gate_w, up_w, down_w, cos, sin, own, attended, normed, grads, hidden, back) = refs[30:44]
     (gain_sems, local, row_loads, stores, weight_stores, swap_sems) = refs[44:50]
-    sems = refs[50:]
+    queries, keys, values, grad_own, attended_own, resid, result_sems = refs[50:57]
+    result_copies = [
+        pltpu.make_async_copy(source, place, result_sems.at[number])
+        for number, (source, place) in enumerate(
+            zip((queries, keys, values, grad_own, attended_own, resid), results)
+        )
+    ]
+    sems = refs[57:]
     out_sems, row_sems, grad_sems, normed_sems = grouped(sems[:8], 2)
     shard_sems = grouped(sems[8:], 3)
 
@@ -600,6 +625,9 @@
             down_gather.start()
         project(step)
 
+    for copy in result_copies[:4]:
+        copy.start()
+
     blocks = seq_len // BLOCK
 
     def swap(head, number):
@@ -647,6 +675,8 @@
     rows = resid[...]
     factor = lax.rsqrt(jnp.mean(rows * rows, axis=-1, keepdims=True) + EPSILON)
     own[1] = (rows * factor * gain_rows[1:2, :]).astype(low)
+    for copy in result_copies[4:]:
+        copy.start()
     normed_gather = own_gather(own.at[1], normed_rows, normed_sems)
     normed_gather.start()
     normed_kept = own_kept(own.at[1], normed_rows, 6)
@@ -716,10 +746,10 @@
     down_store = pltpu.make_async_copy(down_w, down_out, weight_stores.at[2])
     down_store.start()
     feed(0)
-    for step in range(3, ring.half + 1):
-        grad_gather.advance(step)
     for step in range(1, ring.half + 1):
         normed_gather.advance(step)
+        if step + 2 <= ring.half:
+            grad_gather.advance(step + 2)
         feed(step)
     for store in result_stores(ring.half):
         store.wait()
@@ -727,7 +757,7 @@
         gather.finish()
     for gather in (*qkv_gathers, out_shards, gate_gather, up_gather, down_gather):
         gather.finish()
-    for copy in (row_kept, grad_kept, normed_kept, qkv_store, out_store, down_store):
+    for copy in (row_kept, grad_kept, normed_kept, qkv_store, out_store, down_store, *result_copies):
         copy.wait()
     for copy in gain_copies:
         copy.wait_send()
@@ -765,7 +795,7 @@
             all_rows,
         ],
         in_specs=[SMEM] + [VMEM] * 3 + [ANY] * 9,
-        out_specs=[VMEM] * 7 + [ANY] * 10,
+        out_specs=[VMEM] + [ANY] * 16,
         scratch_shapes=[
             pltpu.VMEM((shard_count, *gains.shape), low),
             pltpu.VMEM((model, 3 * width), low),
@@ -784,6 +814,10 @@
             dma((2, 4)),
             dma((3,)),
             dma((2, width // HD, count - 1)),
+            *[pltpu.VMEM((seq_len, width), low)] * 3,
+            *[pltpu.VMEM((size, model), low)] * 2,
+            pltpu.VMEM((size, model), full),
+            dma((6,)),
             *ring_semaphores(count) * 4,
             *ShardGather.semaphores(shard_count) * 7,
         ],
@@ -794,47 +828,18 @@
     )(length, tokens, gains, cotangent, *weights, *tables)
 
 
-def ffn_back_kernel(
-    count,
-    partial,
-    normed_rows,
-    grad_rows,
-    act_in,
-    grad_gate_in,
-    grad_up_in,
-    down_in,
-    out_in,
-    resid,
-    grad_own,
-    gain_rows,
-    grad_gate_w,
-    grad_up_w,
-    grad_down_w,
-    branch,
-    grad_resid,
-    grad_attn,
-    gain_sum,
-    grad_heads,
-    hidden,
-    down_w,
-    out_w,
-    tiles,
-    staged,
-    branch_tile,
-    attended,
-    loads,
-    tile_loads,
-    stores,
-    swap_send,
-    swap_recv,
-    local,
-    slots,
-    terms,
-    ring_send,
-    ring_recv,
-    term_loads,
-):
-    ring = Ring(count)
+def ffn_back_kernel(count, shard_count, *refs):
+    (partial, normed_rows, grad_rows, act_in, grad_gate_in, grad_up_in, down_in, out_in) = refs[:8]
+    resid_in, grad_own_in, gain_rows = refs[8:11]
+    gain_sum, resid_out, attn_out, grad_heads, branch, gate_grad, up_grad, down_grad = refs[11:19]
+    arrived = grouped(refs[19:23], 2)
+    hidden, down_w, out_w, tiles, staged, branch_tile, attended, work = refs[23:31]
+    loads, tile_loads, stores, swap_sems, local, work_loads, work_stores = refs[31:38]
+    reduce_scratch = refs[38:43]
+    resid, grad_own, grad_resid, grad_attn, result_sems = refs[43:48]
+    shard_sems = grouped(refs[48:], 2)
+
+    ring, shards = Ring(count), Shards(shard_count)
     size, model = resid.shape
     heads = grad_heads.shape[1]
     others = [{"seq": (ring.index + offset) % count} for offset in range(1, count)]
@@ -847,59 +852,90 @@
                 (act_in, hidden.at[0]),
                 (down_in, down_w),
                 (out_in, out_w),
+                (resid_in, resid),
+                (grad_own_in, grad_own),
             )
         )
     ]
-    greet(others)
-    reduce = RingReduce(ring, row_piece(partial, size), slots, terms, ring_send, ring_recv, term_loads)
+    greet([*others, *shards.greeted()])
+    reduce = RingReduce(ring, row_piece(partial, size), *reduce_scratch)
     reduce.start()
+    gate, up = (
+        ShardReduce(shards, whole, *one, work, work_loads, work_stores, *sems)
+        for whole, one, sems in zip((gate_grad, up_grad), arrived, shard_sems)
+    )
+    count_tiles = model // TILE
+
+    terms = (
+        (normed_rows, hidden.at[1], gate_grad, inputs[0]),
+        (normed_rows, hidden.at[2], up_grad, inputs[1]),
+        (grad_rows, hidden.at[0], down_grad, inputs[2]),
+    )
+    last = len(terms) * count_tiles - 1
 
     def fetch(tile):
-        lanes = span(tile * TILE, TILE)
-        return [
-            pltpu.make_async_copy(source.at[:, lanes], tiles.at[tile % 2, number], tile_loads.at[tile % 2, number])
-            for number, source in enumerate((normed_rows, grad_rows))
-        ]
+        lanes = pl.ds(tile % count_tiles * TILE, TILE)
+        source = terms[tile // count_tiles][0].at[:, lanes]
+        return pltpu.make_async_copy(source, tiles.at[tile % 3], tile_loads.at[tile % 3])
 
     def store(tile):
-        lanes, slot = span(tile * TILE, TILE), tile % 2
-        copies = [
-            pltpu.make_async_copy(staged.at[slot, number], place.at[lanes], stores.at[slot, number])
-            for number, place in enumerate((grad_gate_w, grad_up_w, grad_down_w))
-        ]
-        copies.append(pltpu.make_async_copy(branch_tile.at[slot], branch.at[:, lanes], stores.at[slot, 3]))
-        return copies
-
-    count_tiles = model // TILE
-    for copy in (inputs[0], *fetch(0), *inputs[1:]):
+        place = terms[tile // count_tiles][2].at[pl.ds(tile % count_tiles * TILE, TILE)]
+        return pltpu.make_async_copy(staged.at[tile % 2], place, stores.at[tile % 2, 0])
+
+    def branch_store(tile):
+        return pltpu.make_async_copy(
+            branch_tile.at[tile % 2], branch.at[:, pl.ds(tile * TILE, TILE)], stores.at[tile % 2, 1]
+        )
+
+    later = {0: inputs[1:2], 1: inputs[5:], count_tiles: inputs[2:3], count_tiles + 2: inputs[3:5]}
+    for copy in (inputs[0], fetch(0), fetch(1)):
         copy.start()
 
     def weights(tile):
+        for copy in later.get(tile, ()):
+            copy.start()
+        slot = tile % 2
+        _, right, _, ready = terms[tile // count_tiles]
+        if tile % count_tiles == 0:
+            ready.wait()
+        if tile + 2 <= last:
+            fetch(tile + 2).start()
+        if tile >= 2:
+            store(tile - 2).wait()
+        fetch(tile).wait()
+        staged[slot] = dot(tiles[tile % 3], right[...], 0, 0).astype(low)
+        store(tile).start()
+
+    def branches(tile):
         slot = tile % 2
         if tile == 0:
-            for copy in inputs[:4]:
-                copy.wait()
-        if tile + 1 < count_tiles:
-            for copy in fetch(tile + 1):
-                copy.start()
+            store(last - 1).wait()
+            store(last).wait()
+            inputs[3].wait()
         if tile >= 2:
-            for copy in store(tile - 2):
-                copy.wait()
-        for copy in fetch(tile):
-            copy.wait()
-        staged[slot, 0] = dot(tiles[slot, 0], hidden[1], 0, 0).astype(low)
-        staged[slot, 1] = dot(tiles[slot, 0], hidden[2], 0, 0).astype(low)
-        staged[slot, 2] = dot(tiles[slot, 1], hidden[0], 0, 0).astype(low)
+            branch_store(tile - 2).wait()
         branch_tile[slot] = dot(hidden[0], down_w[pl.ds(tile * TILE, TILE), :], 1, 1).astype(low)
-        for copy in store(tile):
-            copy.start()
-
-    tasks = [functools.partial(weights, tile) for tile in range(count_tiles)]
-    weave(tasks, [*reduce.steps(), lambda: None])
-    inputs[4].wait()
+        branch_store(tile).start()
+
+    steps = reduce.steps()
+    tasks = [functools.partial(weights, tile) for tile in range(last + 1)]
+    early = count_tiles * 3 // 4
+    weave(tasks[:early], [])
+    steps[0]()
+    weave(tasks[early : count_tiles + 2], [])
+    gate.start()
+    weave(tasks[count_tiles + 2 : 2 * count_tiles + 2], [gate.load, gate.add, gate.pass_on, lambda: None])
+    up.start()
+    weave(tasks[2 * count_tiles + 2 :], [*steps[1:-1], up.load, up.add])
+    tasks = [functools.partial(branches, tile) for tile in range(count_tiles)]
+    weave(tasks, [up.pass_on, lambda: None, steps[-1]])
+    for copy in inputs[4:]:
+        copy.wait()
     gain_total = jnp.zeros((1, model), full)
+    swaps = []
     for part in range(PARTS):
         here = pl.ds(part * reduce.size, reduce.size)
+        there = grad_heads.at[span(ring.index * size + part * reduce.size, reduce.size)]
         grad_normed, rows = reduce.total(part), resid[here, :]
         factor = lax.rsqrt(jnp.mean(rows * rows, axis=-1, keepdims=True) + EPSILON)
         weighted = grad_normed * gain_rows[1:2, :]
@@ -908,60 +944,79 @@
         grad_resid[here, :] = grad
         grad_attn[here, :] = grad.astype(low)
         gain_total += jnp.sum(grad_normed * rows * factor, axis=0, keepdims=True)
+        for number, index in enumerate([other["seq"] for other in others] + [ring.index]):
+            lanes = span(index * heads, heads)
+            attended[here, lanes] = dot(grad_attn[here, :], out_w[:, lanes]).astype(low)
+            source = attended.at[here, lanes]
+            if number < count - 1:
+                sems = (swap_sems.at[0, part, number], swap_sems.at[1, part, number])
+                swap = send_to(others[number], source, there, *sems)
+            else:
+                swap = pltpu.make_async_copy(source, there, local.at[part])
+            swap.start()
+            swaps.append(swap)
     gain_sum[...] = jnp.broadcast_to(gain_total, gain_sum.shape)
-    place = grad_heads.at[span(ring.index * size, size)]
-    swaps = []
-    for number, index in enumerate([other["seq"] for other in others] + [ring.index]):
-        lanes = span(index * heads, heads)
-        attended[:, lanes] = dot(grad_attn[...], out_w[:, lanes]).astype(low)
-        if number < count - 1:
-            swap = send_to(others[number], attended.at[:, lanes], place, swap_send.at[number], swap_recv.at[number])
-        else:
-            swap = pltpu.make_async_copy(attended.at[:, lanes], place, local)
-        swap.start()
-        swaps.append(swap)
+    results = [
+        pltpu.make_async_copy(grad_resid, resid_out, result_sems.at[0]),
+        pltpu.make_async_copy(grad_attn, attn_out, result_sems.at[1]),
+    ]
+    for copy in results:
+        copy.start()
     reduce.finish()
     for tile in (count_tiles - 2, count_tiles - 1):
-        for copy in store(tile):
-            copy.wait()
-    for swap in swaps:
-        swap.wait()
+        branch_store(tile).wait()
+    for one in (gate, up):
+        one.arrive()
+        one.finish()
+    for copy in (*swaps, *results):
+        copy.wait()
 
 
 def ffn_back(partial, normed_rows, grad_rows, hidden, down_w, out_w, resid, grad_own, gain_rows, heads, collective_id):
-    count = lax.axis_size("seq")
+    count, shard_count = lax.axis_size("seq"), lax.axis_size("dp")
     size, model = resid.shape
     seq_len, units = hidden[0].shape
+    chips, shard_rows = shard_count // CORES, model // shard_count
     grad_w = shape_of((model, units), low)
+    dma = pltpu.SemaphoreType.DMA
     return pl.pallas_call(
-        functools.partial(ffn_back_kernel, count),
+        functools.partial(ffn_back_kernel, count, shard_count),
         out_shape=[
+            shape_of((8, model), full),
+            shape_of((size, model), full),
+            shape_of((size, model), low),
+            shape_of((seq_len, heads), low),
+            shape_of((seq_len, model), low),
             grad_w,
             grad_w,
             grad_w,
-            shape_of((seq_len, model), low),
-            shape_of((size, model), full),
-            shape_of((size, model), low),
-            shape_of((8, model), full),
-            shape_of((seq_len, heads), low),
+            *[shape_of((number, shard_rows, units), low) for number in (chips, chips - 1)] * 2,
         ],
-        in_specs=[ANY] * 8 + [VMEM] * 3,
-        out_specs=[ANY] * 4 + [VMEM] * 3 + [ANY],
+        in_specs=[ANY] * 10 + [VMEM],
+        out_specs=[VMEM] + [ANY] * 11,
         scratch_shapes=[
             pltpu.VMEM((3, seq_len, units), low),
             pltpu.VMEM(down_w.shape, low),
             pltpu.VMEM(out_w.shape, low),
-            pltpu.VMEM((2, 2, seq_len, TILE), low),
-            pltpu.VMEM((2, 3, TILE, units), low),
+            pltpu.VMEM((3, seq_len, TILE), low),
+            pltpu.VMEM((2, TILE, units), low),
             pltpu.VMEM((2, seq_len, TILE), low),
             pltpu.VMEM((size, model), low),
-            pltpu.SemaphoreType.DMA((5,)),
-            pltpu.SemaphoreType.DMA((2, 2)),
-            pltpu.SemaphoreType.DMA((2, 4)),
-            pltpu.SemaphoreType.DMA((count - 1,)),
-            pltpu.SemaphoreType.DMA((count - 1,)),
-            pltpu.SemaphoreType.DMA,
+            pltpu.VMEM((chips, 2, shard_rows, units), low),
+            dma((7,)),
+            dma((3,)),
+            dma((2, 2)),
+            dma((2, PARTS, count - 1)),
+            dma((PARTS,)),
+            dma((chips, 2)),
+            dma((chips,)),
             *RingReduce.scratch(count, size, model),
+            pltpu.VMEM((size, model), full),
+            pltpu.VMEM((size, model), low),
+            pltpu.VMEM((size, model), full),
+            pltpu.VMEM((size, model), low),
+            dma((2,)),
+            *[dma((2, chips))] * 4,
         ],
         compiler_params=pltpu.CompilerParams(
             collective_id=collective_id, has_side_effects=True, vmem_limit_bytes=VMEM_LIMIT
@@ -970,146 +1025,75 @@
     )(partial, normed_rows, grad_rows, *hidden, down_w, out_w, resid, grad_own, gain_rows)
 
 
-def attend_back_kernel(
-    count,
-    shard_count,
-    length,
-    grad_heads,
-    queries,
-    keys,
-    values,
-    cos_in,
-    sin_in,
-    rows_in,
-    qkv_w,
-    branch,
-    resid,
-    grad_attn,
-    attended_own,
-    unit_grad_w,
-    output,
-    partial,
-    grad_w,
-    gain_sum,
-    out_sum,
-    owned_w,
-    cos,
-    sin,
-    weights,
-    grads,
-    sum_k,
-    sum_v,
-    row_tiles,
-    staged,
-    grad_staged,
-    out_staged,
-    out_beside,
-    out_across,
-    loads,
-    tile_loads,
-    stores,
-    grad_stores,
-    beside_sems,
-    across_sems,
-    slots,
-    terms,
-    ring_send,
-    ring_recv,
-    term_loads,
-    *shard_scratch,
-):
+def attend_back_kernel(count, shard_count, *refs):
+    length, *head_refs, cos_in, sin_in, rows_in, qkv_in, branch = refs[:10]
+    *own_refs, gain_rows, gain_ffn_sum, down_grad = refs[10:16]
+    output_out, grad_normed, grad_out_w, gain_total, partial, qkv_grad, out_left, out_right = refs[16:24]
+    arrived = grouped(refs[24:32], 2)
+    cos, sin, weights, grads, sum_k, sum_v, row_tiles, staged, grad_staged, work, out_sum = refs[32:43]
+    loads, tile_loads, stores, grad_stores, work_loads, work_stores, out_loads_sem, free_sems = refs[43:51]
+    gain_block, gain_shards, gain_part, gain_parts, gain_sems, gain_part_sems = refs[51:57]
+    slots, terms, ring_send, ring_recv, term_loads, last_send, last_recv, last_loads = refs[57:65]
+    out_scratch = refs[65:70]
+    grad_heads, queries, keys, values, resid, grad_attn, attended_own, output = refs[70:78]
+    shard_sems = grouped(refs[78:], 2)
+
     ring, shards = Ring(count), Shards(shard_count)
     seq_len, width = queries.shape
     size, model = resid.shape
     blocks, tiles = seq_len // BLOCK, model // TILE
     scale = 1.0 / math.sqrt(HD)
     limit = length[0]
+    others = [{"seq": (ring.index + offset) % count} for offset in range(1, count)]
     inputs = [
         pltpu.make_async_copy(source, place, loads.at[number])
         for number, (source, place) in enumerate(
             (
                 (cos_in, cos),
                 (sin_in, sin),
-                (qkv_w, weights),
+                (qkv_in, weights),
+                *zip(own_refs, (resid, grad_attn, attended_own)),
+                *zip(head_refs, (grad_heads, queries, keys, values)),
             )
         )
     ]
-    greet([*ring.next, *shards.greeted()])
+    for load in inputs[4:6]:
+        load.start()
+    greet([*others, *shards.others()])
     reduce = RingReduce(ring, row_piece(branch, size), slots, terms, ring_send, ring_recv, term_loads)
+    last = RingReduce(ring, row_piece(partial, size), slots, terms, last_send, last_recv, last_loads)
     reduce.start()
-    shard_reduce = ShardReduce(shards, unit_grad_w, *shard_scratch)
-    shard_reduce.start()
-    for load in inputs:
-        load.start()
-
-    out_rows = model // shard_count
-
-    def out_term(shard, lanes):
-        return dot(grad_attn[:, span(shard * out_rows, out_rows)], attended_own[:, lanes], 0, 0)
-
-    def beside(offset):
-        return send_to(
-            shards.sibling,
-            out_staged.at[offset],
-            out_beside.at[offset],
-            beside_sems.at[0, offset],
-            beside_sems.at[1, offset],
-        )
-
-    def across(offset):
-        return send_to(
-            {"dp": shards.device(shards.chip_at(offset), shards.core)},
-            out_beside.at[offset],
-            out_across.at[offset - 1],
-            across_sems.at[0, offset],
-            across_sems.at[1, offset],
-        )
-
-    offsets = [*range(1, shards.chips), 0]
-    out_tile = 512
-
-    def out_start(offset):
-        shard = shards.device(shards.chip_at(offset), 1 - shards.core)
-
-        def tile(number, carry):
-            lanes = span(number * out_tile, out_tile)
-            out_staged[offset, :, lanes] = out_term(shard, lanes).astype(low)
-            return carry
-
-        lax.fori_loop(0, model // out_tile, tile, 0)
-        beside(offset).start()
-
-    def out_middle(offset):
-        shard = shards.device(shards.chip_at(offset), shards.core)
-        beside(offset).wait_recv()
-
-        def tile(number, carry):
-            lanes = span(number * out_tile, out_tile)
-            total = out_beside[offset, :, lanes].astype(full) + out_term(shard, lanes)
-            out_beside[offset, :, lanes] = total.astype(low)
-            return carry
-
-        lax.fori_loop(0, model // out_tile, tile, 0)
-        if offset:
-            across(offset).start()
-
-    def out_finish():
-        for offset in range(1, shards.chips):
-            across(offset).wait_recv()
-
-        def tile(number, carry):
-            lanes = span(number * out_tile, out_tile)
-            total = out_beside[0, :, lanes].astype(full)
-            for offset in range(1, shards.chips):
-                total += out_across[offset - 1, :, lanes].astype(full)
-            out_sum[:, lanes] = total.astype(low)
-            return carry
-
-        lax.fori_loop(0, model // out_tile, tile, 0)
-        for offset in offsets:
-            beside(offset).wait_send()
-            if offset:
-                across(offset).wait_send()
+    shard_reduces = [
+        ShardReduce(shards, whole, *one, work, work_loads, work_stores, *sems)
+        for whole, one, sems in zip((out_left, out_right, down_grad, qkv_grad), arrived, shard_sems)
+    ]
+    left, right, down, qkv = shard_reduces
+
+    half = model // 2
+
+    def out_store(tile):
+        rows = pl.ds(tile * TILE, TILE)
+        return [
+            pltpu.make_async_copy(
+                staged.at[tile % 2, :, pl.ds(side * half, half)], whole.at[rows], stores.at[tile % 2, side]
+            )
+            for side, whole in enumerate((out_left, out_right))
+        ]
+
+    def out_back(tile):
+        if tile >= 2:
+            for copy in out_store(tile - 2):
+                copy.wait()
+        staged[tile % 2] = dot(grad_attn[:, pl.ds(tile * TILE, TILE)], attended_own[...], 0, 0).astype(low)
+        for copy in out_store(tile):
+            copy.start()
+
+    def out_spread():
+        for tile in (tiles - 2, tiles - 1):
+            for copy in out_store(tile):
+                copy.wait()
+        left.start()
+        right.start()
 
     def attend_block(head, number):
         lanes = slice(head * HD, (head + 1) * HD)
@@ -1118,7 +1102,7 @@
             sum_k[...] = jnp.zeros_like(sum_k)
             sum_v[...] = jnp.zeros_like(sum_v)
             if head == 0:
-                for load in inputs[:2]:
+                for load in (*inputs[:2], *inputs[6:]):
                     load.wait()
         query_part, grad_part = queries[here, lanes], grad_heads[here, lanes]
         probs = softmax_block(query_part, keys[upto, lanes], number * BLOCK, limit)
@@ -1142,18 +1126,17 @@
 
     def store(number):
         return pltpu.make_async_copy(
-            staged.at[number % 2], partial.at[pl.ds(number * BLOCK, BLOCK)], stores.at[number % 2]
+            staged.at[number % 2], partial.at[pl.ds(number * BLOCK, BLOCK)], stores.at[number % 2, 0]
         )
 
     def grad_store(tile):
         return pltpu.make_async_copy(
-            grad_staged.at[tile % 2], grad_w.at[pl.ds(tile * TILE, TILE)], grad_stores.at[tile % 2]
+            grad_staged.at[tile % 2], qkv_grad.at[pl.ds(tile * TILE, TILE)], grad_stores.at[tile % 2]
         )
 
     def rows_back(number):
         if number == 0:
-            for load in inputs[2:]:
-                load.wait()
+            inputs[2].wait()
             fetch(0).start()
         if number >= 2:
             store(number - 2).wait()
@@ -1169,268 +1152,290 @@
         grad = dot(row_tiles[tile % 2], grads[...], 0, 0)
         grad_staged[tile % 2] = grad.astype(low)
         grad_store(tile).start()
-        shared = grad * weights[pl.ds(tile * TILE, TILE), :].astype(full)
-        gain_sum[:, pl.ds(tile * TILE, TILE)] = lax.dot_general(
+        lanes = pl.ds(tile * TILE, TILE)
+        product = grad * weights[lanes, :].astype(full)
+        shared = product[:, :HD]
+        for first in range(HD, product.shape[1], HD):
+            shared += product[:, first : first + HD]
+        gain = lax.dot_general(
             jnp.ones((8, shared.shape[1]), full),
             shared,
             (((1,), (1,)), ((), ())),
             precision=lax.Precision.HIGHEST,
             preferred_element_type=full,
         )
-
-    def finish_output():
-        for part in range(PARTS):
-            here = pl.ds(part * reduce.size, reduce.size)
-            position = (
-                ring.index * size + part * reduce.size + lax.broadcasted_iota(jnp.int32, (reduce.size, model), 0)
+        row = lax.broadcasted_iota(jnp.int32, gain.shape, 0)
+        gain_block[:, lanes] = jnp.where(row == 0, gain / gain_rows[0:1, lanes], gain_ffn_sum[:, lanes])
+
+    gain_width = model // shard_count
+    gain_copies = [
+        send_to(
+            other,
+            gain_block.at[:, span(other["dp"] * gain_width, gain_width)],
+            gain_shards.at[shards.index],
+            gain_sems.at[0, number],
+            gain_sems.at[1, number],
+        )
+        for number, other in enumerate(shards.others())
+    ]
+    gain_part_copies = [
+        send_to(
+            other, gain_part, gain_parts.at[ring.index], gain_part_sems.at[0, number], gain_part_sems.at[1, number]
+        )
+        for number, other in enumerate(others)
+    ]
+
+    def gains_start():
+        for copy in gain_copies:
+            copy.start()
+
+    def gains_middle():
+        gain_shards[shards.index] = gain_block[:, span(shards.index * gain_width, gain_width)]
+        for copy in gain_copies:
+            copy.wait_recv()
+        gain_part[...] = jnp.sum(gain_shards[...], axis=0)
+        for copy in gain_part_copies:
+            copy.start()
+
+    def gains_end():
+        gain_parts[ring.index] = gain_part[...]
+        for copy in gain_part_copies:
+            copy.wait_recv()
+        gain_total[...] = jnp.sum(gain_parts[...], axis=0)
+        for copy in (*gain_copies, *gain_part_copies):
+            copy.wait_send()
+
+    def out_loads(side):
+        one = shard_reduces[side]
+        lanes = pl.ds(side * half, half)
+        copies = [pltpu.make_async_copy(one.beside_slots.at[0], out_sum.at[:, lanes], out_loads_sem.at[0])]
+        copies += [
+            pltpu.make_async_copy(
+                one.across_slots.at[offset - 1], work.at[offset, 0, :, one.lanes], out_loads_sem.at[offset]
             )
-            total = resid[here, :] + reduce.total(part)
-            output[here, :] = jnp.where(position < limit, total, 0.0).astype(low)
-
-    tasks = [functools.partial(out_start, offset) for offset in offsets] + [shard_reduce.spread]
+            for offset in range(1, shards.chips)
+        ]
+        return copies
+
+    def out_close(side):
+        one = shard_reduces[side]
+        lanes = pl.ds(side * half, half)
+        one.arrive()
+        for copy in out_loads(side):
+            copy.start()
+        for copy in out_loads(side):
+            copy.wait()
+        total = out_sum[:, lanes].astype(full)
+        for offset in range(1, shards.chips):
+            total += work[offset, 0, :, one.lanes].astype(full)
+        out_sum[:, lanes] = total.astype(low)
+
+    rows, out_width = grad_out_w.shape
+
+    def out_piece(index, part):
+        piece = rows // PARTS
+        return out_sum.at[pl.ds(part * piece, piece), span(index * out_width, out_width)]
+
+    out_reduce = RingReduce(ring, out_piece, *out_scratch)
+    for load in (*inputs[6:], *inputs[:4]):
+        load.start()
+    for load in inputs[4:6]:
+        load.wait()
+    for tile in range(tiles):
+        out_back(tile)
+    out_spread()
     attention = [
         functools.partial(attend_block, head, number) for head in range(width // HD) for number in range(blocks)
     ]
-    tasks += attention[:2] + [functools.partial(out_middle, offset) for offset in offsets] + attention[2:]
-    tasks += [functools.partial(rows_back, number) for number in range(blocks)]
-    tasks += [functools.partial(weights_back, tile) for tile in range(tiles)]
-    weave(tasks, [*reduce.steps(), lambda: None])
+    steps = reduce.steps()
+    steps[0]()
+    weave(attention, [left.load, left.add, left.pass_on, right.load, right.add, right.pass_on, *steps[1:-2]])
+    down.start()
+    projections = [functools.partial(rows_back, number) for number in range(blocks)]
+    projections += [functools.partial(weights_back, tile) for tile in range(tiles)]
+    weave(projections, [down.load, steps[-2], down.add, down.stored])
     for number in (blocks - 2, blocks - 1):
         store(number).wait()
     for tile in (tiles - 2, tiles - 1):
         grad_store(tile).wait()
-    owned_w[...] = shard_reduce.total()
-    out_finish()
-    finish_output()
+    qkv.start()
+    gains_start()
+    steps[-1]()
+    for event in (qkv.load, qkv.add, gains_middle, qkv.stored):
+        event()
+    inputs[3].wait()
+    for part in range(PARTS):
+        here = pl.ds(part * reduce.size, reduce.size)
+        position = ring.index * size + part * reduce.size + lax.broadcasted_iota(jnp.int32, (reduce.size, model), 0)
+        total = resid[here, :] + reduce.total(part)
+        output[here, :] = jnp.where(position < limit, total, 0.0).astype(low)
+    output_store = pltpu.make_async_copy(output, output_out, out_loads_sem.at[shards.chips])
+    output_store.start()
     reduce.finish()
-    shard_reduce.finish()
+    reduce.free(free_sems)
+    last.wait_free(free_sems)
+    last.start()
+    for side in range(2):
+        out_close(side)
+    out_reduce.start()
+    down.cross()
+    qkv.cross()
+    for step in range(1, ring.half):
+        out_reduce.advance(step)
+        last.advance(step)
+    gains_end()
+    for part in range(PARTS):
+        grad_out_w[pl.ds(part * out_reduce.size, out_reduce.size), :] = out_reduce.total(part)
+    for part in range(PARTS):
+        grad_normed[pl.ds(part * last.size, last.size), :] = last.total(part)
+    for one in (down, qkv):
+        one.arrive()
+    for one in (*shard_reduces, last, out_reduce):
+        one.finish()
+    output_store.wait()
 
 
 def attend_back(
-    length,
-    grad_heads,
-    queries,
-    keys,
-    values,
-    tables,
-    rows,
-    qkv_w,
-    branch,
-    resid,
-    grad_attn,
-    attended_own,
-    unit_grad_w,
-    collective_id,
+    length, grad_heads, heads, tables, rows, qkv_w, branch, sums, gain_rows, gain_ffn_sum, down_grad, collective_id
 ):
     count, shard_count = lax.axis_size("seq"), lax.axis_size("dp")
-    seq_len, width = queries.shape
+    resid, grad_attn, attended_own = sums
+    seq_len, width = grad_heads.shape
     size, model = resid.shape
-    chips, out_rows, units = shard_count // CORES, model // shard_count, unit_grad_w.shape[1]
+    chips, shard_rows, units = shard_count // CORES, model // shard_count, down_grad.shape[1]
+    half, gain_width = model // 2, model // shard_count
+    widths = (half, half, units, 3 * width)
+    dma = pltpu.SemaphoreType.DMA
+    arrivals = [
+        shape_of((number, shard_rows, one), low) for one in widths for number in (chips, max(chips - 1, 1))
+    ]
+    out_width = model // count
     return pl.pallas_call(
         functools.partial(attend_back_kernel, count, shard_count),
         out_shape=[
             shape_of((size, model), low),
+            shape_of((size, model), full),
+            shape_of((shard_rows, out_width), full),
+            shape_of((8, gain_width), full),
             shape_of((seq_len, model), low),
             shape_of((model, 3 * width), low),
-            shape_of((8, model), full),
-            shape_of((out_rows, model), low),
-            shape_of((out_rows, units), full),
+            shape_of((model, half), low),
+            shape_of((model, half), low),
+            *arrivals,
         ],
-        in_specs=[SMEM] + [VMEM] * 4 + [ANY] * 5 + [VMEM] * 3 + [ANY],
-        out_specs=[VMEM, ANY, ANY, VMEM, VMEM, VMEM],
+        in_specs=[SMEM] + [ANY] * 12 + [VMEM] * 2 + [ANY],
+        out_specs=[ANY] + [VMEM] * 3 + [ANY] * (4 + len(arrivals)),
         scratch_shapes=[
-            pltpu.VMEM((seq_len, HD), full),
-            pltpu.VMEM((seq_len, HD), full),
+            *[pltpu.VMEM((seq_len, HD), full)] * 2,
             pltpu.VMEM((model, 3 * width), low),
             pltpu.VMEM((seq_len, 3 * width), low),
-            pltpu.VMEM((seq_len, HD), full),
-            pltpu.VMEM((seq_len, HD), full),
+            *[pltpu.VMEM((seq_len, HD), full)] * 2,
             pltpu.VMEM((2, seq_len, TILE), low),
             pltpu.VMEM((2, BLOCK, model), low),
             pltpu.VMEM((2, TILE, 3 * width), low),
-            pltpu.VMEM((chips, out_rows, model), low),
-            pltpu.VMEM((chips, out_rows, model), low),
-            pltpu.VMEM((chips - 1, out_rows, model), low),
-            pltpu.SemaphoreType.DMA((3,)),
-            pltpu.SemaphoreType.DMA((2,)),
-            pltpu.SemaphoreType.DMA((2,)),
-            pltpu.SemaphoreType.DMA((2,)),
-            pltpu.SemaphoreType.DMA((2, chips)),
-            pltpu.SemaphoreType.DMA((2, chips)),
+            pltpu.VMEM((chips, 2, shard_rows, max(widths)), low),
+            pltpu.VMEM((shard_rows, model), low),
+            dma((10,)),
+            dma((2,)),
+            dma((2, 2)),
+            dma((2,)),
+            dma((chips, 2)),
+            dma((chips,)),
+            dma((chips + 1,)),
+            pltpu.SemaphoreType.REGULAR((2,)),
+            pltpu.VMEM((8, model), full),
+            pltpu.VMEM((shard_count, 8, gain_width), full),
+            pltpu.VMEM((8, gain_width), full),
+            pltpu.VMEM((count, 8, gain_width), full),
+            dma((2, shard_count - 1)),
+            dma((2, count - 1)),
             *RingReduce.scratch(count, size, model),
-            *ShardReduce.scratch(shard_count, out_rows, units),
+            *RingReduce.scratch(count, size, model)[2:],
+            *RingReduce.scratch(count, shard_rows, out_width),
+            *[pltpu.VMEM((seq_len, width), low)] * 4,
+            pltpu.VMEM((size, model), full),
+            *[pltpu.VMEM((size, model), low)] * 3,
+            *[dma((2, chips))] * (2 * len(widths)),
         ],
         compiler_params=pltpu.CompilerParams(
             collective_id=collective_id, has_side_effects=True, vmem_limit_bytes=VMEM_LIMIT
         ),
-        cost_estimate=pl.CostEstimate(flops=0, bytes_accessed=250_000_000, transcendentals=0),
+        cost_estimate=pl.CostEstimate(flops=0, bytes_accessed=500_000_000, transcendentals=0),
+    )(length, grad_heads, *heads, *tables, rows, qkv_w, branch, *sums, gain_rows, gain_ffn_sum, down_grad)
+
+
+def settle_kernel(count_weights, *refs):
+    pairs = grouped(refs[: 2 * count_weights], 2)
+    grad_normed, tokens, gain_rows, grad_resid, output_in, grad_out_in = refs[2 * count_weights : 2 * count_weights + 6]
+    output, grad_tokens, grad_out, *owned = refs[2 * count_weights + 6 :]
+
+    def total(pair):
+        beside, across = pair
+        return beside[0].astype(full) + jnp.sum(across[...].astype(full), axis=0)
+
+    output[...] = output_in[...]
+    grad_out[...] = grad_out_in[...]
+    for place, pair in zip(owned, pairs[:-1]):
+        place[...] = total(pair)
+    qkv = total(pairs[-1])
+    for number, place in enumerate(owned[-3:]):
+        width = place.shape[1]
+        place[...] = qkv[:, number * width : (number + 1) * width]
+    values = tokens[...].astype(full)
+    factor = lax.rsqrt(jnp.mean(values * values, axis=-1, keepdims=True) + EPSILON)
+    weighted = grad_normed[...] * gain_rows[0:1, :]
+    inner = jnp.mean(weighted * values, axis=-1, keepdims=True)
+    grad_tokens[...] = grad_resid[...] + factor * (weighted - values * (factor * factor * inner))
+
+
+def settle(pairs, grad_normed, tokens, gain_rows, grad_resid, output, grad_out, width):
+    steps = 4
+    size, model = tokens.shape
+    rows = grad_out.shape[0]
+
+    def cut(array):
+        return pl.BlockSpec((array.shape[0] // steps, array.shape[1]), lambda step: (step, 0))
+
+    def whole(array):
+        return pl.BlockSpec(array.shape, lambda step: (0, 0))
+
+    pair_specs = []
+    for beside, across in pairs:
+        pair_specs.append(pl.BlockSpec((1, rows // steps, beside.shape[2]), lambda step: (0, step, 0)))
+        pair_specs.append(
+            pl.BlockSpec((across.shape[0], rows // steps, across.shape[2]), lambda step: (0, step, 0))
+        )
+    outs = [
+        shape_of((size, model), low),
+        shape_of((size, model), full),
+        shape_of(grad_out.shape, full),
+        *[shape_of((rows, beside.shape[2]), full) for beside, _ in pairs[:-1]],
+        *[shape_of((rows, width), full)] * 3,
+    ]
+    return pl.pallas_call(
+        functools.partial(settle_kernel, len(pairs)),
+        grid=(steps,),
+        out_shape=outs,
+        in_specs=[
+            *pair_specs,
+            cut(grad_normed),
+            cut(tokens),
+            whole(gain_rows),
+            cut(grad_resid),
+            cut(output),
+            cut(grad_out),
+        ],
+        out_specs=[cut(out) for out in outs],
+        compiler_params=pltpu.CompilerParams(vmem_limit_bytes=VMEM_LIMIT),
     )(
-        length,
-        grad_heads,
-        queries,
-        keys,
-        values,
-        *tables,
-        rows,
-        qkv_w,
-        branch,
-        resid,
-        grad_attn,
-        attended_own,
-        unit_grad_w,
-    )
-
-
-def last_kernel(
-    count,
-    shard_count,
-    partial,
-    grad_w,
-    up_grad_w,
-    down_grad_w,
-    out_sum,
-    tokens,
-    gain_rows,
-    grad_resid,
-    gain_blocks,
-    grad_tokens,
-    grad_query_w,
-    grad_key_w,
-    grad_value_w,
-    grad_out_w,
-    grad_up_w,
-    grad_down_w,
-    gains,
-    gain_slots,
-    gain_sum,
-    gain_shards,
-    gain_sems,
-    shard_gain_sems,
-    *scratch,
-):
-    out_scratch, ring_scratch = scratch[:5], scratch[5:10]
-    shard_scratch = grouped(scratch[10:], 6)
-    ring, shards = Ring(count), Shards(shard_count)
-    size = tokens.shape[0]
-    rows, width = grad_out_w.shape
-    others = [{"seq": (ring.index + offset) % count} for offset in range(1, count)]
-    greet([*others, *shards.others()])
-
-    def out_piece(index, part):
-        piece = rows // PARTS
-        return out_sum.at[pl.ds(part * piece, piece), span(index * width, width)]
-
-    reduce = RingReduce(ring, row_piece(partial, size), *ring_scratch)
-    out_reduce = RingReduce(ring, out_piece, *out_scratch)
-    reduce.start()
-    out_reduce.start()
-    weights = [
-        ShardReduce(shards, whole, *one) for whole, one in zip((up_grad_w, down_grad_w, grad_w), shard_scratch)
-    ]
-    gain_copies = [
-        send_to(
-            other,
-            gain_blocks.at[other["seq"]],
-            gain_slots.at[ring.index],
-            gain_sems.at[0, number],
-            gain_sems.at[1, number],
-        )
-        for number, other in enumerate(others)
-    ]
-    shard_gain_copies = [
-        send_to(
-            other, gain_sum, gain_shards.at[shards.index], shard_gain_sems.at[0, number], shard_gain_sems.at[1, number]
-        )
-        for number, other in enumerate(shards.others())
-    ]
-    for copy in gain_copies:
-        copy.start()
-    for weight in weights:
-        weight.start()
-    for weight in weights:
-        weight.spread()
-    gain_slots[ring.index] = gain_blocks[ring.index]
-    for copy in gain_copies:
-        copy.wait_recv()
-    gain_sum[...] = jnp.sum(gain_slots[...], axis=0)
-    for copy in shard_gain_copies:
-        copy.start()
-
-    def finish_gains():
-        gain_shards[shards.index] = gain_sum[...]
-        for copy in shard_gain_copies:
-            copy.wait_recv()
-        gains[...] = jnp.sum(gain_shards[...], axis=0)
-
-    def finish_qkv():
-        total = weights[2].total()
-        for number, place in enumerate((grad_query_w, grad_key_w, grad_value_w)):
-            place[...] = total[:, number * width : (number + 1) * width]
-
-    def finish_up():
-        grad_up_w[...] = weights[0].total()
-
-    def finish_down():
-        grad_down_w[...] = weights[1].total()
-
-    out_steps, steps = out_reduce.steps(), reduce.steps()
-    for number, step in enumerate(steps):
-        out_steps[number]()
-        step()
-    finish_gains()
-    finish_up()
-    finish_down()
-    finish_qkv()
-    for part in range(PARTS):
-        grad_out_w[pl.ds(part * out_reduce.size, out_reduce.size), :] = out_reduce.total(part)
-    for part in range(PARTS):
-        here = pl.ds(part * reduce.size, reduce.size)
-        grad_normed, values = reduce.total(part), tokens[here, :].astype(full)
-        factor = lax.rsqrt(jnp.mean(values * values, axis=-1, keepdims=True) + EPSILON)
-        weighted = grad_normed * gain_rows[0:1, :]
-        inner = jnp.mean(weighted * values, axis=-1, keepdims=True)
-        grad_tokens[here, :] = grad_resid[here, :] + factor * (weighted - values * (factor * factor * inner))
-    reduce.finish()
-    out_reduce.finish()
-    for weight in weights:
-        weight.finish()
-    for copy in (*gain_copies, *shard_gain_copies):
-        copy.wait_send()
-
-
-def last(partial, grad_w, up_grad_w, down_grad_w, out_sum, tokens, gain_rows, grad_resid, gain_blocks, collective_id):
-    count, shard_count = lax.axis_size("seq"), lax.axis_size("dp")
-    size = tokens.shape[0]
-    rows, model = out_sum.shape
-    width, units = model // count, up_grad_w.shape[1]
-    block = gain_blocks.shape[1:]
-    return pl.pallas_call(
-        functools.partial(last_kernel, count, shard_count),
-        out_shape=[
-            shape_of(tokens.shape, full),
-            *[shape_of((rows, width), full)] * 4,
-            *[shape_of((rows, units), full)] * 2,
-            shape_of(block, full),
-        ],
-        in_specs=[ANY] * 5 + [VMEM] * 4,
-        out_specs=[VMEM] * 8,
-        scratch_shapes=[
-            pltpu.VMEM((count, *block), full),
-            pltpu.VMEM(block, full),
-            pltpu.VMEM((shard_count, *block), full),
-            pltpu.SemaphoreType.DMA((2, count - 1)),
-            pltpu.SemaphoreType.DMA((2, shard_count - 1)),
-            *RingReduce.scratch(count, rows, width),
-            *RingReduce.scratch(count, size, model),
-            *ShardReduce.scratch(shard_count, rows, units),
-            *ShardReduce.scratch(shard_count, rows, units),
-            *ShardReduce.scratch(shard_count, rows, 3 * width),
-        ],
-        compiler_params=pltpu.CompilerParams(
-            collective_id=collective_id, has_side_effects=True, vmem_limit_bytes=VMEM_LIMIT
-        ),
-        cost_estimate=pl.CostEstimate(flops=0, bytes_accessed=200_000_000, transcendentals=0),
-    )(partial, grad_w, up_grad_w, down_grad_w, out_sum, tokens, gain_rows, grad_resid, gain_blocks)
+        *[one for pair in pairs for one in pair],
+        grad_normed,
+        tokens,
+        gain_rows,
+        grad_resid,
+        output,
+        grad_out,
+    )
 
 
 def body(
@@ -1474,7 +1479,7 @@
     ) = forward(
         lengths, tokens, gains, cotangent, (w_query, w_key, w_value, w_out, w_gate, w_up, w_down), tables, 1
     )
-    grad_w_gate, grad_w_up, grad_w_down, branch, grad_resid, grad_attn, gain_ffn_sum, grad_heads = ffn_back(
+    gain_ffn_sum, grad_resid, grad_attn, grad_heads, branch, _, _, grad_w_down, *gate_up = ffn_back(
         partial2,
         full2,
         grad_full,
@@ -1485,35 +1490,28 @@
         grad_ffn,
         gain_rows,
         head_width,
-        4,
-    )
-    output, partial1, grad_w, gain_attn_sum, out_sum, owned_gate = attend_back(
+        2,
+    )
+    output, grad_normed1, owned_out, gain_sums, _, _, _, _, *arrived = attend_back(
         lengths,
         grad_heads,
-        queries,
-        keys,
-        values,
+        (queries, keys, values),
         tables,
         full1,
         qkv_w,
         branch,
-        resid,
-        grad_attn,
-        attended_tok,
-        grad_w_gate,
-        5,
-    )
-    count, shard_count = lax.axis_size("seq"), lax.axis_size("dp")
-    gain_sums = jnp.stack([gain_attn_sum[0] / gain_rows[0], gain_ffn_sum[0]])
-    piece = gain_sums.shape[1] // (count * shard_count)
-    gain_blocks = gain_sums.reshape(2, shard_count, count, piece).transpose(2, 1, 0, 3)
-    gain_blocks = gain_blocks.reshape(count, shard_count, 2 * piece)
-    gain_blocks = jnp.pad(gain_blocks, ((0, 0), (0, 8 - shard_count), (0, 128 - 2 * piece)))
-    grad_tokens, owned_query, owned_key, owned_value, owned_out, owned_up, owned_down, owned_gains = last(
-        partial1, grad_w, grad_w_up, grad_w_down, out_sum, tokens, gain_rows, grad_resid, gain_blocks, 6
-    )
-    owned_gains = lax.dynamic_index_in_dim(owned_gains, lax.axis_index("dp"), 0, keepdims=False)
-    owned_gain_attn, owned_gain_ffn = owned_gains[:piece], owned_gains[piece : 2 * piece]
+        (resid, grad_attn, attended_tok),
+        gain_rows,
+        gain_ffn_sum,
+        grad_w_down,
+        3,
+    )
+    output, grad_tokens, owned_out, owned_gate, owned_up, owned_down, owned_query, owned_key, owned_value = settle(
+        grouped([*gate_up, *arrived[4:]], 2), grad_normed1, tokens, gain_rows, grad_resid, output, owned_out, head_width
+    )
+    piece = gain_sums.shape[1] // lax.axis_size("seq")
+    owned_gains = lax.dynamic_slice_in_dim(gain_sums, lax.axis_index("seq") * piece, piece, axis=1)
+    owned_gain_attn, owned_gain_ffn = owned_gains[0], owned_gains[1]
     return (
         output,
         grad_tokens,

time: 539 us -> 523 us (0.970)
  local copies, waits for them, and re-layouts: 15.6 us -> 2.73 us
    pallas_call x1, Pallas kernels: 81.8 us -> 163 us  [attend_back(): pl.pallas_call(functools.partial(attend_back_kernel, count, shard_count),...]
    pallas_call x2, Pallas kernels: 175 us -> 102 us  [the longest x1 93.5 us: ffn_back(): pl.pallas_call(functools.partial(ffn_back_kernel, count, shard_count), ou...]
    unnamed x25 -> x0, local copies, waits for them, and re-layouts: 11.9 us -> none
    pallas_call x1, Pallas kernels: 253 us -> 242 us  [forward(): pl.pallas_call(functools.partial(forward_kernel, count, shard_count), out...]
where the time goes in v4:
time: 523 us; the launch traced here: 513 us
  Pallas kernels  508 us (97%)
    pallas_call x1, Pallas kernels, forward(): pl.pallas_call(functools.partial(forward_kernel, count, shard_count), out...  242 us
    pallas_call x1, Pallas kernels, attend_back(): pl.pallas_call(functools.partial(attend_back_kernel, count, shard_count),...  163 us
    pallas_call x1, Pallas kernels, ffn_back(): pl.pallas_call(functools.partial(ffn_back_kernel, count, shard_count), ou...  93.5 us

profile of v4, /device:TPU:0, one launch (start us, length us, event | category | flops | bytes accessed | tf_op | source)
XLA Modules:
  0.0 512.9 jit_solution(3707734535193351345)
XLA Ops:
  1.3 0.7 broadcast_in_dim.10
  2.0 0.7 broadcast_in_dim.9
  2.7 0.1 pad.2.clone
  2.7 0.7 maximum_maximum_fusion.refs_2_
  3.4 242.4 %shard_map.221 = (f32[8,2048]{1,0:T(8,128)}, bf16[1536,256]{1,0:T(8,128)(2,1)}, bf16[1536,256]{1,0:T(8,128)(2,1)}, bf16[1536,256]{1,0:T(8,128)(2,1)}, bf16[192,2...) custom-call(s32[1]{0:T(128)S(6)} %copy.25.refs_0_, ...), custom_call_target="tpu_custom_call" | custom-call | bytes 600000000 | tf_op jit(solution)/shard_map/pallas_call | solution.py:776
  245.9 93.5 %shard_map.222 = (f32[8,2048]{1,0:T(8,128)}, f32[192,2048]{1,0:T(8,128)}, bf16[192,2048]{1,0:T(8,128)(2,1)}, bf16[1536,256]{1,0:T(8,128)(2,1)}, bf16[1536,2048]{...) custom-call(bf16[1536,2048]{1,0:T(8,128)(2,1)} %get-tuple-element.55, ...), custom_call_target="tpu_custom_call" | custom-call | bytes 300000000 | tf_op jit(solution)/shard_map/pallas_call | solution.py:982
  339.4 163.2 %shard_map.223 = (bf16[192,2048]{1,0:T(8,128)(2,1)}, f32[192,2048]{1,0:T(8,128)}, f32[512,256]{1,0:T(8,128)}, f32[8,512]{1,0:T(8,128)}, bf16[1536,2048]{1,0:T(8,...) custom-call(s32[1]{0:T(128)S(6)} %copy.25.refs_0_, ...), custom_call_target="tpu_custom_call" | custom-call | bytes 500000000 | tf_op jit(solution)/shard_map/pallas_call | solution.py:1313
  502.6 8.6 %shard_map.224 = (bf16[192,2048]{1,0:T(8,128)(2,1)}, f32[192,2048]{1,0:T(8,128)}, f32[512,256]{1,0:T(8,128)}, f32[512,1024]{1,0:T(8,128)}, f32[512,1024]{1,0:T(8...) custom-call(bf16[2,512,1024]{2,1,0:T(8,128)(2,1)} %get-tuple-element.66.refs_0_, ...), custom_call_target="tpu_custom_call" | custom-call | tf_op jit(solution)/shard_map/pallas_call | solution.py:1415
  511.2 0.8 constant_dynamic-slice_fusion
  511.9 0.5 slice_bitcast_fusion
  (1 shorter events, 0.0 us)

commit v5 on v4

--- a/solution.py
+++ b/solution.py
@@ -475,9 +475,8 @@
 
 
 def forward_kernel(count, shard_count, *refs):
-    (length, tokens, gains, cotangent, query_in, key_in, value_in, out_in, gate_in, up_in, down_in, cos_in, sin_in) = (
-        refs[:13]
-    )
+    length, tokens, both_gains, cotangent, query_in, key_in, value_in, out_in = refs[:8]
+    gate_in, up_in, down_in, cos_in, sin_in = refs[8:13]
     gain_rows, *results = refs[13:20]
     (all_rows, grad_rows, normed_rows, qkv_out, out_out, down_out, act_out, grad_gate_out, grad_up_out, partial) = (
         refs[20:30]
@@ -485,13 +484,14 @@
     (all_gains, qkv_w, out_w, gate_w, up_w, down_w, cos, sin, own, attended, normed, grads, hidden, back) = refs[30:44]
     (gain_sems, local, row_loads, stores, weight_stores, swap_sems) = refs[44:50]
     queries, keys, values, grad_own, attended_own, resid, result_sems = refs[50:57]
+    gains, acts = refs[57:59]
     result_copies = [
         pltpu.make_async_copy(source, place, result_sems.at[number])
         for number, (source, place) in enumerate(
             zip((queries, keys, values, grad_own, attended_own, resid), results)
         )
     ]
-    sems = refs[57:]
+    sems = refs[59:]
     out_sems, row_sems, grad_sems, normed_sems = grouped(sems[:8], 2)
     shard_sems = grouped(sems[8:], 3)
 
@@ -504,6 +504,9 @@
     tables = [pltpu.make_async_copy(cos_in, cos, local.at[0]), pltpu.make_async_copy(sin_in, sin, local.at[1])]
     for table in tables:
         table.start()
+    row = lax.broadcasted_iota(jnp.int32, gains.shape, 0)
+    both = jnp.where(row == 0, both_gains[0:1, :], both_gains[1:2, :])
+    gains[...] = jnp.where(row < 2, both, 0.0).astype(low)
     greet([*others, *shards.others()])
 
     out_rows, out_width = out_in.shape
@@ -703,22 +706,47 @@
             results.append(pltpu.make_async_copy(back.at[here], partial.at[there], stores.at[side, 3]))
         return results
 
+    def ahead(step):
+        return step >= ring.half - 1
+
+    def ahead_rows(step):
+        return pl.ds(0 if step < ring.half else 2 * size, size * len(owners(step)))
+
+    def grad_acts(step):
+        for load in grad_loads(step):
+            load.start()
+        for load in grad_loads(step):
+            load.wait()
+        rows, there = pl.ds(0, size * len(owners(step))), ahead_rows(step)
+
+        def one(tile, carry):
+            lanes = span(tile * TILE, TILE)
+            acts[there, lanes] = dot(grads[step % 2, rows, :], down_w[:, lanes])
+            return carry
+
+        lax.fori_loop(0, units // TILE, one, 0)
+
     def feed(step):
-        for load in (*normed_loads(step, own.at[1], normed_rows), *grad_loads(step)):
+        loads = normed_loads(step, own.at[1], normed_rows)
+        if not ahead(step):
+            loads += grad_loads(step)
+        for load in loads:
             load.start()
         if step > 0:
             for store in result_stores(step - 1):
                 store.wait()
-        for load in (*normed_loads(step, own.at[1], normed_rows), *grad_loads(step)):
+        for load in loads:
             load.wait()
         rows = pl.ds(0, size * len(owners(step)))
-        slot = step % 2
 
         def forward(tile, carry):
             lanes = span(tile * TILE, TILE)
             gate = dot(normed[rows, :], gate_w[:, lanes])
             up = dot(normed[rows, :], up_w[:, lanes])
-            grad_act = dot(grads[slot, rows, :], down_w[:, lanes])
+            if ahead(step):
+                grad_act = acts[ahead_rows(step), lanes]
+            else:
+                grad_act = dot(grads[step % 2, rows, :], down_w[:, lanes])
             sigmoid = 1.0 / (1.0 + jnp.exp(-gate))
             silu = gate * sigmoid
             hidden[0, rows, lanes] = (silu * up).astype(low)
@@ -751,6 +779,9 @@
         if step + 2 <= ring.half:
             grad_gather.advance(step + 2)
         feed(step)
+        if step == ring.half - 2:
+            grad_acts(step + 1)
+            grad_acts(step + 2)
     for store in result_stores(ring.half):
         store.wait()
     for gather in (out_gather, row_gather, grad_gather, normed_gather):
@@ -766,7 +797,7 @@
             swap(head, number).wait_send()
 
 
-def forward(length, tokens, gains, cotangent, weights, tables, collective_id):
+def forward(length, tokens, both_gains, cotangent, weights, tables, collective_id):
     count, shard_count = lax.axis_size("seq"), lax.axis_size("dp")
     size, model = tokens.shape
     seq_len, width, units = size * count, weights[0].shape[1], weights[4].shape[1]
@@ -797,7 +828,7 @@
         in_specs=[SMEM] + [VMEM] * 3 + [ANY] * 9,
         out_specs=[VMEM] + [ANY] * 16,
         scratch_shapes=[
-            pltpu.VMEM((shard_count, *gains.shape), low),
+            pltpu.VMEM((shard_count, 16, both_gains.shape[1]), low),
             pltpu.VMEM((model, 3 * width), low),
             pltpu.VMEM((model, model), low),
             *[pltpu.VMEM((model, units), low)] * 3,
@@ -818,6 +849,8 @@
             *[pltpu.VMEM((size, model), low)] * 2,
             pltpu.VMEM((size, model), full),
             dma((6,)),
+            pltpu.VMEM((16, both_gains.shape[1]), low),
+            pltpu.VMEM((3 * size, units), full),
             *ring_semaphores(count) * 4,
             *ShardGather.semaphores(shard_count) * 7,
         ],
@@ -825,7 +858,7 @@
             collective_id=collective_id, has_side_effects=True, vmem_limit_bytes=VMEM_LIMIT
         ),
         cost_estimate=pl.CostEstimate(flops=0, bytes_accessed=600_000_000, transcendentals=0),
-    )(length, tokens, gains, cotangent, *weights, *tables)
+    )(length, tokens, both_gains, cotangent, *weights, *tables)
 
 
 def ffn_back_kernel(count, shard_count, *refs):
@@ -919,16 +952,18 @@
 
     steps = reduce.steps()
     tasks = [functools.partial(weights, tile) for tile in range(last + 1)]
-    early = count_tiles * 3 // 4
+    early = count_tiles // 2
     weave(tasks[:early], [])
     steps[0]()
     weave(tasks[early : count_tiles + 2], [])
     gate.start()
     weave(tasks[count_tiles + 2 : 2 * count_tiles + 2], [gate.load, gate.add, gate.pass_on, lambda: None])
     up.start()
-    weave(tasks[2 * count_tiles + 2 :], [*steps[1:-1], up.load, up.add])
+    for step in steps[1:-1]:
+        step()
+    weave(tasks[2 * count_tiles + 2 :], [up.load, up.add])
     tasks = [functools.partial(branches, tile) for tile in range(count_tiles)]
-    weave(tasks, [up.pass_on, lambda: None, steps[-1]])
+    weave(tasks, [up.pass_on, steps[-1], lambda: None])
     for copy in inputs[4:]:
         copy.wait()
     gain_total = jnp.zeros((1, model), full)
@@ -1241,28 +1276,26 @@
         load.start()
     for load in inputs[4:6]:
         load.wait()
+    steps = reduce.steps()
     for tile in range(tiles):
         out_back(tile)
+        if tile == tiles // 2:
+            steps[0]()
     out_spread()
     attention = [
         functools.partial(attend_block, head, number) for head in range(width // HD) for number in range(blocks)
     ]
-    steps = reduce.steps()
-    steps[0]()
-    weave(attention, [left.load, left.add, left.pass_on, right.load, right.add, right.pass_on, *steps[1:-2]])
+    weave(attention, [left.load, left.add, left.pass_on, right.load, right.add, right.pass_on, *steps[1:-1]])
     down.start()
     projections = [functools.partial(rows_back, number) for number in range(blocks)]
     projections += [functools.partial(weights_back, tile) for tile in range(tiles)]
-    weave(projections, [down.load, steps[-2], down.add, down.stored])
+    weave(projections, [down.load, down.add, down.stored, steps[-1], lambda: None])
     for number in (blocks - 2, blocks - 1):
         store(number).wait()
     for tile in (tiles - 2, tiles - 1):
         grad_store(tile).wait()
     qkv.start()
     gains_start()
-    steps[-1]()
-    for event in (qkv.load, qkv.add, gains_middle, qkv.stored):
-        event()
     inputs[3].wait()
     for part in range(PARTS):
         here = pl.ds(part * reduce.size, reduce.size)
@@ -1279,10 +1312,15 @@
         out_close(side)
     out_reduce.start()
     down.cross()
-    qkv.cross()
-    for step in range(1, ring.half):
+    last.advance(1)
+    qkv.load()
+    qkv.add()
+    out_reduce.advance(1)
+    qkv.pass_on()
+    gains_middle()
+    for step in range(2, ring.half):
+        last.advance(step)
         out_reduce.advance(step)
-        last.advance(step)
     gains_end()
     for part in range(PARTS):
         grad_out_w[pl.ds(part * out_reduce.size, out_reduce.size), :] = out_reduce.total(part)
@@ -1455,9 +1493,7 @@
     seq_len = tokens.shape[0] * lax.axis_size("seq")
     head_width = w_query.shape[1]
     tables = rope_tables(seq_len)
-    gains = jnp.concatenate(
-        [gain_attn[None], gain_ffn[None], jnp.zeros((14, gain_attn.shape[0]), gain_attn.dtype)], axis=0
-    )
+    both_gains = jnp.stack([gain_attn, gain_ffn]).astype(jnp.float32)
     (
         gain_rows,
         queries,
@@ -1477,7 +1513,7 @@
         grad_up,
         partial2,
     ) = forward(
-        lengths, tokens, gains, cotangent, (w_query, w_key, w_value, w_out, w_gate, w_up, w_down), tables, 1
+        lengths, tokens, both_gains, cotangent, (w_query, w_key, w_value, w_out, w_gate, w_up, w_down), tables, 1
     )
     gain_ffn_sum, grad_resid, grad_attn, grad_heads, branch, _, _, grad_w_down, *gate_up = ffn_back(
         partial2,

time: 523 us -> 522 us (level)
  no operation moved by 1% of the time
where the time goes in v5:
time: 522 us; the launch traced here: 511 us
  Pallas kernels  506 us (97%)
    pallas_call x1, Pallas kernels, forward(): pl.pallas_call(functools.partial(forward_kernel, count, shard_count), out...  245 us
    pallas_call x1, Pallas kernels, attend_back(): pl.pallas_call(functools.partial(attend_back_kernel, count, shard_count),...  163 us
    pallas_call x1, Pallas kernels, ffn_back(): pl.pallas_call(functools.partial(ffn_back_kernel, count, shard_count), ou...  89.8 us

profile of v5, /device:TPU:0, one launch (start us, length us, event | category | flops | bytes accessed | tf_op | source)
XLA Modules:
  0.0 511.5 jit_solution(9369980040509493937)
XLA Ops:
  1.3 0.7 stack.10
  2.0 0.7 stack.9
  2.7 0.6 maximum_convert_fusion.refs_2_
  3.3 244.9 %shard_map.221 = (f32[8,2048]{1,0:T(8,128)}, bf16[1536,256]{1,0:T(8,128)(2,1)}, bf16[1536,256]{1,0:T(8,128)(2,1)}, bf16[1536,256]{1,0:T(8,128)(2,1)}, bf16[192,2...) custom-call(s32[1]{0:T(128)S(6)} %copy.25.refs_0_, ...), custom_call_target="tpu_custom_call" | custom-call | bytes 600000000 | tf_op jit(solution)/shard_map/pallas_call | solution.py:807
  248.1 89.8 %shard_map.222 = (f32[8,2048]{1,0:T(8,128)}, f32[192,2048]{1,0:T(8,128)}, bf16[192,2048]{1,0:T(8,128)(2,1)}, bf16[1536,256]{1,0:T(8,128)(2,1)}, bf16[1536,2048]{...) custom-call(bf16[1536,2048]{1,0:T(8,128)(2,1)} %get-tuple-element.55, ...), custom_call_target="tpu_custom_call" | custom-call | bytes 300000000 | tf_op jit(solution)/shard_map/pallas_call | solution.py:1017
  337.9 163.2 %shard_map.223 = (bf16[192,2048]{1,0:T(8,128)(2,1)}, f32[192,2048]{1,0:T(8,128)}, f32[512,256]{1,0:T(8,128)}, f32[8,512]{1,0:T(8,128)}, bf16[1536,2048]{1,0:T(8,...) custom-call(s32[1]{0:T(128)S(6)} %copy.25.refs_0_, ...), custom_call_target="tpu_custom_call" | custom-call | bytes 500000000 | tf_op jit(solution)/shard_map/pallas_call | solution.py:1351
  501.2 8.6 %shard_map.224 = (bf16[192,2048]{1,0:T(8,128)(2,1)}, f32[192,2048]{1,0:T(8,128)}, f32[512,256]{1,0:T(8,128)}, f32[512,1024]{1,0:T(8,128)}, f32[512,1024]{1,0:T(8...) custom-call(bf16[2,512,1024]{2,1,0:T(8,128)(2,1)} %get-tuple-element.66.refs_0_, ...), custom_call_target="tpu_custom_call" | custom-call | tf_op jit(solution)/shard_map/pallas_call | solution.py:1453
  509.8 0.8 constant_dynamic-slice_fusion
  510.5 0.5 slice_bitcast_fusion

commit v6 on v5

--- a/solution.py
+++ b/solution.py
@@ -542,6 +542,20 @@
         gather.start()
 
     piece = size // PARTS
+
+    def own_gather(source, whole, pair):
+        return RingGather(ring, lambda part: source.at[pl.ds(part * piece, piece)], row_piece(whole, size), *pair)
+
+    def own_kept(source, whole, number):
+        return pltpu.make_async_copy(source, whole.at[span(ring.index * size, size)], local.at[number])
+
+    position = ring.index * size + lax.broadcasted_iota(jnp.int32, (size, model), 0)
+    grad_own[...] = jnp.where(position < limit, cotangent[...].astype(full), 0.0).astype(low)
+    grad_gather = own_gather(grad_own, grad_rows, grad_sems)
+    grad_kept = own_kept(grad_own, grad_rows, 4)
+    grad_kept.start()
+    grad_gather.start()
+
     rows = tokens[...].astype(full)
     rows = rows * lax.rsqrt(jnp.mean(rows * rows, axis=-1, keepdims=True) + EPSILON)
     all_gains[shards.index] = gains[...]
@@ -552,22 +566,11 @@
         gain_rows[:, shard * gain_width : (shard + 1) * gain_width] = all_gains[shard, :8, :].astype(full)
     own[0] = (rows * gain_rows[0:1, :]).astype(low)
 
-    def own_gather(source, whole, pair):
-        return RingGather(ring, lambda part: source.at[pl.ds(part * piece, piece)], row_piece(whole, size), *pair)
-
-    def own_kept(source, whole, number):
-        return pltpu.make_async_copy(source, whole.at[span(ring.index * size, size)], local.at[number])
-
     row_gather = own_gather(own.at[0], all_rows, row_sems)
     row_gather.start()
     row_kept = own_kept(own.at[0], all_rows, 3)
     row_kept.start()
     gate_gather.start()
-    position = ring.index * size + lax.broadcasted_iota(jnp.int32, (size, model), 0)
-    grad_own[...] = jnp.where(position < limit, cotangent[...].astype(full), 0.0).astype(low)
-    grad_gather = own_gather(grad_own, grad_rows, grad_sems)
-    grad_kept = own_kept(grad_own, grad_rows, 4)
-    grad_kept.start()
 
     def owners(step):
         if step in (0, ring.half):
@@ -624,7 +627,7 @@
         if step == 2:
             gate_gather.pass_on()
         if step == ring.half:
-            grad_gather.start()
+            grad_gather.advance(1)
             down_gather.start()
         project(step)
 
@@ -659,7 +662,7 @@
             swap(head, number).start()
     swap_kept.start()
     up_gather.pass_on()
-    grad_gather.advance(1)
+    grad_gather.advance(2)
     out_shards.pass_on()
     out_shards.arrive()
     out_store = pltpu.make_async_copy(out_w, out_out, weight_stores.at[1])
@@ -766,7 +769,7 @@
         for store in result_stores(step):
             store.start()
 
-    grad_gather.advance(2)
+    grad_gather.advance(3)
     down_gather.pass_on()
     gate_gather.arrive()
     up_gather.arrive()
@@ -776,8 +779,8 @@
     feed(0)
     for step in range(1, ring.half + 1):
         normed_gather.advance(step)
-        if step + 2 <= ring.half:
-            grad_gather.advance(step + 2)
+        if step + 3 <= ring.half:
+            grad_gather.advance(step + 3)
         feed(step)
         if step == ring.half - 2:
             grad_acts(step + 1)

time: 522 us -> 523 us (level)
  no operation moved by 1% of the time
where the time goes in v6:
time: 523 us; the launch traced here: 513 us
  Pallas kernels  508 us (97%)
    pallas_call x1, Pallas kernels, forward(): pl.pallas_call(functools.partial(forward_kernel, count, shard_count), out...  245 us
    pallas_call x1, Pallas kernels, attend_back(): pl.pallas_call(functools.partial(attend_back_kernel, count, shard_count),...  164 us
    pallas_call x1, Pallas kernels, ffn_back(): pl.pallas_call(functools.partial(ffn_back_kernel, count, shard_count), ou...  89.7 us

profile of v6, /device:TPU:0, one launch (start us, length us, event | category | flops | bytes accessed | tf_op | source)
XLA Modules:
  0.0 512.6 jit_solution(8037943027856007030)
XLA Ops:
  1.3 0.7 stack.10
  2.0 0.7 stack.9
  2.7 0.6 maximum_convert_fusion.refs_2_
  3.3 245.5 %shard_map.221 = (f32[8,2048]{1,0:T(8,128)}, bf16[1536,256]{1,0:T(8,128)(2,1)}, bf16[1536,256]{1,0:T(8,128)(2,1)}, bf16[1536,256]{1,0:T(8,128)(2,1)}, bf16[192,2...) custom-call(s32[1]{0:T(128)S(6)} %copy.25.refs_0_, ...), custom_call_target="tpu_custom_call" | custom-call | bytes 600000000 | tf_op jit(solution)/shard_map/pallas_call | solution.py:810
  248.7 89.7 %shard_map.222 = (f32[8,2048]{1,0:T(8,128)}, f32[192,2048]{1,0:T(8,128)}, bf16[192,2048]{1,0:T(8,128)(2,1)}, bf16[1536,256]{1,0:T(8,128)(2,1)}, bf16[1536,2048]{...) custom-call(bf16[1536,2048]{1,0:T(8,128)(2,1)} %get-tuple-element.55, ...), custom_call_target="tpu_custom_call" | custom-call | bytes 300000000 | tf_op jit(solution)/shard_map/pallas_call | solution.py:1020
  338.5 163.8 %shard_map.223 = (bf16[192,2048]{1,0:T(8,128)(2,1)}, f32[192,2048]{1,0:T(8,128)}, f32[512,256]{1,0:T(8,128)}, f32[8,512]{1,0:T(8,128)}, bf16[1536,2048]{1,0:T(8,...) custom-call(s32[1]{0:T(128)S(6)} %copy.25.refs_0_, ...), custom_call_target="tpu_custom_call" | custom-call | bytes 500000000 | tf_op jit(solution)/shard_map/pallas_call | solution.py:1354
  502.3 8.6 %shard_map.224 = (bf16[192,2048]{1,0:T(8,128)(2,1)}, f32[192,2048]{1,0:T(8,128)}, f32[512,256]{1,0:T(8,128)}, f32[512,1024]{1,0:T(8,128)}, f32[512,1024]{1,0:T(8...) custom-call(bf16[2,512,1024]{2,1,0:T(8,128)(2,1)} %get-tuple-element.66.refs_0_, ...), custom_call_target="tpu_custom_call" | custom-call | tf_op jit(solution)/shard_map/pallas_call | solution.py:1456
  510.9 0.8 constant_dynamic-slice_fusion
  511.6 0.5 slice_bitcast_fusion
